TPU v7x, 32 devices: a whole 2x2x4 slice. The times are simulated.
32 devices in a mesh: dp: 4 (over x, core), tensor: 8 (over z, y).
Axes of the slice: x: 2, y: 2, z: 4, core: 2. Of those that a mesh axis runs over, the one named last changes fastest.
Arguments:
- tokens: bfloat16 [12288, 1024], P(('dp', 'tensor')), may hold values from -6 to 6, as said below
- memory: bfloat16 [12288, 1024], P(('dp', 'tensor')), may hold values from -6 to 6, as said below
- self_qkv: bfloat16 [1024, 3, 1024], P(None, None, 'tensor'), may hold values from -1 to 1, as said below
- self_out: bfloat16 [1024, 1024], P('tensor'), may hold values from -3 to 3
- cross_q: bfloat16 [1024, 1024], P(None, 'tensor'), may hold values from -1 to 1, as said below
- cross_kv: bfloat16 [1024, 2, 1024], P(None, None, 'tensor'), may hold values from -1 to 1, as said below
- cross_out: bfloat16 [1024, 1024], P('tensor'), may hold values from -6 to 6
- hidden_weight: bfloat16 [1024, 4096], P(None, 'tensor'), may hold values from -0.1875 to 0.1875
- hidden_bias: bfloat16 [4096], P('tensor'), may hold values from -3 to 3
- output_weight: bfloat16 [4096, 1024], P('tensor'), may hold values from -0.75 to 0.75
- output_bias: float32 [1024], replicated, may hold values from -5 to 5
- norm_gain: float32 [3, 1024], replicated, may hold values from 0.25 to 1.75
- norm_shift: float32 [3, 1024], replicated, may hold values from -3 to 3
- grad_output: bfloat16 [12288, 1024], P(('dp', 'tensor')), may hold values from -6 to 6
Outputs:
- layer_output: bfloat16 [12288, 1024], P(('dp', 'tensor'))
- grad_tokens: float32 [12288, 1024], P(('dp', 'tensor'))
- grad_memory: float32 [12288, 1024], P(('dp', 'tensor'))
- grad_self_qkv: float32 [1024, 3, 1024], P(None, None, 'tensor')
- grad_self_out: float32 [1024, 1024], P('tensor')
- grad_cross_q: float32 [1024, 1024], P(None, 'tensor')
- grad_cross_kv: float32 [1024, 2, 1024], P(None, None, 'tensor')
- grad_cross_out: float32 [1024, 1024], P('tensor')
- grad_hidden_weight: float32 [1024, 4096], P(None, 'tensor')
- grad_hidden_bias: float32 [4096], P('tensor')
- grad_output_weight: float32 [4096, 1024], P('tensor')
- grad_output_bias: float32 [1024], replicated
- grad_norm_gain: float32 [3, 1024], replicated
- grad_norm_shift: float32 [3, 1024], replicated
Inputs may be any that keep to these rules, and one draw needn't show every extreme that they name: `tokens`: independent entries of mean zero and deviation one. `memory`: independent entries of mean zero and deviation one. `self_qkv`: independent entries of mean zero and deviation 1 / sqrt(1024). `cross_q`: independent entries of mean zero and deviation 1 / sqrt(1024). `cross_kv`: independent entries of mean zero and deviation 1 / sqrt(1024).
All inputs are finite; a program needn't handle non-finite values.
Results may differ from a plain program's by a relative error of at most 0.023.
Values may be sent and summed in bfloat16 or wider, within the bound.
A program may use at most 256 MiB of HBM per device.

v0:
```python
import jax
import jax.numpy as jnp
from jax import lax
from jax.sharding import PartitionSpec as P

DH = 64
LEN = 1024
MEM = 1024


residual_alpha = 300.0**0.25
norm_eps = 1e-05
masked_score = -1e30
contract_rows = (((0,), (0,)), ((), ()))
contract_cols = (((1,), (1,)), ((), ()))


def for_sending(value):
    return jax.tree.map(lambda a: a.astype(jnp.bfloat16) if a.dtype == jnp.float32 else a, value)


def normalize(rows_in, gain_row, shift_row):
    row_mean = jnp.mean(rows_in, axis=-1, keepdims=True)
    centered = rows_in - row_mean
    variance = jnp.mean(centered * centered, axis=-1, keepdims=True)
    return centered * lax.rsqrt(variance + norm_eps) * gain_row + shift_row


def gelu_tanh(values):
    return jax.nn.gelu(values, approximate=True)


def weight_grad(left_rows, right_rows):
    return lax.dot_general(left_rows, right_rows, contract_rows, preferred_element_type=jnp.float32)


def back_product(row_values, weight):
    return lax.dot_general(row_values, weight, contract_cols, preferred_element_type=jnp.float32)


def causal_mask(offset, block_rows, key_count):
    row_pos = offset + jnp.arange(block_rows, dtype=jnp.int32)[:, None]
    col_pos = jnp.arange(key_count, dtype=jnp.int32)[None, :]
    return col_pos <= row_pos


def attend_forward(queries, keys_in, values_in, causal):
    block_rows = min(512, queries.shape[1])
    outputs = []
    lse_list = []
    for offset in range(0, queries.shape[1], block_rows):
        query_block = queries[:, offset : offset + block_rows]
        scores = jnp.einsum(
            "sqhd,skhd->shqk", query_block, keys_in, preferred_element_type=jnp.float32
        ) * DH ** (-0.5)
        if causal:
            scores = jnp.where(
                causal_mask(offset, block_rows, keys_in.shape[1]), scores, masked_score
            )
        row_top = jnp.max(scores, axis=-1, keepdims=True)
        exp_scores = jnp.exp(scores - row_top)
        row_total = jnp.sum(exp_scores, axis=-1, keepdims=True)
        probs_low = (exp_scores / row_total).astype(jnp.bfloat16)
        outputs.append(
            jnp.einsum("shqk,skhd->sqhd", probs_low, values_in, preferred_element_type=jnp.float32)
        )
        lse_list.append(row_top + jnp.log(row_total))
    return (jnp.concatenate(outputs, 1), lse_list)


def attend_backward(queries, keys_in, values_in, lse_list, grad_heads, causal):
    block_rows = min(512, queries.shape[1])
    scale_factor = DH ** (-0.5)
    grad_keys = jnp.zeros(keys_in.shape, jnp.float32)
    grad_values = jnp.zeros(values_in.shape, jnp.float32)
    query_grads = []
    for position, offset in enumerate(range(0, queries.shape[1], block_rows)):
        query_block = queries[:, offset : offset + block_rows]
        grad_block = grad_heads[:, offset : offset + block_rows]
        scores = (
            jnp.einsum("sqhd,skhd->shqk", query_block, keys_in, preferred_element_type=jnp.float32)
            * scale_factor
        )
        if causal:
            scores = jnp.where(
                causal_mask(offset, block_rows, keys_in.shape[1]), scores, masked_score
            )
        probs = jnp.exp(scores - lse_list[position])
        grad_values = grad_values + jnp.einsum(
            "shqk,sqhd->skhd",
            probs.astype(jnp.bfloat16),
            grad_block,
            preferred_element_type=jnp.float32,
        )
        grad_probs = jnp.einsum(
            "sqhd,skhd->shqk", grad_block, values_in, preferred_element_type=jnp.float32
        )
        row_dot = jnp.sum(grad_probs * probs, axis=-1, keepdims=True)
        grad_scores = (probs * (grad_probs - row_dot)).astype(jnp.bfloat16)
        query_grads.append(
            jnp.einsum("shqk,skhd->sqhd", grad_scores, keys_in, preferred_element_type=jnp.float32)
            * scale_factor
        )
        grad_keys = (
            grad_keys
            + jnp.einsum(
                "shqk,sqhd->skhd", grad_scores, query_block, preferred_element_type=jnp.float32
            )
            * scale_factor
        )
    return (jnp.concatenate(query_grads, 1), grad_keys, grad_values)


def reduce_forward(row_values, weight):
    own_rows = row_values.shape[0] // lax.axis_size("tensor")

    def row_term(offset, row_count):
        return jnp.dot(row_values, weight, preferred_element_type=jnp.float32)

    return lax.psum_scatter(
        row_term(jnp.int32(0), lax.axis_size("tensor") * own_rows),
        "tensor",
        scatter_dimension=0,
        tiled=True,
    )


def reduce_back(row_values, weight):
    own_rows = row_values.shape[0] // lax.axis_size("tensor")

    def row_term(offset, row_count):
        return back_product(row_values, weight)

    return lax.psum_scatter(
        row_term(jnp.int32(0), own_rows * lax.axis_size("tensor")).astype(jnp.bfloat16),
        "tensor",
        scatter_dimension=0,
        tiled=True,
    ).astype(jnp.float32)


def grad_rows_of(values):
    return lax.all_gather(values, "tensor", axis=0, tiled=True)


def fetch_again(values):
    return jax.tree.map(
        lambda part, own: part.astype(own.dtype),
        lax.all_gather(for_sending(values), "tensor", axis=0, tiled=True),
        values,
    )


def per_device(
    tokens,
    memory,
    self_qkv,
    self_out,
    cross_q,
    cross_kv,
    cross_out,
    hidden_weight,
    hidden_bias,
    output_weight,
    output_bias,
    norm_gain,
    norm_shift,
    grad_output,
):
    head_width = self_out.shape[0]
    local_heads = head_width // DH
    tokens_all, memory_all = (
        lax.all_gather(tokens, "tensor", axis=0, tiled=True),
        lax.all_gather(memory, "tensor", axis=0, tiled=True),
    )
    seq_count = tokens_all.shape[0] // LEN
    qkv_weight = self_qkv.reshape(self_qkv.shape[0], -1)
    mixed = jnp.dot(tokens_all, qkv_weight, preferred_element_type=jnp.float32).astype(jnp.bfloat16)
    mixed = mixed.reshape(seq_count, LEN, 3, local_heads, DH)
    self_query, self_key, self_value = (mixed[:, :, 0], mixed[:, :, 1], mixed[:, :, 2])
    self_attended, self_lse = attend_forward(self_query, self_key, self_value, True)
    self_heads = self_attended.astype(jnp.bfloat16).reshape(-1, head_width)
    branch_one = reduce_forward(self_heads, self_out)
    normed_one, pull_one = jax.vjp(
        normalize,
        residual_alpha * tokens.astype(jnp.float32) + branch_one,
        norm_gain[0],
        norm_shift[0],
    )
    normed_one_low = normed_one.astype(jnp.bfloat16)
    normed_one_all = lax.all_gather(normed_one_low, "tensor", axis=0, tiled=True)
    cross_queries = jnp.dot(normed_one_all, cross_q, preferred_element_type=jnp.float32).astype(
        jnp.bfloat16
    )
    cross_queries = cross_queries.reshape(seq_count, LEN, local_heads, DH)
    kv_weight = cross_kv.reshape(cross_kv.shape[0], -1)
    memory_mixed = jnp.dot(memory_all, kv_weight, preferred_element_type=jnp.float32).astype(
        jnp.bfloat16
    )
    memory_mixed = memory_mixed.reshape(seq_count, MEM, 2, local_heads, DH)
    cross_keys, cross_values = (memory_mixed[:, :, 0], memory_mixed[:, :, 1])
    cross_attended, cross_lse = attend_forward(cross_queries, cross_keys, cross_values, False)
    cross_heads = cross_attended.astype(jnp.bfloat16).reshape(-1, head_width)
    branch_two = reduce_forward(cross_heads, cross_out)
    normed_two, pull_two = jax.vjp(
        normalize, residual_alpha * normed_one + branch_two, norm_gain[1], norm_shift[1]
    )
    normed_two_low = normed_two.astype(jnp.bfloat16)
    normed_two_all = lax.all_gather(normed_two_low, "tensor", axis=0, tiled=True)
    hidden_pre = (
        jnp.dot(normed_two_all, hidden_weight, preferred_element_type=jnp.float32) + hidden_bias
    )
    activated, gelu_pull = jax.vjp(gelu_tanh, hidden_pre)
    activated_low = activated.astype(jnp.bfloat16)
    piece_rows = activated_low
    branch_three = lax.psum_scatter(
        jnp.dot(piece_rows, output_weight, preferred_element_type=jnp.float32).astype(jnp.bfloat16),
        "tensor",
        scatter_dimension=0,
        tiled=True,
    ).astype(jnp.float32)
    layer_out, pull_three = jax.vjp(
        normalize,
        residual_alpha * normed_two + branch_three + output_bias,
        norm_gain[2],
        norm_shift[2],
    )
    grad_three, gain_three, shift_three = pull_three(grad_output.astype(jnp.float32))
    bias_out_grad = jnp.sum(grad_three, axis=0)
    grad_three_low = grad_three.astype(jnp.bfloat16)
    grad_three_all = lax.all_gather(grad_three_low, "tensor", axis=0, tiled=True)
    out_weight_grad = weight_grad(activated_low, grad_three_all)
    grad_act = back_product(grad_three_all, output_weight)
    grad_hidden = gelu_pull(grad_act)[0].astype(jnp.bfloat16)
    hidden_bias_grad = jnp.sum(grad_hidden, axis=0, dtype=jnp.float32)
    hidden_weight_grad = weight_grad(normed_two_all, grad_hidden)
    piece_rows = grad_hidden
    grad_two_in = residual_alpha * grad_three + lax.psum_scatter(
        back_product(piece_rows, hidden_weight).astype(jnp.bfloat16),
        "tensor",
        scatter_dimension=0,
        tiled=True,
    ).astype(jnp.float32)
    grad_two, gain_two, shift_two = pull_two(grad_two_in)
    grad_two_all = grad_rows_of(grad_two.astype(jnp.bfloat16))
    cross_out_grad = weight_grad(cross_heads, grad_two_all)
    grad_cross_heads = back_product(grad_two_all, cross_out).astype(jnp.bfloat16)
    grad_cross_heads = grad_cross_heads.reshape(seq_count, LEN, local_heads, DH)
    grad_cq, grad_ck, grad_cv = attend_backward(
        cross_queries, cross_keys, cross_values, cross_lse, grad_cross_heads, False
    )
    grad_cq_low = grad_cq.astype(jnp.bfloat16).reshape(-1, head_width)
    grad_kv_low = jnp.stack([grad_ck, grad_cv], 2).astype(jnp.bfloat16).reshape(-1, 2 * head_width)
    tokens_back, memory_back = fetch_again((tokens, memory))
    normed_one_back = fetch_again(normed_one_low)
    cross_q_grad = weight_grad(normed_one_back, grad_cq_low)
    cross_kv_grad = weight_grad(memory_back, grad_kv_low).reshape(cross_kv.shape)
    grad_memory = reduce_back(grad_kv_low, kv_weight)
    grad_one_in = residual_alpha * grad_two + reduce_back(grad_cq_low, cross_q)
    grad_one, gain_one, shift_one = pull_one(grad_one_in)
    grad_one_all = grad_rows_of(grad_one.astype(jnp.bfloat16))
    self_out_grad = weight_grad(self_heads, grad_one_all)
    grad_self_heads = back_product(grad_one_all, self_out).astype(jnp.bfloat16)
    grad_self_heads = grad_self_heads.reshape(seq_count, LEN, local_heads, DH)
    grad_sq, grad_sk, grad_sv = attend_backward(
        self_query, self_key, self_value, self_lse, grad_self_heads, True
    )
    grad_mixed = (
        jnp.stack([grad_sq, grad_sk, grad_sv], 2).astype(jnp.bfloat16).reshape(-1, 3 * head_width)
    )
    self_qkv_grad = weight_grad(tokens_back, grad_mixed).reshape(self_qkv.shape)
    grad_tokens = residual_alpha * grad_one + reduce_back(grad_mixed, qkv_weight)
    (
        self_qkv_grad,
        self_out_grad,
        cross_q_grad,
        cross_kv_grad,
        cross_out_grad,
        hidden_weight_grad,
        hidden_bias_grad,
        out_weight_grad,
    ) = (
        lax.psum(self_qkv_grad.astype(jnp.bfloat16), "dp").astype(jnp.float32),
        lax.psum(self_out_grad.astype(jnp.bfloat16), "dp").astype(jnp.float32),
        lax.psum(cross_q_grad.astype(jnp.bfloat16), "dp").astype(jnp.float32),
        lax.psum(cross_kv_grad.astype(jnp.bfloat16), "dp").astype(jnp.float32),
        lax.psum(cross_out_grad.astype(jnp.bfloat16), "dp").astype(jnp.float32),
        lax.psum(hidden_weight_grad.astype(jnp.bfloat16), "dp").astype(jnp.float32),
        lax.psum(hidden_bias_grad.astype(jnp.bfloat16), "dp").astype(jnp.float32),
        lax.psum(out_weight_grad.astype(jnp.bfloat16), "dp").astype(jnp.float32),
    )
    gain_stack = jnp.stack([gain_one, gain_two, gain_three])
    shift_stack = jnp.stack([shift_one, shift_two, shift_three])
    gain_total, shift_total, bias_total = lax.psum(
        (gain_stack, shift_stack, bias_out_grad), ("dp", "tensor")
    )
    return (
        layer_out.astype(jnp.bfloat16),
        grad_tokens,
        grad_memory,
        self_qkv_grad,
        self_out_grad,
        cross_q_grad,
        cross_kv_grad,
        cross_out_grad,
        hidden_weight_grad,
        hidden_bias_grad,
        out_weight_grad,
        bias_total,
        gain_total,
        shift_total,
    )


def solution(mesh):
    return jax.shard_map(
        per_device,
        mesh=mesh,
        in_specs=(
            P(("dp", "tensor"), None),
            P(("dp", "tensor"), None),
            P(None, None, "tensor"),
            P("tensor", None),
            P(None, "tensor"),
            P(None, None, "tensor"),
            P("tensor", None),
            P(None, "tensor"),
            P("tensor"),
            P("tensor", None),
            P(),
            P(),
            P(),
            P(("dp", "tensor"), None),
        ),
        out_specs=(
            P(("dp", "tensor"), None),
            P(("dp", "tensor"), None),
            P(("dp", "tensor"), None),
            P(None, None, "tensor"),
            P("tensor", None),
            P(None, "tensor"),
            P(None, None, "tensor"),
            P("tensor", None),
            P(None, "tensor"),
            P("tensor"),
            P("tensor", None),
            P(),
            P(),
            P(),
        ),
        check_vma=False,
    )
```

profile of v0, /device:TPU:0, one launch (start us, length us, event | category | flops | bytes accessed | tf_op | source)
XLA Modules:
  0.0 2033.6 jit_solution(14718104662921084152)
XLA Ops:
  12.4 99.6 %all-gather.8.cloned.1.call-done = bf16[3072,1024]{1,0:T(8,128)(2,1)} async-done(((bf16[384,1024]{1,0:T(8,128)(2,1)}), bf16[3072,1024]{1,0:T(8,128)(2,1)}) %all-gather.8.cloned.1.call-update) | async-done | bytes 6291472 | tf_op jit(solution)/shard_map/all_gather | solution.py:173
  112.0 6.4 convolution_convert_fusion.5
  118.4 4.5 reshape.248
  122.9 6.4 fusion.105
  161.5 6.4 fusion.114
  168.8 204.7 %reduce-scatter.8.cloned.1.call-done = f32[384,1024]{1,0:T(8,128)} async-done(((f32[3072,1024]{1,0:T(8,128)}), f32[384,1024]{1,0:T(8,128)}) %reduce-scatter.8.cloned.1.call-update) | async-done | bytes 1572880 | tf_op jit(solution)/shard_map/reduce_scatter | solution.py:120
  376.9 97.1 %all-gather.10.cloned.1.call-done = bf16[3072,1024]{1,0:T(8,128)(2,1)} async-done(((bf16[384,1024]{1,0:T(8,128)(2,1)}), bf16[3072,1024]{1,0:T(8,128)(2,1)}) %all-gather.10.cloned.1.call-update) | async-done | bytes 6291472 | tf_op jit(solution)/shard_map/all_gather | solution.py:174
  473.9 5.8 convolution_convert_fusion.6
  479.8 6.6 reshape.249
  486.3 5.2 fusion.106
  491.5 4.7 copy.78
  499.8 74.0 %all-gather.12.cloned.1.call-done = bf16[3072,1024]{1,0:T(8,128)(2,1)} async-done(((bf16[384,1024]{1,0:T(8,128)(2,1)}), bf16[3072,1024]{1,0:T(8,128)(2,1)}) %all-gather.12.cloned.1.call-update) | async-done | bytes 6291472 | tf_op jit(solution)/shard_map/all_gather | solution.py:191
  573.8 5.5 convolution_convert_fusion.9
  612.6 6.4 fusion.115
  619.1 205.5 %reduce-scatter.10.cloned.1.call-done = f32[384,1024]{1,0:T(8,128)} async-done(((f32[3072,1024]{1,0:T(8,128)}), f32[384,1024]{1,0:T(8,128)}) %reduce-scatter.10.cloned.1.call-update) | async-done | bytes 1572880 | tf_op jit(solution)/shard_map/reduce_scatter | solution.py:120
  829.0 98.2 %all-gather.14.cloned.1.call-done = bf16[3072,1024]{1,0:T(8,128)(2,1)} async-done(((bf16[384,1024]{1,0:T(8,128)(2,1)}), bf16[3072,1024]{1,0:T(8,128)(2,1)}) %all-gather.14.cloned.1.call-update) | async-done | bytes 6291472 | tf_op jit(solution)/shard_map/all_gather | solution.py:209
  927.2 5.8 fusion.116
  935.6 6.1 convolution_convert_fusion.2
  941.8 116.2 %reduce-scatter.12.cloned.1.call-done = bf16[384,1024]{1,0:T(8,128)(2,1)} async-done(((bf16[3072,1024]{1,0:T(8,128)(2,1)}), bf16[384,1024]{1,0:T(8,128)(2,1)}) %reduce-scatter.12.cloned.1.call-update) | async-done | bytes 786448 | tf_op jit(solution)/shard_map/reduce_scatter | solution.py:216
  1067.0 98.3 %all-gather.16.cloned.1.call-done = bf16[3072,1024]{1,0:T(8,128)(2,1)} async-done(((bf16[384,1024]{1,0:T(8,128)(2,1)}), bf16[3072,1024]{1,0:T(8,128)(2,1)}) %all-gather.16.cloned.1.call-update) | async-done | bytes 6291472 | tf_op jit(solution)/shard_map/all_gather | solution.py:231
  1165.2 11.8 fusion.97
  1178.7 5.6 convolution_convert_fusion.1
  1184.4 116.2 %reduce-scatter.14.cloned.1.call-done = bf16[384,1024]{1,0:T(8,128)(2,1)} async-done(((bf16[3072,1024]{1,0:T(8,128)(2,1)}), bf16[384,1024]{1,0:T(8,128)(2,1)}) %reduce-scatter.14.cloned.1.call-update) | async-done | bytes 786448 | tf_op jit(solution)/shard_map/reduce_scatter | solution.py:238
  1309.5 98.2 %all-gather.18.cloned.1.call-done = bf16[3072,1024]{1,0:T(8,128)(2,1)} async-done(((bf16[384,1024]{1,0:T(8,128)(2,1)}), bf16[3072,1024]{1,0:T(8,128)(2,1)}) %all-gather.18.cloned.1.call-update) | async-done | bytes 6291472 | tf_op jit(solution)/shard_map/all_gather | solution.py:143
  1407.7 5.5 convolution_convert_fusion.8
  1426.8 10.4 multiply_reduce_fusion.3
  1437.3 9.6 multiply_convert_fusion.3
  1449.0 6.2 multiply_reduce_fusion.2
  1455.2 6.6 multiply_convert_fusion.2
  1469.6 116.1 %reduce-scatter.16.cloned.1.call-done = bf16[384,1024]{1,0:T(8,128)(2,1)} async-done(((bf16[3072,1024]{1,0:T(8,128)(2,1)}), bf16[384,1024]{1,0:T(8,128)(2,1)}) %reduce-scatter.16.cloned.1.call-update) | async-done | bytes 786448 | tf_op jit(solution)/shard_map/reduce_scatter | solution.py:134
  1600.4 7.2 fusion.8
  1618.3 8.3 convolution_convert_fusion.11
  1626.7 9.3 convolution_convert_fusion.10
  1639.4 4.5 convolution_convert_fusion.14
  1644.0 5.3 convolution_convert_fusion.15
  1649.3 42.6 %all-gather.20.cloned.1.call-done = bf16[3072,1024]{1,0:T(8,128)(2,1)} async-done(((bf16[384,1024]{1,0:T(8,128)(2,1)}), bf16[3072,1024]{1,0:T(8,128)(2,1)}) %all-gather.20.cloned.1.call-update) | async-done | bytes 6291472 | tf_op jit(solution)/shard_map/all_gather | solution.py:143
  1691.9 4.6 convolution_convert_fusion.7
  1702.1 10.4 multiply_reduce_fusion.1
  1712.5 9.8 multiply_convert_fusion.1
  1725.1 6.4 multiply_reduce_fusion
  1731.4 6.4 multiply_convert_fusion
  1760.8 4.6 convolution_convert_fusion.16
  1765.4 6.5 convolution_convert_fusion.4
  1772.6 6.0 psum.83
  1779.2 32.4 %reduce-scatter.20.cloned.1.call-done = bf16[384,1024]{1,0:T(8,128)(2,1)} async-done(((bf16[3072,1024]{1,0:T(8,128)(2,1)}), bf16[384,1024]{1,0:T(8,128)(2,1)}) %reduce-scatter.20.cloned.1.call-update) | async-done | bytes 786448 | tf_op jit(solution)/shard_map/reduce_scatter | solution.py:134
  1814.2 41.2 %all-reduce = (f32[1024]{0:T(1024)}, f32[3,1024]{1,0:T(4,128)}, f32[3,1024]{1,0:T(4,128)}) all-reduce(f32[1024]{0:T(1024)S(1)} %copy-done.73, f32[3,1024]{1,0:T(4,128)S(1)} %get-tuple-element.82, f32[3,1024]{1,0:T(4,128)S(1)} %get-tuple-element.83), channel_id=1, replica_groups=mesh['dp'=4,'tensor'=8] {'dp','tensor'}, use_global_device_ids=true, to_apply=%region_41.42 | all-reduce | flops 7168 | bytes 57344 | tf_op jit(solution)/shard_map/psum | solution.py:294
  1855.4 46.9 %all-reduce.4.cloned.1.call-done = (bf16[1024,3,128]{2,0,1:T(8,128)(2,1)}, bf16[128,1024]{1,0:T(8,128)(2,1)}, bf16[1024,128]{1,0:T(8,128)(2,1)}, bf16[1024,2,128...) async-done(((bf16[1024,3,128]{2,0,1:T(8,128)(2,1)}, bf16[128,1024]{1,0:T(8,128)(2,1)}, ...) | async-done | bytes 4194320 | tf_op jit(solution)/shard_map/psum | solution.py:283
  1915.8 108.5 %reduce-scatter.18.cloned.1.call-done = bf16[384,1024]{1,0:T(8,128)(2,1)} async-done(((bf16[3072,1024]{1,0:T(8,128)(2,1)}), bf16[384,1024]{1,0:T(8,128)(2,1)}) %reduce-scatter.18.cloned.1.call-update) | async-done | bytes 786448 | tf_op jit(solution)/shard_map/reduce_scatter | solution.py:134
  (353 shorter events, 207.2 us)
Async XLA Ops:
  7.2 928.5 %copy-start = (bf16[512,1024]{1,0:T(8,128)(2,1)S(1)}, bf16[512,1024]{1,0:T(8,128)(2,1)}, u32[]{:S(2)}) copy-start(bf16[512,1024]{1,0:T(8,128)(2,1)} %param.23) | copy-start | bytes 3145732
  7.2 104.8 %all-gather.8.cloned.1.call-start = ((), (), s32[]{:S(2)}) async-start(), calls=%async_computation.7 | async-start | bytes 7077888 | tf_op jit(solution)/shard_map/all_gather | solution.py:173
  7.9 365.6 %reduce-scatter.8.cloned.1.call-start = ((), (), s32[]{:S(2)}) async-start(), calls=%async_computation.8 | async-start | bytes 14155776 | tf_op jit(solution)/shard_map/reduce_scatter | solution.py:120
  168.0 205.6 %copy-start.34 = (bf16[384,1024]{1,0:T(8,128)(2,1)S(1)}, bf16[384,1024]{1,0:T(8,128)(2,1)}, u32[]{:S(2)}) copy-start(bf16[384,1024]{1,0:T(8,128)(2,1)} %param.14) | copy-start | bytes 2359300
  168.0 306.0 %all-gather.10.cloned.1.call-start = ((), (), s32[]{:S(2)}) async-start(), calls=%async_computation.9 | async-start | bytes 7077888 | tf_op jit(solution)/shard_map/all_gather | solution.py:174
  168.7 405.1 %all-gather.12.cloned.1.call-start = ((), (), s32[]{:S(2)}) async-start(), calls=%async_computation.10 | async-start | bytes 7077888 | tf_op jit(solution)/shard_map/all_gather | solution.py:191
  375.3 449.3 %copy-start.51 = (f32[384]{0:T(512)}, f32[384]{0:T(512)S(1)}, u32[]{:S(2)}) copy-start(f32[384]{0:T(512)S(1)} %broadcast_multiply_fusion.2) | copy-start | bytes 4612
  375.6 104.2 %copy-start.65 = (f32[384]{0:T(512)}, f32[384]{0:T(512)S(1)}, u32[]{:S(2)}) copy-start(f32[384]{0:T(512)S(1)} %multiply_reduce_fusion.12) | copy-start | bytes 4612
  375.6 449.0 %copy-start.53 = (f32[384]{0:T(512)}, f32[384]{0:T(512)S(1)}, u32[]{:S(2)}) copy-start(f32[384]{0:T(512)S(1)} %fusion.88) | copy-start | bytes 4612
  376.8 447.7 %reduce-scatter.10.cloned.1.call-start = ((), (), s32[]{:S(2)}) async-start(), calls=%async_computation.11 | async-start | bytes 14155776 | tf_op jit(solution)/shard_map/reduce_scatter | solution.py:120
  619.0 210.0 %copy-start.79 = (bf16[512]{0:T(512)(128)(2,1)S(1)}, bf16[512]{0:T(512)(128)(2,1)}, u32[]{:S(2)}) copy-start(bf16[512]{0:T(512)(128)(2,1)} %param.22) | copy-start | bytes 3076
  619.0 308.2 %all-gather.14.cloned.1.call-start = ((), (), s32[]{:S(2)}) async-start(), calls=%async_computation.12 | async-start | bytes 7077888 | tf_op jit(solution)/shard_map/all_gather | solution.py:209
  828.9 229.1 %reduce-scatter.12.cloned.1.call-start = ((), (), s32[]{:S(2)}) async-start(), calls=%async_computation.13 | async-start | bytes 7077888 | tf_op jit(solution)/shard_map/reduce_scatter | solution.py:216
  829.0 336.2 %copy-start.77 = (f32[512]{0:T(512)}, f32[512]{0:T(512)S(1)}, u32[]{:S(2)}) copy-start(f32[512]{0:T(512)S(1)} %convert_element_type.228) | copy-start | bytes 6148
  941.7 116.3 %copy-start.76 = (f32[1024]{0:T(1024)S(1)}, f32[1024]{0:T(1024)}, u32[]{:S(2)}) copy-start(f32[1024]{0:T(1024)} %param.24) | copy-start | bytes 12292
  941.7 223.5 %all-gather.16.cloned.1.call-start = ((), (), s32[]{:S(2)}) async-start(), calls=%async_computation.14 | async-start | bytes 7077888 | tf_op jit(solution)/shard_map/all_gather | solution.py:231
  1066.9 233.7 %reduce-scatter.14.cloned.1.call-start = ((), (), s32[]{:S(2)}) async-start(), calls=%async_computation.15 | async-start | bytes 7077888 | tf_op jit(solution)/shard_map/reduce_scatter | solution.py:238
  1184.3 223.4 %copy-start.43 = (bf16[128,1024]{1,0:T(8,128)(2,1)S(1)}, bf16[128,1024]{1,0:T(8,128)(2,1)}, u32[]{:S(2)}) copy-start(bf16[128,1024]{1,0:T(8,128)(2,1)} %param.20) | copy-start | bytes 786436
  1184.3 223.4 %all-gather.18.cloned.1.call-start = ((), (), s32[]{:S(2)}) async-start(), calls=%async_computation.16 | async-start | bytes 7077888 | tf_op jit(solution)/shard_map/all_gather | solution.py:143
  1309.4 276.4 %reduce-scatter.16.cloned.1.call-start = ((), (), s32[]{:S(2)}) async-start(), calls=%async_computation.17 | async-start | bytes 7077888 | tf_op jit(solution)/shard_map/reduce_scatter | solution.py:134
  1309.4 145.8 %copy-start.48 = (f32[3,2,512]{2,1,0:T(2,128)}, f32[3,2,512]{2,1,0:T(2,128)S(1)}, u32[]{:S(2)}) copy-start(f32[3,2,512]{2,1,0:T(2,128)S(1)} %log_add_fusion.2) | copy-start | bytes 36868
  1309.5 117.4 %copy-start.23 = (bf16[3,1024,1,2,64]{1,4,3,0,2:T(8,128)(2,1)S(1)}, bf16[3,1024,1,2,64]{1,4,3,0,2:T(8,128)(2,1)}, u32[]{:S(2)}) copy-start(bf16[3,1024,1,2,64]{1,4,3,0,2:T(8,128)(2,1)} %copy.78) | copy-start | bytes 2359300
  1465.0 120.8 %copy-start.52 = (f32[384]{0:T(512)S(1)}, f32[384]{0:T(512)}, u32[]{:S(2)}) copy-start(f32[384]{0:T(512)} %copy-done.51) | copy-start | bytes 4612
  1465.0 120.7 %copy-start.54 = (f32[384]{0:T(512)S(1)}, f32[384]{0:T(512)}, u32[]{:S(2)}) copy-start(f32[384]{0:T(512)} %copy-done.53) | copy-start | bytes 4612
  1465.1 120.7 %copy-start.64 = (f32[384]{0:T(512)S(1)}, f32[384]{0:T(512)}, u32[]{:S(2)}) copy-start(f32[384]{0:T(512)} %copy-done.63) | copy-start | bytes 4612
  1469.5 119.4 %copy-start.66 = (f32[384]{0:T(512)S(1)}, f32[384]{0:T(512)}, u32[]{:S(2)}) copy-start(f32[384]{0:T(512)} %copy-done.65) | copy-start | bytes 4612
  1469.5 124.1 %copy-start.56 = (f32[3,2,512]{2,1,0:T(2,128)S(1)}, f32[3,2,512]{2,1,0:T(2,128)}, u32[]{:S(2)}) copy-start(f32[3,2,512]{2,1,0:T(2,128)} %copy-done.55) | copy-start | bytes 36868
  1469.5 124.1 %copy-start.60 = (f32[3,2,512]{2,1,0:T(2,128)S(1)}, f32[3,2,512]{2,1,0:T(2,128)}, u32[]{:S(2)}) copy-start(f32[3,2,512]{2,1,0:T(2,128)} %copy-done.59) | copy-start | bytes 36868
  1469.6 124.7 %copy-start.58 = (f32[3,2,512]{2,1,0:T(2,128)S(1)}, f32[3,2,512]{2,1,0:T(2,128)}, u32[]{:S(2)}) copy-start(f32[3,2,512]{2,1,0:T(2,128)} %copy-done.57) | copy-start | bytes 36868
  1469.6 124.7 %copy-start.62 = (f32[3,2,512]{2,1,0:T(2,128)S(1)}, f32[3,2,512]{2,1,0:T(2,128)}, u32[]{:S(2)}) copy-start(f32[3,2,512]{2,1,0:T(2,128)} %copy-done.61) | copy-start | bytes 36868
  1469.6 125.3 %copy-start.27 = (bf16[3,512,2,64]{1,3,2,0:T(8,128)(2,1)S(1)}, bf16[3,512,2,64]{1,3,2,0:T(8,128)(2,1)}, u32[]{:S(2)}) copy-start(bf16[3,512,2,64]{1,3,2,0:T(8,128)(2,1)} %copy.79) | copy-start | bytes 1179652
  1469.6 222.3 %all-gather.20.cloned.1.call-start = ((), (), s32[]{:S(2)}) async-start(), calls=%async_computation.18 | async-start | bytes 7077888 | tf_op jit(solution)/shard_map/all_gather | solution.py:143
  1593.6 218.1 %reduce-scatter.20.cloned.1.call-start = ((), (), s32[]{:S(2)}) async-start(), calls=%async_computation.20 | async-start | bytes 7077888 | tf_op jit(solution)/shard_map/reduce_scatter | solution.py:134
  1618.0 284.3 %all-reduce.4.cloned.1.call-start = ((), (), s32[]{:S(2)}) async-start(), calls=%async_computation.21 | async-start | bytes 8388608 | tf_op jit(solution)/shard_map/psum | solution.py:283
  1639.4 52.5 %copy-start.45 = (bf16[128,1024]{1,0:T(8,128)(2,1)S(1)}, bf16[128,1024]{1,0:T(8,128)(2,1)}, u32[]{:S(2)}) copy-start(bf16[128,1024]{1,0:T(8,128)(2,1)} %param.17) | copy-start | bytes 786436
  1649.3 52.7 %copy-start.21 = (bf16[3,1024,1,2,64]{1,4,3,0,2:T(8,128)(2,1)S(1)}, bf16[3,1024,1,2,64]{1,4,3,0,2:T(8,128)(2,1)}, u32[]{:S(2)}) copy-start(bf16[3,1024,1,2,64]{1,4,3,0,2:T(8,128)(2,1)} %copy-done.20) | copy-start | bytes 2359300
  1649.3 52.7 %copy-start.47 = (f32[3,2,512]{2,1,0:T(2,128)S(1)}, f32[3,2,512]{2,1,0:T(2,128)}, u32[]{:S(2)}) copy-start(f32[3,2,512]{2,1,0:T(2,128)} %log_add_fusion.1) | copy-start | bytes 36868
  1702.1 23.0 %slice-start.6 = ((s8[12582912]{0:T(1024)(128)(4,1)}), s8[4194304]{0:T(1024)(128)(4,1)S(1)}, s32[]{:S(2)}) async-start(s8[12582912]{0:T(1024)(128)(4,1)} %bitcast.199), calls=%async_computation.28 | async-start | bytes 8388608
  1765.4 258.9 %reduce-scatter.18.cloned.1.call-start = ((), (), s32[]{:S(2)}) async-start(), calls=%async_computation.19 | async-start | bytes 7077888 | tf_op jit(solution)/shard_map/reduce_scatter | solution.py:134
  1772.0 42.1 %copy-start.67 = (f32[1024]{0:T(1024)S(1)}, f32[1024]{0:T(1024)}, u32[]{:S(2)}) copy-start(f32[1024]{0:T(1024)} %get-tuple-element.20) | copy-start | bytes 12292
  1772.0 42.1 %copy-start.68 = (f32[1024]{0:T(1024)S(1)}, f32[1024]{0:T(1024)}, u32[]{:S(2)}) copy-start(f32[1024]{0:T(1024)} %get-tuple-element.23) | copy-start | bytes 12292
  1772.0 42.1 %copy-start.69 = (f32[1024]{0:T(1024)S(1)}, f32[1024]{0:T(1024)}, u32[]{:S(2)}) copy-start(f32[1024]{0:T(1024)} %get-tuple-element.14) | copy-start | bytes 12292
  1772.0 42.1 %copy-start.70 = (f32[1024]{0:T(1024)S(1)}, f32[1024]{0:T(1024)}, u32[]{:S(2)}) copy-start(f32[1024]{0:T(1024)} %get-tuple-element.18) | copy-start | bytes 12292
  1772.0 42.1 %copy-start.71 = (f32[1024]{0:T(1024)S(1)}, f32[1024]{0:T(1024)}, u32[]{:S(2)}) copy-start(f32[1024]{0:T(1024)} %get-tuple-element.16) | copy-start | bytes 12292
  1772.0 42.1 %copy-start.72 = (f32[1024]{0:T(1024)S(1)}, f32[1024]{0:T(1024)}, u32[]{:S(2)}) copy-start(f32[1024]{0:T(1024)} %get-tuple-element.19) | copy-start | bytes 12292
  1772.0 42.1 %copy-start.73 = (f32[1024]{0:T(1024)S(1)}, f32[1024]{0:T(1024)}, u32[]{:S(2)}) copy-start(f32[1024]{0:T(1024)} %get-tuple-element.22) | copy-start | bytes 12292
  1902.3 122.0 %copy-start.13 = (f32[384,1024]{1,0:T(8,128)S(1)}, f32[384,1024]{1,0:T(8,128)}, u32[]{:S(2)}) copy-start(f32[384,1024]{1,0:T(8,128)} %copy-done.12) | copy-start | bytes 4718596
  1907.8 119.0 %copy-start.1 = (bf16[512,1024]{1,0:T(8,128)(2,1)S(1)}, bf16[512,1024]{1,0:T(8,128)(2,1)}, u32[]{:S(2)}) copy-start(bf16[512,1024]{1,0:T(8,128)(2,1)} %param.23) | copy-start | bytes 3145732
  (69 other events, 431.4 us)
Sparse Core Ops, SparseCore 0:
  10.2 101.7 all-gather.7
  168.1 205.4 reduce-scatter.7
  375.8 98.1 all-gather.9
  476.6 97.1 all-gather.11
  619.1 205.3 reduce-scatter.9
  829.0 98.1 all-gather.13
  941.9 116.1 reduce-scatter.11
  1067.0 98.1 all-gather.15
  1184.4 116.1 reduce-scatter.13
  1309.5 98.1 all-gather.17
  1469.6 116.0 reduce-scatter.15
  1593.7 98.1 all-gather.19
  1695.5 116.1 reduce-scatter.19
  1815.5 86.7 all-reduce.3
  1906.2 118.0 reduce-scatter.17
where the time goes:
time: 2040 us; the launch traced here: 2030 us
  waiting for transfers between devices  1560 us (76%)
  matrix products  216 us (11%)
  local copies, waits for them, and re-layouts  101 us (5%)
  other arithmetic  96.4 us (5%)
  blocking collectives  47.2 us (2%)
    reduce_scatter x2, waiting for transfers between devices, reduce_forward(): lax.psum_scatter(row_term(jnp.int32(0), lax.axis_size('tensor') * own_row...  410 us
    reduce_scatter x3, waiting for transfers between devices, reduce_back(): lax.psum_scatter(row_term(jnp.int32(0), own_rows * lax.axis_size('tensor'...  257 us
    all_gather x2, waiting for transfers between devices, grad_rows_of(): return lax.all_gather(values, 'tensor', axis=0, tiled=True)  141 us
    reduce_scatter x1, waiting for transfers between devices, per_device(): lax.psum_scatter(jnp.dot(piece_rows, output_weight, preferred_element_typ...  116 us
    reduce_scatter x1, waiting for transfers between devices, per_device(): lax.psum_scatter(back_product(piece_rows, hidden_weight).astype(jnp.bfloa...  116 us
    all_gather x1, waiting for transfers between devices, per_device(): lax.all_gather(tokens, 'tensor', axis=0, tiled=True)  99.6 us
    all_gather x1, waiting for transfers between devices, per_device(): lax.all_gather(grad_three_low, 'tensor', axis=0, tiled=True)  98.3 us
    all_gather x1, waiting for transfers between devices, per_device(): lax.all_gather(normed_two_low, 'tensor', axis=0, tiled=True)  98.2 us
  transfers between devices with their start and end apart: 15, of which 15 were waited for; matrix products, arithmetic and copies ran while one was open for 9% of the time, Pallas kernels for 0%

commit v1 on v0

v1 whole, which is shorter than its diff:
```python
import functools
import math

import jax
import jax.numpy as jnp
from jax import lax
from jax.experimental import pallas as pl
from jax.experimental.pallas import tpu as pltpu
from jax.sharding import PartitionSpec as P

MESH = pl.DeviceIdType.MESH
DH = 64
LANES = 128
LEN = 1024

residual_alpha = 300.0**0.25
norm_eps = 1e-05

def greet(peers):
    barrier = pltpu.get_barrier_semaphore()
    for p in peers:
        pl.semaphore_signal(barrier, inc=1, device_id={"tensor": p}, device_id_type=MESH)
    pl.semaphore_wait(barrier, len(peers))

def to_heads_kernel(count, tsize, pairs, block, *refs):
    ins, outs = refs[:count], refs[count:2*count]
    send_sem, recv_sem = refs[2*count:]
    me = lax.axis_index("tensor")
    blocks = ins[0].shape[0] // block
    per_seq = LEN // block
    wide = ins[0].shape[1] // LANES
    seqs = tsize * blocks // per_seq
    greet([lax.rem(me + i, tsize) for i in range(1, tsize)])
    def unit(a, u):
        j, p = u // wide, u % wide
        g = me * blocks + j
        q = (g // per_seq) * wide + p
        dst, slot, k = q // pairs, q % pairs, g % per_seq
        src = ins[a].at[pl.ds(pl.multiple_of(j * block, block), block), pl.ds(pl.multiple_of(p * LANES, LANES), LANES)]
        to = outs[a].at[slot, pl.ds(pl.multiple_of(k * block, block), block), :]
        return dst, src, to, send_sem.at[a, u], recv_sem.at[a, slot * per_seq + k]
    for a in range(count):
        def start(u, _):
            dst, src, to, ss, rs = unit(a, u)
            @pl.when(dst == me)
            def _():
                pltpu.make_async_copy(src, to, rs).start()
            @pl.when(dst != me)
            def _():
                pltpu.make_async_remote_copy(src, to, ss, rs, device_id={"tensor": dst}, device_id_type=MESH).start()
            return 0
        lax.fori_loop(0, blocks * wide, start, 0)
    for a in range(count):
        def done(u, _):
            dst, src, to, ss, rs = unit(a, u)
            @pl.when(dst != me)
            def _():
                pltpu.make_async_remote_copy(src, to, ss, rs, device_id={"tensor": dst}, device_id_type=MESH).wait_send()
            return 0
        lax.fori_loop(0, blocks * wide, done, 0)
        def got(r, _):
            slot, k = r // per_seq, r % per_seq
            @pl.when(me * pairs + slot < seqs * wide)
            def _():
                to = outs[a].at[slot, pl.ds(pl.multiple_of(k * block, block), block), :]
                pltpu.make_async_copy(to, to, recv_sem.at[a, r]).wait()
            return 0
        lax.fori_loop(0, pairs * per_seq, got, 0)

def to_heads(arrays, tsize, cid):
    n, d = arrays[0].shape
    block = math.gcd(n, LEN)
    wide = d // LANES
    seqs = n * tsize // LEN
    pairs = -(-seqs * wide // tsize)
    count = len(arrays)
    return pl.pallas_call(
        functools.partial(to_heads_kernel, count, tsize, pairs, block),
        out_shape=[jax.ShapeDtypeStruct((pairs, LEN, LANES), jnp.bfloat16)] * count,
        in_specs=[pl.BlockSpec(memory_space=pl.ANY)] * count,
        out_specs=[pl.BlockSpec(memory_space=pl.ANY)] * count,
        scratch_shapes=[pltpu.SemaphoreType.DMA((count, n // block * wide)), pltpu.SemaphoreType.DMA((count, pairs * LEN // block))],
        compiler_params=pltpu.CompilerParams(collective_id=cid, has_side_effects=True),
    )(*arrays)

def to_tokens_kernel(count, tsize, pairs, block, *refs):
    ins, outs = refs[:count], refs[count:2*count]
    send_sem, recv_sem = refs[2*count:]
    me = lax.axis_index("tensor")
    blocks = outs[0].shape[0] // block
    per_seq = LEN // block
    wide = outs[0].shape[1] // LANES
    seqs = tsize * blocks // per_seq
    greet([lax.rem(me + i, tsize) for i in range(1, tsize)])
    def unit(a, u):
        slot, k = u // per_seq, u % per_seq
        q = me * pairs + slot
        g = (q // wide) * per_seq + k
        dst, j, p = g // blocks, g % blocks, q % wide
        src = ins[a].at[slot, pl.ds(pl.multiple_of(k * block, block), block), :]
        to = outs[a].at[pl.ds(pl.multiple_of(j * block, block), block), pl.ds(pl.multiple_of(p * LANES, LANES), LANES)]
        return q < seqs * wide, dst, src, to, send_sem.at[a, u], recv_sem.at[a, j * wide + p]
    for a in range(count):
        def start(u, _):
            real, dst, src, to, ss, rs = unit(a, u)
            @pl.when(real & (dst == me))
            def _():
                pltpu.make_async_copy(src, to, rs).start()
            @pl.when(real & (dst != me))
            def _():
                pltpu.make_async_remote_copy(src, to, ss, rs, device_id={"tensor": dst}, device_id_type=MESH).start()
            return 0
        lax.fori_loop(0, pairs * per_seq, start, 0)
    for a in range(count):
        def done(u, _):
            real, dst, src, to, ss, rs = unit(a, u)
            @pl.when(real & (dst != me))
            def _():
                pltpu.make_async_remote_copy(src, to, ss, rs, device_id={"tensor": dst}, device_id_type=MESH).wait_send()
            return 0
        lax.fori_loop(0, pairs * per_seq, done, 0)
        def got(r, _):
            j, p = r // wide, r % wide
            to = outs[a].at[pl.ds(pl.multiple_of(j * block, block), block), pl.ds(pl.multiple_of(p * LANES, LANES), LANES)]
            pltpu.make_async_copy(to, to, recv_sem.at[a, r]).wait()
            return 0
        lax.fori_loop(0, blocks * wide, got, 0)

def to_tokens(arrays, n, d, tsize, cid):
    pairs = arrays[0].shape[0]
    block = math.gcd(n, LEN)
    wide = d // LANES
    count = len(arrays)
    return pl.pallas_call(
        functools.partial(to_tokens_kernel, count, tsize, pairs, block),
        out_shape=[jax.ShapeDtypeStruct((n, d), jnp.bfloat16)] * count,
        in_specs=[pl.BlockSpec(memory_space=pl.ANY)] * count,
        out_specs=[pl.BlockSpec(memory_space=pl.ANY)] * count,
        scratch_shapes=[pltpu.SemaphoreType.DMA((count, pairs * LEN // block)), pltpu.SemaphoreType.DMA((count, n // block * wide))],
        compiler_params=pltpu.CompilerParams(collective_id=cid, has_side_effects=True),
    )(*arrays)

def lane_half(shape, h):
    return (lax.broadcasted_iota(jnp.int32, shape, len(shape)-1) // 64) == h

NT = (((1,), (1,)), ((), ()))
NN = (((1,), (0,)), ((), ()))
LOG2E = math.log2(math.e)
def dot(a, b, dims):
    return lax.dot_general(a, b, dims, preferred_element_type=jnp.float32)

def fwd_kernel(causal, bq, q_ref, k_ref, v_ref, o_ref, lse_ref):
    def block(i):
        keys = bq * (i + 1) if causal else LEN
        rows = pl.ds(i * bq, bq)
        q = q_ref[0, rows, :] * jnp.bfloat16(0.125)
        k = k_ref[0, :keys, :]
        total = None
        for h in (0, 1):
            qh = jnp.where(lane_half(q.shape, h), q, jnp.bfloat16(0))
            s = dot(qh, k, NT)
            if causal:
                tail = s[:, keys - bq:]
                r = lax.broadcasted_iota(jnp.int32, tail.shape, 0)
                c = lax.broadcasted_iota(jnp.int32, tail.shape, 1)
                tail = jnp.where(c <= r, tail, -1e30)
                s = tail if keys == bq else jnp.concatenate([s[:, :keys - bq], tail], 1)
            m = jnp.max(s, axis=-1, keepdims=True)
            e = jnp.exp2((s - m) * LOG2E)
            l = jnp.sum(e, axis=-1, keepdims=True)
            v = v_ref[0, :keys, :]
            o = dot(e.astype(jnp.bfloat16), v, NN) / l
            total = o if h == 0 else jnp.where(lane_half(o.shape, 0), total, o)
            lse = m * LOG2E + jnp.log2(l)
            lse_ref[0, h:h+1, rows] = jnp.transpose(jnp.broadcast_to(lse, (bq, 128)))[0:1]
        o_ref[0, rows, :] = total.astype(jnp.bfloat16)
    for i in range(LEN // bq):
        block(i)

def attend_fwd(q, k, v, causal, bq=256):
    pairs = q.shape[0]
    spec = pl.BlockSpec((1, LEN, LANES), lambda i: (i, 0, 0))
    return pl.pallas_call(
        functools.partial(fwd_kernel, causal, bq),
        grid=(pairs,),
        out_shape=[jax.ShapeDtypeStruct(q.shape, jnp.bfloat16), jax.ShapeDtypeStruct((pairs, 8, LEN), jnp.float32)],
        in_specs=[spec] * 3,
        out_specs=[spec, pl.BlockSpec((1, 8, LEN), lambda i: (i, 0, 0))],
        compiler_params=pltpu.CompilerParams(vmem_limit_bytes=48 << 20),
        cost_estimate=pl.CostEstimate(flops=pairs * 2 * 2 * 2 * LEN * LEN * 64, bytes_accessed=pairs * LEN * LANES * 8, transcendentals=pairs * 2 * LEN * LEN),
    )(q, k, v)

def bwd_kernel(causal, bq, q_ref, k_ref, v_ref, o_ref, lse_ref, do_ref, dq_ref, dk_ref, dv_ref, dk_acc, dv_acc):
    dk_acc[...] = jnp.zeros_like(dk_acc)
    dv_acc[...] = jnp.zeros_like(dv_acc)
    kt = jnp.transpose(k_ref[0])
    for i in range(LEN // bq):
        keys = bq * (i + 1) if causal else LEN
        rows = pl.ds(i * bq, bq)
        q = q_ref[0, rows, :] * jnp.bfloat16(0.125)
        do = do_ref[0, rows, :]
        prod = jnp.transpose(do.astype(jnp.float32) * o_ref[0, rows, :].astype(jnp.float32))
        k = k_ref[0, :keys, :]
        v = v_ref[0, :keys, :]
        dqt = None
        for h in (0, 1):
            mask = lane_half(q.shape, h)
            qh = jnp.where(mask, q, jnp.bfloat16(0))
            doh = jnp.where(mask, do, jnp.bfloat16(0))
            delta = jnp.sum(prod[64 * h:64 * h + 64], axis=0, keepdims=True)
            s = dot(k, qh, NT)
            p = jnp.exp2(s * LOG2E - lse_ref[0, h:h+1, rows])
            if causal:
                tail = p[keys - bq:, :]
                r = lax.broadcasted_iota(jnp.int32, tail.shape, 1)
                c = lax.broadcasted_iota(jnp.int32, tail.shape, 0)
                tail = jnp.where(c <= r, tail, 0.0)
                p = tail if keys == bq else jnp.concatenate([p[:keys - bq], tail], 0)
            dp = dot(v, doh, NT)
            ds = (p * (dp - delta)).astype(jnp.bfloat16)
            dv_acc[:keys, :] += dot(p.astype(jnp.bfloat16), doh, NN)
            dk_acc[:keys, :] += dot(ds, qh, NN)
            part = dot(kt[64 * h:64 * h + 64, :keys], ds, NN)
            dqt = part if h == 0 else jnp.concatenate([dqt, part], 0)
        dq_ref[0, rows, :] = (jnp.transpose(dqt) * 0.125).astype(jnp.bfloat16)
    dk_ref[0] = dk_acc[...].astype(jnp.bfloat16)
    dv_ref[0] = dv_acc[...].astype(jnp.bfloat16)

def attend_bwd(q, k, v, o, lse, do, causal, bq=256):
    pairs = q.shape[0]
    spec = pl.BlockSpec((1, LEN, LANES), lambda i: (i, 0, 0))
    return pl.pallas_call(
        functools.partial(bwd_kernel, causal, bq),
        grid=(pairs,),
        out_shape=[jax.ShapeDtypeStruct(q.shape, jnp.bfloat16)] * 3,
        in_specs=[spec] * 4 + [pl.BlockSpec((1, 8, LEN), lambda i: (i, 0, 0)), spec],
        out_specs=[spec] * 3,
        scratch_shapes=[pltpu.VMEM((LEN, LANES), jnp.float32)] * 2,
        compiler_params=pltpu.CompilerParams(vmem_limit_bytes=48 << 20),
        cost_estimate=pl.CostEstimate(flops=pairs * 5 * 2 * 2 * LEN * LEN * 64, bytes_accessed=pairs * LEN * LANES * 16, transcendentals=pairs * 2 * LEN * LEN),
    )(q, k, v, o, lse, do)


def cols_kernel(count, x_ref, w_ref, *outs):
    out = dot(x_ref[...], w_ref[0], NN)
    width = out.shape[1] // count
    for i, o_ref in enumerate(outs):
        o_ref[...] = out[:, i * width : (i + 1) * width].astype(o_ref.dtype)


def cols_product(x, weight, count, dtype=jnp.bfloat16):
    n, d = x.shape
    t, _, c = weight.shape
    width = c // count
    return pl.pallas_call(
        functools.partial(cols_kernel, count),
        grid=(t,),
        out_shape=[jax.ShapeDtypeStruct((n, t * width), dtype)] * count,
        in_specs=[
            pl.BlockSpec((n, d), lambda i: (0, 0)),
            pl.BlockSpec((1, d, c), lambda i: (i, 0, 0)),
        ],
        out_specs=[pl.BlockSpec((n, width), lambda i: (0, i))] * count,
        compiler_params=pltpu.CompilerParams(vmem_limit_bytes=48 << 20),
        cost_estimate=pl.CostEstimate(
            flops=2 * n * d * t * c, bytes_accessed=2 * (t * d * c + n * d + n * t * c), transcendentals=0
        ),
    )(x, weight)


def back_kernel(count, *refs):
    ys, w_ref, o_ref = refs[:count], refs[count], refs[count + 1]
    y = jnp.concatenate([y_ref[...] for y_ref in ys], 1) if count > 1 else ys[0][...]
    term = dot(y, w_ref[0], NT)

    @pl.when(pl.program_id(0) == 0)
    def _():
        o_ref[...] = term

    @pl.when(pl.program_id(0) != 0)
    def _():
        o_ref[...] += term


def back_product(ys, weight):
    count = len(ys)
    n = ys[0].shape[0]
    t, d, c = weight.shape
    width = c // count
    return pl.pallas_call(
        functools.partial(back_kernel, count),
        grid=(t,),
        out_shape=jax.ShapeDtypeStruct((n, d), jnp.float32),
        in_specs=[pl.BlockSpec((n, width), lambda i: (0, i))] * count
        + [pl.BlockSpec((1, d, c), lambda i: (i, 0, 0))],
        out_specs=pl.BlockSpec((n, d), lambda i: (0, 0)),
        compiler_params=pltpu.CompilerParams(vmem_limit_bytes=48 << 20),
        cost_estimate=pl.CostEstimate(
            flops=2 * n * d * t * c, bytes_accessed=2 * (t * d * c + 2 * n * d + n * t * c), transcendentals=0
        ),
    )(*ys, weight)


def grad_kernel(count, x_ref, *refs):
    ys, o_ref, xt_ref = refs[:count], refs[count], refs[count + 1]

    @pl.when(pl.program_id(0) == 0)
    def _():
        xt_ref[...] = jnp.transpose(x_ref[...])

    y = jnp.concatenate([y_ref[...] for y_ref in ys], 1) if count > 1 else ys[0][...]
    o_ref[0] = dot(xt_ref[...], y, NN).astype(o_ref.dtype)


def cols_grad(x, ys, t):
    count = len(ys)
    n, d = x.shape
    width = max(ys[0].shape[1] // t, LANES)
    blocks = ys[0].shape[1] // width
    c = width * count
    out = pl.pallas_call(
        functools.partial(grad_kernel, count),
        grid=(blocks,),
        out_shape=jax.ShapeDtypeStruct((blocks, d, c), jnp.bfloat16),
        in_specs=[pl.BlockSpec((n, d), lambda i: (0, 0))]
        + [pl.BlockSpec((n, width), lambda i: (0, i))] * count,
        out_specs=pl.BlockSpec((1, d, c), lambda i: (i, 0, 0)),
        scratch_shapes=[pltpu.VMEM((d, n), jnp.bfloat16)],
        compiler_params=pltpu.CompilerParams(vmem_limit_bytes=48 << 20),
        cost_estimate=pl.CostEstimate(
            flops=2 * n * d * t * c, bytes_accessed=2 * (t * d * c + n * d + n * t * c), transcendentals=0
        ),
    )(x, *ys)
    return narrow(out, count, t)


def gather_weight(weight):
    dp, t = lax.axis_size("dp"), lax.axis_size("tensor")
    rows = weight.shape[0] // dp
    share = lax.dynamic_slice_in_dim(weight, lax.axis_index("dp") * rows, rows, 0)
    whole = lax.all_gather(share, ("tensor", "dp"), axis=0, tiled=True)
    return whole.reshape(t, weight.shape[0], weight.shape[1])


def widen(weight, count):
    t, r, c = weight.shape
    width = c // count
    if width % LANES == 0:
        return weight
    m = LANES // width
    parts = weight.reshape(t // m, m, r, count, width).transpose(0, 2, 3, 1, 4)
    return parts.reshape(t // m, r, count * LANES)


def narrow(grad, count, t):
    blocks, r, c = grad.shape
    if blocks == t:
        return grad
    m = t // blocks
    parts = grad.reshape(blocks, r, count, m, c // count // m).transpose(0, 3, 1, 2, 4)
    return parts.reshape(t, r, c // m)


def swap(value, axis, bit):
    size = lax.axis_size(axis)
    return lax.ppermute(value, axis, [(i, i ^ bit) for i in range(size)])


def pick(value, index, axis):
    return lax.dynamic_index_in_dim(value, index, axis, keepdims=False)


def reduce_grad(grad):
    dp, t = lax.axis_size("dp"), lax.axis_size("tensor")
    own_dp, own_t = lax.axis_index("dp"), lax.axis_index("tensor")
    _, r, c = grad.shape
    core, side, line, depth = own_dp % 2, own_t % 2, own_t // 2, t // 2
    halves = grad.reshape(t, 2, r // 2, c)
    total = pick(halves, core, 1) + swap(pick(halves, 1 - core, 1), "dp", 1)
    pairs = total.reshape(depth, 2, r // 2, c)
    total = pick(pairs, side, 1) + swap(pick(pairs, 1 - side, 1), "tensor", 1)
    result = pick(total, line, 0)
    for sign in (1, -1):
        passed = None
        for step in range(depth - 1):
            far = line + sign * (depth - 1 - step)
            part = pick(total, jnp.clip(far, 0, depth - 1), 0)
            passed = part if passed is None else part + passed
            lines = range(step + 1) if sign == 1 else range(depth - 1 - step, depth)
            passed = lax.ppermute(
                passed, "tensor", [(2 * i + j, 2 * (i + sign) + j) for i in lines for j in range(2)]
            )
        result = result + passed
    bit = 2
    while bit < dp:
        result = result + swap(result, "dp", bit)
        bit *= 2
    other = swap(result, "dp", 1)
    first = jnp.where(core == 0, result, other)
    second = jnp.where(core == 0, other, result)
    return jnp.concatenate([first, second], 0).astype(jnp.float32)


def normalize(rows_in, gain_row, shift_row):
    row_mean = jnp.mean(rows_in, axis=-1, keepdims=True)
    centered = rows_in - row_mean
    variance = jnp.mean(centered * centered, axis=-1, keepdims=True)
    return centered * lax.rsqrt(variance + norm_eps) * gain_row + shift_row


def gelu_tanh(values):
    return jax.nn.gelu(values, approximate=True)


def product(values, weight):
    return jnp.dot(values, weight, preferred_element_type=jnp.float32)


def rows_grad(left, right, t):
    out = lax.dot_general(left, right, (((0,), (0,)), ((), ())), preferred_element_type=jnp.float32)
    return out.astype(jnp.bfloat16).reshape(t, -1, right.shape[1])


def per_device(
    tokens,
    memory,
    self_qkv,
    self_out,
    cross_q,
    cross_kv,
    cross_out,
    hidden_weight,
    hidden_bias,
    output_weight,
    output_bias,
    norm_gain,
    norm_shift,
    grad_output,
):
    low = jnp.bfloat16
    t = lax.axis_size("tensor")
    n, d = tokens.shape
    w_qkv = widen(gather_weight(self_qkv.reshape(d, -1)), 3)
    w_kv = widen(gather_weight(cross_kv.reshape(d, -1)), 2)
    w_so = gather_weight(self_out).reshape(d, d)
    w_cq = widen(gather_weight(cross_q), 1)
    w_co = gather_weight(cross_out).reshape(d, d)
    w_hid = gather_weight(hidden_weight)
    w_out = gather_weight(output_weight).reshape(-1, d)
    bias_all = lax.all_gather(hidden_bias, "tensor", axis=0, tiled=True)

    qkv = cols_product(tokens, w_qkv, 3)
    sq, sk, sv = to_heads(qkv, t, 0)
    so, s_lse = attend_fwd(sq, sk, sv, True, 512)
    (self_heads,) = to_tokens([so], n, d, t, 1)
    branch_one = product(self_heads, w_so)
    normed_one, pull_one = jax.vjp(
        normalize, residual_alpha * tokens.astype(jnp.float32) + branch_one, norm_gain[0], norm_shift[0]
    )
    normed_one_low = normed_one.astype(low)
    kv = cols_product(memory, w_kv, 2)
    cq = cols_product(normed_one_low, w_cq, 1)
    cq, ck, cv = to_heads([*cq, *kv], t, 2)
    co, c_lse = attend_fwd(cq, ck, cv, False, 512)
    (cross_heads,) = to_tokens([co], n, d, t, 3)
    branch_two = product(cross_heads, w_co)
    normed_two, pull_two = jax.vjp(
        normalize, residual_alpha * normed_one + branch_two, norm_gain[1], norm_shift[1]
    )
    normed_two_low = normed_two.astype(low)
    (hidden_low,) = cols_product(normed_two_low, w_hid, 1, jnp.float32)
    hidden_pre = hidden_low + bias_all
    activated, gelu_pull = jax.vjp(gelu_tanh, hidden_pre)
    activated_low = activated.astype(low)
    branch_three = product(activated_low, w_out)
    layer_out, pull_three = jax.vjp(
        normalize, residual_alpha * normed_two + branch_three + output_bias, norm_gain[2], norm_shift[2]
    )
    grad_three, gain_three, shift_three = pull_three(grad_output.astype(jnp.float32))
    bias_out_grad = jnp.sum(grad_three, axis=0)
    grad_three_low = grad_three.astype(low)
    out_weight_grad = reduce_grad(rows_grad(activated_low, grad_three_low, t))
    grad_act = lax.dot_general(grad_three_low, w_out, NT, preferred_element_type=jnp.float32)
    grad_hidden = gelu_pull(grad_act)[0].astype(low)
    hidden_bias_grad = jnp.sum(grad_hidden, axis=0, dtype=jnp.float32)
    hidden_weight_grad = reduce_grad(cols_grad(normed_two_low, [grad_hidden], t))
    grad_two, gain_two, shift_two = pull_two(
        residual_alpha * grad_three + back_product([grad_hidden], w_hid)
    )
    grad_two_low = grad_two.astype(low)
    cross_out_grad = reduce_grad(rows_grad(cross_heads, grad_two_low, t))
    grad_co = lax.dot_general(grad_two_low, w_co, NT, preferred_element_type=jnp.float32).astype(low)
    (grad_co,) = to_heads([grad_co], t, 4)
    cross_grads = attend_bwd(cq, ck, cv, co, c_lse, grad_co, False, 256)
    g_cq, g_ck, g_cv = to_tokens(cross_grads, n, d, t, 5)
    cross_q_grad = reduce_grad(cols_grad(normed_one_low, [g_cq], t))
    cross_kv_grad = reduce_grad(cols_grad(memory, [g_ck, g_cv], t)).reshape(cross_kv.shape)
    grad_memory = back_product([g_ck, g_cv], w_kv)
    grad_one, gain_one, shift_one = pull_one(residual_alpha * grad_two + back_product([g_cq], w_cq))
    grad_one_low = grad_one.astype(low)
    self_out_grad = reduce_grad(rows_grad(self_heads, grad_one_low, t))
    grad_so = lax.dot_general(grad_one_low, w_so, NT, preferred_element_type=jnp.float32).astype(low)
    (grad_so,) = to_heads([grad_so], t, 6)
    self_grads = attend_bwd(sq, sk, sv, so, s_lse, grad_so, True, 256)
    g_qkv = to_tokens(self_grads, n, d, t, 7)
    self_qkv_grad = reduce_grad(cols_grad(tokens, g_qkv, t)).reshape(self_qkv.shape)
    grad_tokens = residual_alpha * grad_one + back_product(g_qkv, w_qkv)
    gain_total, shift_total, bias_total, hidden_bias_total = lax.psum(
        (
            jnp.stack([gain_one, gain_two, gain_three]),
            jnp.stack([shift_one, shift_two, shift_three]),
            bias_out_grad,
            hidden_bias_grad,
        ),
        ("dp", "tensor"),
    )
    units = hidden_bias.shape[0]
    hidden_bias_total = lax.dynamic_slice_in_dim(hidden_bias_total, lax.axis_index("tensor") * units, units, 0)
    return (
        layer_out.astype(low),
        grad_tokens,
        grad_memory,
        self_qkv_grad,
        self_out_grad,
        cross_q_grad,
        cross_kv_grad,
        cross_out_grad,
        hidden_weight_grad,
        hidden_bias_total,
        out_weight_grad,
        bias_total,
        gain_total,
        shift_total,
    )


def solution(mesh):
    return jax.shard_map(
        per_device,
        mesh=mesh,
        in_specs=(
            P(("dp", "tensor"), None),
            P(("dp", "tensor"), None),
            P(None, None, "tensor"),
            P("tensor", None),
            P(None, "tensor"),
            P(None, None, "tensor"),
            P("tensor", None),
            P(None, "tensor"),
            P("tensor"),
            P("tensor", None),
            P(),
            P(),
            P(),
            P(("dp", "tensor"), None),
        ),
        out_specs=(
            P(("dp", "tensor"), None),
            P(("dp", "tensor"), None),
            P(("dp", "tensor"), None),
            P(None, None, "tensor"),
            P("tensor", None),
            P(None, "tensor"),
            P(None, None, "tensor"),
            P("tensor", None),
            P(None, "tensor"),
            P("tensor"),
            P("tensor", None),
            P(),
            P(),
            P(),
        ),
        check_vma=False,
    )
```

time: 2040 us -> 1250 us (0.61)
  waiting for transfers between devices: 1560 us -> 447 us
  Pallas kernels: 0 us -> 334 us
  matrix products: 216 us -> 44.5 us
  starting transfers between devices: 0.87 us -> 143 us
  blocking collectives: 47.2 us -> 83.3 us
  other arithmetic: 96.4 us -> 63.6 us
    reduce_scatter x7 -> x0, waiting for transfers between devices: 900 us -> none  [the longest x2 410 us: reduce_forward(): lax.psum_scatter(row_term(jnp.int32(0), lax.axis_size('tensor') * own_row...]
    pallas_call x0 -> x24, Pallas kernels: none -> 334 us  [the longest x4 106 us: to_heads(): pl.pallas_call(functools.partial(to_heads_kernel, count, tsize, pairs, bl...]
    all_gather x7, waiting for transfers between devices: 608 us -> 283 us  [gather_weight(): whole = lax.all_gather(share, ('tensor', 'dp'), axis=0, tiled=True)]
    dot_general x45 -> x9, matrix products: 216 us -> 44.5 us  [the longest x3 15.6 us: product(): return jnp.dot(values, weight, preferred_element_type=jnp.float32)]
    ppermute x0 -> x70, waiting for transfers between devices: none -> 165 us  [the longest x28 118 us: swap(): return lax.ppermute(value, axis, [(i, i ^ bit) for i in range(size)])]
    ppermute x0 -> x70, starting transfers between devices: none -> 143 us  [the longest x42 122 us: reduce_grad(): lax.ppermute(passed, 'tensor', [(2 * i + j, 2 * (i + sign) + j) for i in...]
    psum x1 -> x0, waiting for transfers between devices: 46.9 us -> none  [per_device(): lax.psum(self_qkv_grad.astype(jnp.bfloat16), 'dp').astype(jnp.float32)]
    convert_element_type x21 -> x10, other arithmetic: 54.8 us -> 8.06 us  [the longest x7 7.38 us: reduce_grad(): return jnp.concatenate([first, second], 0).astype(jnp.float32)]
  transfers between devices with their start and end apart: 15 -> 77, of which waited for: 15 -> 30; matrix products, arithmetic and copies ran while one was open for 9% -> 9% of each run, Pallas kernels for 0% -> 13%
where the time goes in v1:
time: 1250 us; the launch traced here: 1230 us
  waiting for transfers between devices  447 us (36%)
  Pallas kernels  334 us (27%)
  starting transfers between devices  143 us (11%)
  local copies, waits for them, and re-layouts  99.1 us (8%)
  blocking collectives  83.3 us (7%)
  other arithmetic  63.6 us (5%)
  matrix products  44.5 us (4%)
  between operations  16.6 us (1%)
    all_gather x7, waiting for transfers between devices, gather_weight(): whole = lax.all_gather(share, ('tensor', 'dp'), axis=0, tiled=True)  283 us
    ppermute x42, starting transfers between devices, reduce_grad(): lax.ppermute(passed, 'tensor', [(2 * i + j, 2 * (i + sign) + j) for i in...  122 us
    ppermute x28, waiting for transfers between devices, swap(): return lax.ppermute(value, axis, [(i, i ^ bit) for i in range(size)])  118 us
    pallas_call x4, Pallas kernels, to_heads(): pl.pallas_call(functools.partial(to_heads_kernel, count, tsize, pairs, bl...  106 us
    pallas_call x4, Pallas kernels, to_tokens(): pl.pallas_call(functools.partial(to_tokens_kernel, count, tsize, pairs, b...  99.7 us
    psum x1, blocking collectives, per_device(): lax.psum((jnp.stack([gain_one, gain_two, gain_three]), jnp.stack([shift_o...  55.4 us
    unnamed x220, local copies, waits for them, and re-layouts  47.6 us
    ppermute x42, waiting for transfers between devices, reduce_grad(): lax.ppermute(passed, 'tensor', [(2 * i + j, 2 * (i + sign) + j) for i in...  46.3 us
  transfers between devices with their start and end apart: 77, of which 30 were waited for; matrix products, arithmetic and copies ran while one was open for 9% of the time, Pallas kernels for 13%

profile of v1, /device:TPU:0, one launch (start us, length us, event | category | flops | bytes accessed | tf_op | source)
XLA Modules:
  0.0 1231.3 jit_solution(711176215160467654)
XLA Ops:
  17.6 27.9 %all-gather = bf16[8,1,512]{2,1,0:T(2,128)(2,1)S(1)} all-gather(bf16[1,1,512]{2,1,0:T(2,128)(2,1)S(1)} %reshape.212), channel_id=1, replica_groups=mesh['dp'=4,'tensor'=8] {'tensor'}, dimensions={0}, use_global_device_ids=true | all-gather | bytes 9216 | tf_op jit(solution)/shard_map/all_gather | solution.py:450
  45.7 30.5 %all-gather.15.cloned.1.call-done = bf16[8192,256]{1,0:T(8,128)(2,1)} async-done(((bf16[256,256]{1,0:T(8,128)(2,1)}), bf16[8192,256]{1,0:T(8,128)(2,1)}) %all-gather.15.cloned.1.call-update) | async-done | bytes 4194320 | tf_op jit(solution)/shard_map/all_gather | solution.py:341
  76.2 6.4 shard_map.250
  84.3 72.0 %all-gather.9.cloned.1.call-done = bf16[8192,384]{0,1:T(8,128)(2,1)} async-done(((bf16[256,384]{0,1:T(8,128)(2,1)}), bf16[8192,384]{0,1:T(8,128)(2,1)}) %all-gather.9.cloned.1.call-update) | async-done | bytes 6291472 | tf_op jit(solution)/shard_map/all_gather | solution.py:341
  156.4 8.7 copy.42
  165.0 8.0 shard_map.245
  175.6 38.4 %shard_map.246 = (bf16[3,1024,128]{2,1,0:T(8,128)(2,1)}, bf16[3,1024,128]{2,1,0:T(8,128)(2,1)}, bf16[3,1024,128]{2,1,0:T(8,128)(2,1)}) custom-call(bf16[384,1024]{1,0:T(8,128)(2,1)} %copy-done.34, bf16[384,1024]{1,0:T(8,128)(2,1)} %copy-done.35, bf16[384,1024]{1,0:T(8,128)(2,1)} %copy-done.36), custom_call_target="tpu_custom_call" | custom-call | tf_op jit(solution)/shard_map/pallas_call | solution.py:77
  217.5 8.2 shard_map.247
  226.6 13.9 %shard_map.248 = bf16[384,1024]{1,0:T(8,128)(2,1)} custom-call(bf16[3,1024,128]{2,1,0:T(8,128)(2,1)} %copy-done.22), custom_call_target="tpu_custom_call" | custom-call | tf_op jit(solution)/shard_map/pallas_call | solution.py:134
  244.1 38.3 %all-gather.13.cloned.1.call-done = bf16[8192,128]{1,0:T(8,128)(2,1)} async-done(((bf16[256,128]{1,0:T(8,128)(2,1)}), bf16[8192,128]{1,0:T(8,128)(2,1)}) %all-gather.13.cloned.1.call-update) | async-done | bytes 2097168 | tf_op jit(solution)/shard_map/all_gather | solution.py:341
  288.1 38.3 %shard_map.251 = (bf16[3,1024,128]{2,1,0:T(8,128)(2,1)}, bf16[3,1024,128]{2,1,0:T(8,128)(2,1)}, bf16[3,1024,128]{2,1,0:T(8,128)(2,1)}) custom-call(bf16[384,1024]{1,0:T(8,128)(2,1)} %copy-done.15, bf16[384,1024]{1,0:T(8,128)(2,1)} %copy-done.26, bf16[384,1024]{1,0:T(8,128)(2,1)} %copy-done.27), custom_call_target="tpu_custom_call" | custom-call | tf_op jit(solution)/shard_map/pallas_call | solution.py:77
  329.8 10.2 shard_map.252
  340.9 13.9 %shard_map.253 = bf16[384,1024]{1,0:T(8,128)(2,1)} custom-call(bf16[3,1024,128]{2,1,0:T(8,128)(2,1)} %copy-done.24), custom_call_target="tpu_custom_call" | custom-call | tf_op jit(solution)/shard_map/pallas_call | solution.py:134
  359.3 72.1 %all-gather.19.cloned.1.call-done = bf16[8192,512]{1,0:T(8,128)(2,1)} async-done(((bf16[256,512]{1,0:T(8,128)(2,1)}), bf16[8192,512]{1,0:T(8,128)(2,1)}) %all-gather.19.cloned.1.call-update) | async-done | bytes 8388624 | tf_op jit(solution)/shard_map/all_gather | solution.py:341
  431.4 9.9 shard_map.254
  441.3 69.6 %all-gather.21.cloned.1.call-done = bf16[4096,1024]{1,0:T(8,128)(2,1)} async-done(((bf16[128,1024]{1,0:T(8,128)(2,1)}), bf16[4096,1024]{1,0:T(8,128)(2,1)}) %all-gather.21.cloned.1.call-update) | async-done | bytes 8388624 | tf_op jit(solution)/shard_map/all_gather | solution.py:341
  510.9 9.7 fusion.31
  524.6 9.9 convert_reduce_fusion
  534.5 9.5 shard_map.255
  549.2 14.7 %shard_map.256.do_ref = bf16[3,1024,128]{2,1,0:T(8,128)(2,1)} custom-call(bf16[384,1024]{1,0:T(8,128)(2,1)} %convolution_convert_fusion.4.refs_0_), custom_call_target="tpu_custom_call" | custom-call | tf_op jit(solution)/shard_map/pallas_call | solution.py:77
  568.5 16.9 %shard_map.257 = (bf16[3,1024,128]{2,1,0:T(8,128)(2,1)S(1)}, bf16[3,1024,128]{2,1,0:T(8,128)(2,1)S(1)}, bf16[3,1024,128]{2,1,0:T(8,128)(2,1)S(1)}) custom-call(bf16[3,1024,128]{2,1,0:T(8,128)(2,1)S(1)} %copy-done.44, bf16[3,1024,128]{2,1,0:T(8,128)(2,1)S(1)} %copy-done.46, bf16[3,1024,128]{2,1,0:T(8,128)(2,1)S(1)} %copy-done.48, ...), custom_call_target="tpu_custom_call" | custom-call | flops 4026531840 | bytes 6291456 | tf_op jit(solution)/shard_map/pallas_call | solution.py:232
  588.1 36.2 %shard_map.258 = (bf16[384,1024]{1,0:T(8,128)(2,1)}, bf16[384,1024]{1,0:T(8,128)(2,1)}, bf16[384,1024]{1,0:T(8,128)(2,1)}) custom-call(bf16[3,1024,128]{2,1,0:T(8,128)(2,1)} %copy-done.28, bf16[3,1024,128]{2,1,0:T(8,128)(2,1)} %copy-done.29, bf16[3,1024,128]{2,1,0:T(8,128)(2,1)} %copy-done.30), custom_call_target="tpu_custom_call" | custom-call | tf_op jit(solution)/shard_map/pallas_call | solution.py:134
  636.4 14.3 %shard_map.260.do_ref = bf16[3,1024,128]{2,1,0:T(8,128)(2,1)} custom-call(bf16[384,1024]{1,0:T(8,128)(2,1)} %convolution_convert_fusion.3.refs_0_), custom_call_target="tpu_custom_call" | custom-call | tf_op jit(solution)/shard_map/pallas_call | solution.py:77
  655.3 12.1 shard_map.261
  670.0 35.6 %shard_map.262 = (bf16[384,1024]{1,0:T(8,128)(2,1)}, bf16[384,1024]{1,0:T(8,128)(2,1)}, bf16[384,1024]{1,0:T(8,128)(2,1)}) custom-call(bf16[3,1024,128]{2,1,0:T(8,128)(2,1)} %copy-done.31, bf16[3,1024,128]{2,1,0:T(8,128)(2,1)} %copy-done.32, bf16[3,1024,128]{2,1,0:T(8,128)(2,1)} %copy-done.33), custom_call_target="tpu_custom_call" | custom-call | tf_op jit(solution)/shard_map/pallas_call | solution.py:134
  709.0 8.9 shard_map.263
  718.0 7.5 shard_map.265
  731.7 7.9 shard_map.268
  739.6 11.1 convolution_convert_fusion
  757.2 6.1 shard_map.267
  770.1 6.0 shard_map.264
  790.1 9.7 collective-permute-done.11
  801.9 9.2 collective-permute-done.21
  812.4 9.7 collective-permute-done.41
  856.9 25.5 %collective-permute-start.14 = (bf16[64,1024]{1,0:T(8,128)(2,1)S(1)}, bf16[64,1024]{1,0:T(8,128)(2,1)S(1)}, u32[]{:S(2)}, u32[]{:S(2)}) collective-permute-start(bf16[64,1024]{1,0:T(8,128)(2,1)S(1)} %get-tuple-element.168), channel_id=1, source_target_pairs={{0,2},{1,3},{2,4},{3,5},{4,6},{5,7},{8,10},{9,11},{10,12},{11,13},... | collective-permute-start | bytes 393224 | tf_op jit(solution)/shard_map/ppermute | solution.py:390
  912.6 55.4 %all-reduce = (f32[4096]{0:T(1024)}, f32[1024]{0:T(1024)}, f32[3,1024]{1,0:T(4,128)}, f32[3,1024]{1,0:T(4,128)}) all-reduce(f32[4096]{0:T(1024)} %get-tuple-element.190, f32[1024]{0:T(1024)} %get-tuple-element.140, f32[3,1024]{1,0:T(4,128)S(1)} %get-tuple-element.192, ...), channel_id=1, replica_groups=mesh['dp'=4,'tensor'=8] {'dp','tensor'}, use_global_device_ids=true, to_apply=%region_13.0 | all-reduce | flops 11264 | bytes 90112 | tf_op jit(solution)/shard_map/psum | solution.py:508
  1006.3 8.5 collective-permute-done.1
  1032.2 27.6 %collective-permute-done.51 = bf16[4,512,512]{2,1,0:T(8,128)(2,1)} collective-permute-done((bf16[4,512,512]{2,1,0:T(8,128)(2,1)}, bf16[4,512,512]{2,1,0:T(8,128)(2,1)}, u32[]{:S(2)}, u32[]{:S(2)}) %collective-permute-start.51) | collective-permute-done | bytes 2097184 | tf_op jit(solution)/shard_map/ppermute | solution.py:366
  1066.5 37.6 %collective-permute-done.61 = bf16[4,256,1024]{2,1,0:T(8,128)(2,1)S(1)} collective-permute-done((bf16[4,256,1024]{2,1,0:T(8,128)(2,1)}, bf16[4,256,1024]{2,1,0:T(8,128)(2,1)S(1)}, u32[]{:S(2)}, u32[]{:S(2)}) %collective-permute-start.61) | collective-permute-done | bytes 2097184 | tf_op jit(solution)/shard_map/ppermute | solution.py:366
  1117.4 5.1 collective-permute-done.62
  1127.8 5.9 collective-permute-done.53
  1139.3 8.5 collective-permute-done.3
  1151.3 6.1 collective-permute-done.63
  1157.5 5.2 collective-permute-start.4
  1170.6 7.2 collective-permute-start.54
  1183.3 8.7 collective-permute-start.64
  1203.7 4.7 collective-permute-done.58
  1212.2 5.3 collective-permute-done.68
  (502 shorter events, 301.8 us)
Async XLA Ops:
  7.2 69.0 %all-gather.15.cloned.1.call-start = ((), (), s32[]{:S(2)}) async-start(), calls=%async_computation.3 | async-start | bytes 4325376 | tf_op jit(solution)/shard_map/all_gather | solution.py:341
  9.2 147.1 %all-gather.9.cloned.1.call-start = ((), (), s32[]{:S(2)}) async-start(), calls=%async_computation | async-start | bytes 6488064 | tf_op jit(solution)/shard_map/all_gather | solution.py:341
  10.3 230.2 %all-gather.11.cloned.1.call-start = ((), (), s32[]{:S(2)}) async-start(), calls=%async_computation.1 | async-start | bytes 2162688 | tf_op jit(solution)/shard_map/all_gather | solution.py:341
  11.9 270.6 %all-gather.13.cloned.1.call-start = ((), (), s32[]{:S(2)}) async-start(), calls=%async_computation.2 | async-start | bytes 2162688 | tf_op jit(solution)/shard_map/all_gather | solution.py:341
  13.4 341.4 %all-gather.17.cloned.1.call-start = ((), (), s32[]{:S(2)}) async-start(), calls=%async_computation.4 | async-start | bytes 2162688 | tf_op jit(solution)/shard_map/all_gather | solution.py:341
  15.0 416.4 %all-gather.19.cloned.1.call-start = ((), (), s32[]{:S(2)}) async-start(), calls=%async_computation.5 | async-start | bytes 8650752 | tf_op jit(solution)/shard_map/all_gather | solution.py:341
  15.8 495.1 %all-gather.21.cloned.1.call-start = ((), (), s32[]{:S(2)}) async-start(), calls=%async_computation.6 | async-start | bytes 8650752 | tf_op jit(solution)/shard_map/all_gather | solution.py:341
  754.0 219.7 %collective-permute-start = (bf16[8,512,384]{2,1,0:T(8,128)(2,1)}, bf16[8,512,384]{2,1,0:T(8,128)(2,1)}, u32[]{:S(2)}, u32[]{:S(2)}) collective-permute-start(bf16[8,512,384]{2,1,0:T(8,128)(2,1)} %dynamic-slice_bitcast_fusion.2), channel_id=1, source_target_pairs={{0,8},{8,0},{16,24},{24,16},{1,9},{9,1},{17,25},{25,17},{2,10},{10... | collective-permute-start | bytes 9437192 | tf_op jit(solution)/shard_map/ppermute | solution.py:366
  755.4 27.7 %collective-permute-start.10 = (bf16[8,64,1024]{2,1,0:T(8,128)(2,1)}, bf16[8,64,1024]{2,1,0:T(8,128)(2,1)}, u32[]{:S(2)}, u32[]{:S(2)}) collective-permute-start(bf16[8,64,1024]{2,1,0:T(8,128)(2,1)} %dynamic-slice_bitcast_fusion.10), channel_id=1, source_target_pairs={{0,8},{8,0},{16,24},{24,16},{1,9},{9,1},{17,25},{25,17},{2,10},{10... | collective-permute-start | bytes 3145736 | tf_op jit(solution)/shard_map/ppermute | solution.py:366
  756.7 28.0 %collective-permute-start.20 = (bf16[8,512,128]{2,1,0:T(8,128)(2,1)}, bf16[8,512,128]{2,1,0:T(8,128)(2,1)}, u32[]{:S(2)}, u32[]{:S(2)}) collective-permute-start(bf16[8,512,128]{2,1,0:T(8,128)(2,1)} %dynamic-slice_bitcast_fusion.9), channel_id=1, source_target_pairs={{0,8},{8,0},{16,24},{24,16},{1,9},{9,1},{17,25},{25,17},{2,10},{10... | collective-permute-start | bytes 3145736 | tf_op jit(solution)/shard_map/ppermute | solution.py:366
  766.6 115.8 %collective-permute-start.30 = (bf16[8,512,256]{2,1,0:T(8,128)(2,1)}, bf16[8,512,256]{2,1,0:T(8,128)(2,1)}, u32[]{:S(2)}, u32[]{:S(2)}) collective-permute-start(bf16[8,512,256]{2,1,0:T(8,128)(2,1)} %dynamic-slice_bitcast_fusion.5), channel_id=1, source_target_pairs={{0,8},{8,0},{16,24},{24,16},{1,9},{9,1},{17,25},{25,17},{2,10},{10... | collective-permute-start | bytes 6291464 | tf_op jit(solution)/shard_map/ppermute | solution.py:366
  769.6 18.8 %collective-permute-start.40 = (bf16[8,64,1024]{2,1,0:T(8,128)(2,1)}, bf16[8,64,1024]{2,1,0:T(8,128)(2,1)}, u32[]{:S(2)}, u32[]{:S(2)}) collective-permute-start(bf16[8,64,1024]{2,1,0:T(8,128)(2,1)} %dynamic-slice_bitcast_fusion.7), channel_id=1, source_target_pairs={{0,8},{8,0},{16,24},{24,16},{1,9},{9,1},{17,25},{25,17},{2,10},{10... | collective-permute-start | bytes 3145736 | tf_op jit(solution)/shard_map/ppermute | solution.py:366
  783.2 197.7 %collective-permute-start.50 = (bf16[8,512,512]{2,1,0:T(8,128)(2,1)}, bf16[8,512,512]{2,1,0:T(8,128)(2,1)}, u32[]{:S(2)}, u32[]{:S(2)}) collective-permute-start(bf16[8,512,512]{2,1,0:T(8,128)(2,1)} %dynamic-slice_bitcast_fusion.1), channel_id=1, source_target_pairs={{0,8},{8,0},{16,24},{24,16},{1,9},{9,1},{17,25},{25,17},{2,10},{10... | collective-permute-start | bytes 12582920 | tf_op jit(solution)/shard_map/ppermute | solution.py:366
  784.6 15.2 %collective-permute-start.11 = (bf16[4,64,1024]{2,1,0:T(8,128)(2,1)S(1)}, bf16[4,64,1024]{2,1,0:T(8,128)(2,1)S(1)}, u32[]{:S(2)}, u32[]{:S(2)}) collective-permute-start(bf16[4,64,1024]{2,1,0:T(8,128)(2,1)S(1)} %dynamic-slice_bitcast_fusion.17), channel_id=1, source_target_pairs={{0,1},{1,0},{2,3},{3,2},{4,5},{5,4},{6,7},{7,6},{8,9},{9,8},{10,11... | collective-permute-start | bytes 1572872 | tf_op jit(solution)/shard_map/ppermute | solution.py:366
  788.5 22.6 %collective-permute-start.21 = (bf16[4,512,128]{2,1,0:T(8,128)(2,1)S(1)}, bf16[4,512,128]{2,1,0:T(8,128)(2,1)S(1)}, u32[]{:S(2)}, u32[]{:S(2)}) collective-permute-start(bf16[4,512,128]{2,1,0:T(8,128)(2,1)S(1)} %dynamic-slice_bitcast_fusion.16), channel_id=1, source_target_pairs={{0,1},{1,0},{2,3},{3,2},{4,5},{5,4},{6,7},{7,6},{8,9},{9,8},{10,11... | collective-permute-start | bytes 1572872 | tf_op jit(solution)/shard_map/ppermute | solution.py:366
  799.8 22.3 %collective-permute-start.41 = (bf16[4,64,1024]{2,1,0:T(8,128)(2,1)S(1)}, bf16[4,64,1024]{2,1,0:T(8,128)(2,1)S(1)}, u32[]{:S(2)}, u32[]{:S(2)}) collective-permute-start(bf16[4,64,1024]{2,1,0:T(8,128)(2,1)S(1)} %dynamic-slice_bitcast_fusion.15), channel_id=1, source_target_pairs={{0,1},{1,0},{2,3},{3,2},{4,5},{5,4},{6,7},{7,6},{8,9},{9,8},{10,11... | collective-permute-start | bytes 1572872 | tf_op jit(solution)/shard_map/ppermute | solution.py:366
  822.1 16.5 %collective-permute-start.15 = (bf16[64,1024]{1,0:T(8,128)(2,1)S(1)}, bf16[64,1024]{1,0:T(8,128)(2,1)S(1)}, u32[]{:S(2)}, u32[]{:S(2)}) collective-permute-start(bf16[64,1024]{1,0:T(8,128)(2,1)S(1)} %get-tuple-element.171), channel_id=1, source_target_pairs={{6,4},{7,5},{14,12},{15,13},{22,20},{23,21},{30,28},{31,29}} | collective-permute-start | bytes 393224 | tf_op jit(solution)/shard_map/ppermute | solution.py:390
  852.3 135.1 %collective-permute-start.60 = (bf16[8,256,1024]{2,1,0:T(8,128)(2,1)}, bf16[8,256,1024]{2,1,0:T(8,128)(2,1)}, u32[]{:S(2)}, u32[]{:S(2)}) collective-permute-start(bf16[8,256,1024]{2,1,0:T(8,128)(2,1)} %dynamic-slice_bitcast_fusion), channel_id=1, source_target_pairs={{0,8},{8,0},{16,24},{24,16},{1,9},{9,1},{17,25},{25,17},{2,10},{10... | collective-permute-start | bytes 12582920 | tf_op jit(solution)/shard_map/ppermute | solution.py:366
  856.9 28.6 %collective-permute-start.14 = (bf16[64,1024]{1,0:T(8,128)(2,1)S(1)}, bf16[64,1024]{1,0:T(8,128)(2,1)S(1)}, u32[]{:S(2)}, u32[]{:S(2)}) collective-permute-start(bf16[64,1024]{1,0:T(8,128)(2,1)S(1)} %get-tuple-element.168), channel_id=1, source_target_pairs={{0,2},{1,3},{2,4},{3,5},{4,6},{5,7},{8,10},{9,11},{10,12},{11,13},... | collective-permute-start | bytes 393224 | tf_op jit(solution)/shard_map/ppermute | solution.py:390
  908.8 62.7 %collective-permute-start.19 = (bf16[64,1024]{1,0:T(8,128)(2,1)S(1)}, bf16[64,1024]{1,0:T(8,128)(2,1)}, u32[]{:S(2)}, u32[]{:S(2)}) collective-permute-start(bf16[64,1024]{1,0:T(8,128)(2,1)S(1)} %add.552), channel_id=1, source_target_pairs={{0,8},{8,0},{16,24},{24,16},{1,9},{9,1},{17,25},{25,17},{2,10},{10... | collective-permute-start | bytes 393224 | tf_op jit(solution)/shard_map/ppermute | solution.py:366
  910.3 69.3 %collective-permute-start.31 = (bf16[4,512,256]{2,1,0:T(8,128)(2,1)S(1)}, bf16[4,512,256]{2,1,0:T(8,128)(2,1)}, u32[]{:S(2)}, u32[]{:S(2)}) collective-permute-start(bf16[4,512,256]{2,1,0:T(8,128)(2,1)S(1)} %dynamic-slice_bitcast_fusion.8), channel_id=1, source_target_pairs={{0,1},{1,0},{2,3},{3,2},{4,5},{5,4},{6,7},{7,6},{8,9},{9,8},{10,11... | collective-permute-start | bytes 3145736 | tf_op jit(solution)/shard_map/ppermute | solution.py:366
  973.2 24.4 %collective-permute-start.49 = (bf16[64,1024]{1,0:T(8,128)(2,1)S(1)}, bf16[64,1024]{1,0:T(8,128)(2,1)}, u32[]{:S(2)}, u32[]{:S(2)}) collective-permute-start(bf16[64,1024]{1,0:T(8,128)(2,1)S(1)} %add.579), channel_id=1, source_target_pairs={{0,8},{8,0},{16,24},{24,16},{1,9},{9,1},{17,25},{25,17},{2,10},{10... | collective-permute-start | bytes 393224 | tf_op jit(solution)/shard_map/ppermute | solution.py:366
  977.3 37.5 %collective-permute-start.1 = (bf16[4,512,384]{2,1,0:T(8,128)(2,1)S(1)}, bf16[4,512,384]{2,1,0:T(8,128)(2,1)S(1)}, u32[]{:S(2)}, u32[]{:S(2)}) collective-permute-start(bf16[4,512,384]{2,1,0:T(8,128)(2,1)S(1)} %dynamic-slice_bitcast_fusion.6), channel_id=1, source_target_pairs={{0,1},{1,0},{2,3},{3,2},{4,5},{5,4},{6,7},{7,6},{8,9},{9,8},{10,11... | collective-permute-start | bytes 4718600 | tf_op jit(solution)/shard_map/ppermute | solution.py:366
  985.3 74.5 %collective-permute-start.51 = (bf16[4,512,512]{2,1,0:T(8,128)(2,1)}, bf16[4,512,512]{2,1,0:T(8,128)(2,1)}, u32[]{:S(2)}, u32[]{:S(2)}) collective-permute-start(bf16[4,512,512]{2,1,0:T(8,128)(2,1)} %dynamic-slice_bitcast_fusion.4), channel_id=1, source_target_pairs={{0,1},{1,0},{2,3},{3,2},{4,5},{5,4},{6,7},{7,6},{8,9},{9,8},{10,11... | collective-permute-start | bytes 6291464 | tf_op jit(solution)/shard_map/ppermute | solution.py:366
  994.0 110.0 %collective-permute-start.61 = (bf16[4,256,1024]{2,1,0:T(8,128)(2,1)}, bf16[4,256,1024]{2,1,0:T(8,128)(2,1)S(1)}, u32[]{:S(2)}, u32[]{:S(2)}) collective-permute-start(bf16[4,256,1024]{2,1,0:T(8,128)(2,1)} %dynamic-slice_bitcast_fusion.3), channel_id=1, source_target_pairs={{0,1},{1,0},{2,3},{3,2},{4,5},{5,4},{6,7},{7,6},{8,9},{9,8},{10,11... | collective-permute-start | bytes 6291464 | tf_op jit(solution)/shard_map/ppermute | solution.py:366
  1004.7 159.1 %collective-permute-start.36 = (bf16[512,256]{1,0:T(8,128)(2,1)}, bf16[512,256]{1,0:T(8,128)(2,1)}, u32[]{:S(2)}, u32[]{:S(2)}) collective-permute-start(bf16[512,256]{1,0:T(8,128)(2,1)} %get-tuple-element.153), channel_id=1, source_target_pairs={{4,2},{5,3},{6,4},{7,5},{12,10},{13,11},{14,12},{15,13},{20,18},{2... | collective-permute-start | bytes 786440 | tf_op jit(solution)/shard_map/ppermute | solution.py:390
  1018.4 46.3 %collective-permute-start.5 = (bf16[512,384]{0,1:T(8,128)(2,1)}, bf16[512,384]{0,1:T(8,128)(2,1)}, u32[]{:S(2)}, u32[]{:S(2)}) collective-permute-start(bf16[512,384]{0,1:T(8,128)(2,1)} %bitcast.262), channel_id=1, source_target_pairs={{6,4},{7,5},{14,12},{15,13},{22,20},{23,21},{30,28},{31,29}} | collective-permute-start | bytes 1179656 | tf_op jit(solution)/shard_map/ppermute | solution.py:390
  1025.6 84.6 %collective-permute-start.2 = (bf16[512,384]{0,1:T(8,128)(2,1)}, bf16[512,384]{0,1:T(8,128)(2,1)}, u32[]{:S(2)}, u32[]{:S(2)}) collective-permute-start(bf16[512,384]{0,1:T(8,128)(2,1)} %bitcast.261), channel_id=1, source_target_pairs={{0,2},{1,3},{8,10},{9,11},{16,18},{17,19},{24,26},{25,27}} | collective-permute-start | bytes 1179656 | tf_op jit(solution)/shard_map/ppermute | solution.py:390
  1062.5 45.5 %collective-permute-start.52 = (bf16[512,512]{1,0:T(8,128)(2,1)S(1)}, bf16[512,512]{1,0:T(8,128)(2,1)S(1)}, u32[]{:S(2)}, u32[]{:S(2)}) collective-permute-start(bf16[512,512]{1,0:T(8,128)(2,1)S(1)} %get-tuple-element.137), channel_id=1, source_target_pairs={{0,2},{1,3},{8,10},{9,11},{16,18},{17,19},{24,26},{25,27}} | collective-permute-start | bytes 1572872 | tf_op jit(solution)/shard_map/ppermute | solution.py:390
  1065.8 46.9 %collective-permute-start.6 = (bf16[512,384]{0,1:T(8,128)(2,1)S(1)}, bf16[512,384]{0,1:T(8,128)(2,1)S(1)}, u32[]{:S(2)}, u32[]{:S(2)}) collective-permute-start(bf16[512,384]{0,1:T(8,128)(2,1)S(1)} %bitcast_add_fusion.24), channel_id=1, source_target_pairs={{4,2},{5,3},{6,4},{7,5},{12,10},{13,11},{14,12},{15,13},{20,18},{2... | collective-permute-start | bytes 1179656 | tf_op jit(solution)/shard_map/ppermute | solution.py:390
  1105.4 21.6 %collective-permute-start.55 = (bf16[512,512]{1,0:T(8,128)(2,1)S(1)}, bf16[512,512]{1,0:T(8,128)(2,1)S(1)}, u32[]{:S(2)}, u32[]{:S(2)}) collective-permute-start(bf16[512,512]{1,0:T(8,128)(2,1)S(1)} %get-tuple-element.138), channel_id=1, source_target_pairs={{6,4},{7,5},{14,12},{15,13},{22,20},{23,21},{30,28},{31,29}} | collective-permute-start | bytes 1572872 | tf_op jit(solution)/shard_map/ppermute | solution.py:390
  1108.0 14.5 %collective-permute-start.62 = (bf16[256,1024]{1,0:T(8,128)(2,1)S(1)}, bf16[256,1024]{1,0:T(8,128)(2,1)S(1)}, u32[]{:S(2)}, u32[]{:S(2)}) collective-permute-start(bf16[256,1024]{1,0:T(8,128)(2,1)S(1)} %get-tuple-element.133), channel_id=1, source_target_pairs={{0,2},{1,3},{8,10},{9,11},{16,18},{17,19},{24,26},{25,27}} | collective-permute-start | bytes 1572872 | tf_op jit(solution)/shard_map/ppermute | solution.py:390
  1110.3 23.5 %collective-permute-start.53 = (bf16[512,512]{1,0:T(8,128)(2,1)S(1)}, bf16[512,512]{1,0:T(8,128)(2,1)S(1)}, u32[]{:S(2)}, u32[]{:S(2)}) collective-permute-start(bf16[512,512]{1,0:T(8,128)(2,1)S(1)} %bitcast_add_fusion.18), channel_id=1, source_target_pairs={{0,2},{1,3},{2,4},{3,5},{8,10},{9,11},{10,12},{11,13},{16,18},{17,... | collective-permute-start | bytes 1572872 | tf_op jit(solution)/shard_map/ppermute | solution.py:390
  1112.7 70.6 %collective-permute-start.34 = (bf16[512,256]{1,0:T(8,128)(2,1)}, bf16[512,256]{1,0:T(8,128)(2,1)}, u32[]{:S(2)}, u32[]{:S(2)}) collective-permute-start(bf16[512,256]{1,0:T(8,128)(2,1)} %get-tuple-element.152), channel_id=1, source_target_pairs={{0,2},{1,3},{2,4},{3,5},{4,6},{5,7},{8,10},{9,11},{10,12},{11,13},... | collective-permute-start | bytes 786440 | tf_op jit(solution)/shard_map/ppermute | solution.py:390
  1122.5 25.3 %collective-permute-start.3 = (bf16[512,384]{0,1:T(8,128)(2,1)S(1)}, bf16[512,384]{0,1:T(8,128)(2,1)S(1)}, u32[]{:S(2)}, u32[]{:S(2)}) collective-permute-start(bf16[512,384]{0,1:T(8,128)(2,1)S(1)} %bitcast_add_fusion.26), channel_id=1, source_target_pairs={{0,2},{1,3},{2,4},{3,5},{8,10},{9,11},{10,12},{11,13},{16,18},{17,... | collective-permute-start | bytes 1179656 | tf_op jit(solution)/shard_map/ppermute | solution.py:390
  1127.0 23.0 %collective-permute-start.65 = (bf16[256,1024]{1,0:T(8,128)(2,1)S(1)}, bf16[256,1024]{1,0:T(8,128)(2,1)S(1)}, u32[]{:S(2)}, u32[]{:S(2)}) collective-permute-start(bf16[256,1024]{1,0:T(8,128)(2,1)S(1)} %get-tuple-element.134), channel_id=1, source_target_pairs={{6,4},{7,5},{14,12},{15,13},{22,20},{23,21},{30,28},{31,29}} | collective-permute-start | bytes 1572872 | tf_op jit(solution)/shard_map/ppermute | solution.py:390
  1133.8 23.7 %collective-permute-start.63 = (bf16[256,1024]{1,0:T(8,128)(2,1)S(1)}, bf16[256,1024]{1,0:T(8,128)(2,1)S(1)}, u32[]{:S(2)}, u32[]{:S(2)}) collective-permute-start(bf16[256,1024]{1,0:T(8,128)(2,1)S(1)} %bitcast_add_fusion.13), channel_id=1, source_target_pairs={{0,2},{1,3},{2,4},{3,5},{8,10},{9,11},{10,12},{11,13},{16,18},{17,... | collective-permute-start | bytes 1572872 | tf_op jit(solution)/shard_map/ppermute | solution.py:390
  1147.8 20.1 %collective-permute-start.56 = (bf16[512,512]{1,0:T(8,128)(2,1)}, bf16[512,512]{1,0:T(8,128)(2,1)}, u32[]{:S(2)}, u32[]{:S(2)}) collective-permute-start(bf16[512,512]{1,0:T(8,128)(2,1)} %get-tuple-element.136), channel_id=1, source_target_pairs={{4,2},{5,3},{6,4},{7,5},{12,10},{13,11},{14,12},{15,13},{20,18},{2... | collective-permute-start | bytes 1572872 | tf_op jit(solution)/shard_map/ppermute | solution.py:390
  1150.1 20.5 %collective-permute-start.7 = (bf16[512,384]{0,1:T(8,128)(2,1)}, bf16[512,384]{0,1:T(8,128)(2,1)}, u32[]{:S(2)}, u32[]{:S(2)}) collective-permute-start(bf16[512,384]{0,1:T(8,128)(2,1)} %bitcast_add_fusion.25), channel_id=1, source_target_pairs={{2,0},{3,1},{4,2},{5,3},{6,4},{7,5},{10,8},{11,9},{12,10},{13,11},... | collective-permute-start | bytes 1179656 | tf_op jit(solution)/shard_map/ppermute | solution.py:390
  1157.5 20.3 %collective-permute-start.4 = (bf16[512,384]{0,1:T(8,128)(2,1)}, bf16[512,384]{0,1:T(8,128)(2,1)}, u32[]{:S(2)}, u32[]{:S(2)}) collective-permute-start(bf16[512,384]{0,1:T(8,128)(2,1)} %bitcast_add_fusion.27), channel_id=1, source_target_pairs={{0,2},{1,3},{2,4},{3,5},{4,6},{5,7},{8,10},{9,11},{10,12},{11,13},... | collective-permute-start | bytes 1179656 | tf_op jit(solution)/shard_map/ppermute | solution.py:390
  1163.8 16.6 %collective-permute-start.66 = (bf16[256,1024]{1,0:T(8,128)(2,1)}, bf16[256,1024]{1,0:T(8,128)(2,1)}, u32[]{:S(2)}, u32[]{:S(2)}) collective-permute-start(bf16[256,1024]{1,0:T(8,128)(2,1)} %get-tuple-element.132), channel_id=1, source_target_pairs={{4,2},{5,3},{6,4},{7,5},{12,10},{13,11},{14,12},{15,13},{20,18},{2... | collective-permute-start | bytes 1572872 | tf_op jit(solution)/shard_map/ppermute | solution.py:390
  1167.9 24.1 %collective-permute-start.37 = (bf16[512,256]{1,0:T(8,128)(2,1)}, bf16[512,256]{1,0:T(8,128)(2,1)S(1)}, u32[]{:S(2)}, u32[]{:S(2)}) collective-permute-start(bf16[512,256]{1,0:T(8,128)(2,1)} %bitcast_add_fusion.30), channel_id=1, source_target_pairs={{2,0},{3,1},{4,2},{5,3},{6,4},{7,5},{10,8},{11,9},{12,10},{13,11},... | collective-permute-start | bytes 786440 | tf_op jit(solution)/shard_map/ppermute | solution.py:390
  1170.6 23.7 %collective-permute-start.54 = (bf16[512,512]{1,0:T(8,128)(2,1)S(1)}, bf16[512,512]{1,0:T(8,128)(2,1)S(1)}, u32[]{:S(2)}, u32[]{:S(2)}) collective-permute-start(bf16[512,512]{1,0:T(8,128)(2,1)S(1)} %copy-done.86), channel_id=1, source_target_pairs={{0,2},{1,3},{2,4},{3,5},{4,6},{5,7},{8,10},{9,11},{10,12},{11,13},... | collective-permute-start | bytes 1572872 | tf_op jit(solution)/shard_map/ppermute | solution.py:390
  1177.8 16.8 %collective-permute-start.57 = (bf16[512,512]{1,0:T(8,128)(2,1)S(1)}, bf16[512,512]{1,0:T(8,128)(2,1)S(1)}, u32[]{:S(2)}, u32[]{:S(2)}) collective-permute-start(bf16[512,512]{1,0:T(8,128)(2,1)S(1)} %bitcast_add_fusion.17), channel_id=1, source_target_pairs={{2,0},{3,1},{4,2},{5,3},{6,4},{7,5},{10,8},{11,9},{12,10},{13,11},... | collective-permute-start | bytes 1572872 | tf_op jit(solution)/shard_map/ppermute | solution.py:390
  1180.3 20.5 %collective-permute-start.8 = (bf16[512,384]{0,1:T(8,128)(2,1)S(1)}, bf16[512,384]{0,1:T(8,128)(2,1)S(1)}, u32[]{:S(2)}, u32[]{:S(2)}) collective-permute-start(bf16[512,384]{0,1:T(8,128)(2,1)S(1)} %fusion.15), channel_id=1, source_target_pairs={{0,16},{8,24},{16,0},{24,8},{1,17},{9,25},{17,1},{25,9},{2,18},{10... | collective-permute-start | bytes 1179656 | tf_op jit(solution)/shard_map/ppermute | solution.py:366
  1183.3 18.2 %collective-permute-start.64 = (bf16[256,1024]{1,0:T(8,128)(2,1)S(1)}, bf16[256,1024]{1,0:T(8,128)(2,1)S(1)}, u32[]{:S(2)}, u32[]{:S(2)}) collective-permute-start(bf16[256,1024]{1,0:T(8,128)(2,1)S(1)} %copy-done.85), channel_id=1, source_target_pairs={{0,2},{1,3},{2,4},{3,5},{4,6},{5,7},{8,10},{9,11},{10,12},{11,13},... | collective-permute-start | bytes 1572872 | tf_op jit(solution)/shard_map/ppermute | solution.py:390
  1195.8 12.6 %collective-permute-start.58 = (bf16[512,512]{1,0:T(8,128)(2,1)S(1)}, bf16[512,512]{1,0:T(8,128)(2,1)}, u32[]{:S(2)}, u32[]{:S(2)}) collective-permute-start(bf16[512,512]{1,0:T(8,128)(2,1)S(1)} %fusion.14), channel_id=1, source_target_pairs={{0,16},{8,24},{16,0},{24,8},{1,17},{9,25},{17,1},{25,9},{2,18},{10... | collective-permute-start | bytes 1572872 | tf_op jit(solution)/shard_map/ppermute | solution.py:366
  1203.1 14.4 %collective-permute-start.68 = (bf16[256,1024]{1,0:T(8,128)(2,1)S(1)}, bf16[256,1024]{1,0:T(8,128)(2,1)S(1)}, u32[]{:S(2)}, u32[]{:S(2)}) collective-permute-start(bf16[256,1024]{1,0:T(8,128)(2,1)S(1)} %fusion.13), channel_id=1, source_target_pairs={{0,16},{8,24},{16,0},{24,8},{1,17},{9,25},{17,1},{25,9},{2,18},{10... | collective-permute-start | bytes 1572872 | tf_op jit(solution)/shard_map/ppermute | solution.py:366
  (137 other events, 1432.3 us)
Sparse Core Ops, SparseCore 0:
  11.5 64.6 all-gather.14
  79.6 76.6 all-gather.8
  159.8 64.0 all-gather.10
  227.2 55.2 all-gather.12
  285.2 66.6 all-gather.16
  355.2 76.1 all-gather.18
  434.8 76.0 all-gather.20

commit v2 on v1

--- a/solution.py
+++ b/solution.py
@@ -301,7 +301,11 @@
     )(*ys, weight)
 
 
-def grad_kernel(count, x_ref, *refs):
+def by_side(grad, t):
+    return jnp.swapaxes(grad.reshape(t // 2, 2, *grad.shape[1:]), 0, 1)
+
+
+def cols_grad_kernel(count, x_ref, *refs):
     ys, o_ref, xt_ref = refs[:count], refs[count], refs[count + 1]
 
     @pl.when(pl.program_id(0) == 0)
@@ -309,29 +313,85 @@
         xt_ref[...] = jnp.transpose(x_ref[...])
 
     y = jnp.concatenate([y_ref[...] for y_ref in ys], 1) if count > 1 else ys[0][...]
-    o_ref[0] = dot(xt_ref[...], y, NN).astype(o_ref.dtype)
+    out = dot(xt_ref[...], y, NN).astype(o_ref.dtype)
+    d = out.shape[0]
+    for j in range(out.shape[1] // LANES):
+        o_ref[0, 0, j * d : j * d + d, :] = out[:, j * LANES : j * LANES + LANES]
 
 
 def cols_grad(x, ys, t):
     count = len(ys)
     n, d = x.shape
-    width = max(ys[0].shape[1] // t, LANES)
-    blocks = ys[0].shape[1] // width
+    blocks = min(t, ys[0].shape[1] // LANES)
+    width = ys[0].shape[1] // blocks
     c = width * count
+    whole = blocks == t
     out = pl.pallas_call(
-        functools.partial(grad_kernel, count),
+        functools.partial(cols_grad_kernel, count),
         grid=(blocks,),
-        out_shape=jax.ShapeDtypeStruct((blocks, d, c), jnp.bfloat16),
+        out_shape=jax.ShapeDtypeStruct(
+            (2, t // 2, c // LANES * d, LANES) if whole else (blocks, 1, c // LANES * d, LANES), jnp.bfloat16
+        ),
         in_specs=[pl.BlockSpec((n, d), lambda i: (0, 0))]
         + [pl.BlockSpec((n, width), lambda i: (0, i))] * count,
-        out_specs=pl.BlockSpec((1, d, c), lambda i: (i, 0, 0)),
+        out_specs=pl.BlockSpec(
+            (1, 1, c // LANES * d, LANES), (lambda i: (i % 2, i // 2, 0, 0)) if whole else (lambda i: (i, 0, 0, 0))
+        ),
         scratch_shapes=[pltpu.VMEM((d, n), jnp.bfloat16)],
         compiler_params=pltpu.CompilerParams(vmem_limit_bytes=48 << 20),
         cost_estimate=pl.CostEstimate(
-            flops=2 * n * d * t * c, bytes_accessed=2 * (t * d * c + n * d + n * t * c), transcendentals=0
+            flops=2 * n * d * blocks * c, bytes_accessed=2 * (blocks * d * c + n * d + n * blocks * c), transcendentals=0
         ),
     )(x, *ys)
-    return narrow(out, count, t)
+    if whole:
+        return out
+    m = t // blocks
+    parts = out.reshape(blocks, count, d, m, LANES // m).transpose(0, 3, 1, 2, 4)
+    return by_side(parts.reshape(t, count * d // m, LANES), t)
+
+
+def cols_result(total, count, d, width):
+    total = total.astype(jnp.float32)
+    if width < LANES:
+        return total.reshape(count, d, width).transpose(1, 0, 2).reshape(d, count * width)
+    return total.reshape(-1, d, LANES).transpose(1, 0, 2).reshape(d, count * width)
+
+
+def rows_grad_kernel(x_ref, y_ref, o_ref):
+    out = dot(jnp.transpose(x_ref[...]), y_ref[...], NN).astype(o_ref.dtype)
+    r = out.shape[0]
+    for j in range(out.shape[1] // LANES):
+        o_ref[0, 0, j * r : j * r + r, :] = out[:, j * LANES : j * LANES + LANES]
+
+
+def rows_grad(x, y, t):
+    n, d = y.shape
+    blocks = min(t, x.shape[1] // LANES)
+    r = x.shape[1] // blocks
+    whole = blocks == t
+    size = d // LANES * r
+    out = pl.pallas_call(
+        rows_grad_kernel,
+        grid=(blocks,),
+        out_shape=jax.ShapeDtypeStruct((2, t // 2, size, LANES) if whole else (blocks, 1, size, LANES), jnp.bfloat16),
+        in_specs=[pl.BlockSpec((n, r), lambda i: (0, i)), pl.BlockSpec((n, d), lambda i: (0, 0))],
+        out_specs=pl.BlockSpec(
+            (1, 1, size, LANES), (lambda i: (i % 2, i // 2, 0, 0)) if whole else (lambda i: (i, 0, 0, 0))
+        ),
+        compiler_params=pltpu.CompilerParams(vmem_limit_bytes=48 << 20),
+        cost_estimate=pl.CostEstimate(
+            flops=2 * n * d * blocks * r, bytes_accessed=2 * (blocks * d * r + n * d + n * blocks * r), transcendentals=0
+        ),
+    )(x, y)
+    if whole:
+        return out
+    m = t // blocks
+    parts = out.reshape(blocks, d // LANES, m, r // m, LANES).transpose(0, 2, 1, 3, 4)
+    return by_side(parts.reshape(t, size // m, LANES), t)
+
+
+def rows_result(total, r, d):
+    return total.astype(jnp.float32).reshape(d // LANES, r, LANES).transpose(1, 0, 2).reshape(r, d)
 
 
 def gather_weight(weight):
@@ -352,53 +412,323 @@
     return parts.reshape(t // m, r, count * LANES)
 
 
-def narrow(grad, count, t):
-    blocks, r, c = grad.shape
-    if blocks == t:
-        return grad
-    m = t // blocks
-    parts = grad.reshape(blocks, r, count, m, c // count // m).transpose(0, 3, 1, 2, 4)
-    return parts.reshape(t, r, c // m)
-
-
 def swap(value, axis, bit):
     size = lax.axis_size(axis)
     return lax.ppermute(value, axis, [(i, i ^ bit) for i in range(size)])
 
 
-def pick(value, index, axis):
-    return lax.dynamic_index_in_dim(value, index, axis, keepdims=False)
-
-
-def reduce_grad(grad):
-    dp, t = lax.axis_size("dp"), lax.axis_size("tensor")
-    own_dp, own_t = lax.axis_index("dp"), lax.axis_index("tensor")
-    _, r, c = grad.shape
-    core, side, line, depth = own_dp % 2, own_t % 2, own_t // 2, t // 2
-    halves = grad.reshape(t, 2, r // 2, c)
-    total = pick(halves, core, 1) + swap(pick(halves, 1 - core, 1), "dp", 1)
-    pairs = total.reshape(depth, 2, r // 2, c)
-    total = pick(pairs, side, 1) + swap(pick(pairs, 1 - side, 1), "tensor", 1)
-    result = pick(total, line, 0)
-    for sign in (1, -1):
-        passed = None
-        for step in range(depth - 1):
-            far = line + sign * (depth - 1 - step)
-            part = pick(total, jnp.clip(far, 0, depth - 1), 0)
-            passed = part if passed is None else part + passed
-            lines = range(step + 1) if sign == 1 else range(depth - 1 - step, depth)
-            passed = lax.ppermute(
-                passed, "tensor", [(2 * i + j, 2 * (i + sign) + j) for i in lines for j in range(2)]
-            )
-        result = result + passed
-    bit = 2
-    while bit < dp:
-        result = result + swap(result, "dp", bit)
+def settle(total):
+    bit = 4
+    while bit < lax.axis_size("dp"):
+        total = total + swap(total, "dp", bit)
         bit *= 2
-    other = swap(result, "dp", 1)
-    first = jnp.where(core == 0, result, other)
-    second = jnp.where(core == 0, other, result)
-    return jnp.concatenate([first, second], 0).astype(jnp.float32)
+    return total
+
+
+gather_ahead = 1
+def x_rows(half):
+    return min(max(int(half * 0.36 / 16 + 0.5), 0) * 16, half // 32 * 16)
+
+def piece_list(shapes, size):
+    pieces = []
+    for w, (r, c) in enumerate(shapes):
+        rows = r
+        while rows % 64 == 0 and rows * c > size:
+            rows //= 2
+        pieces += [(w, at, rows) for at in range(0, r, rows)]
+    return pieces
+
+def gather_kernel(t_size, pieces, count, *refs):
+    ins, outs = refs[:count], refs[count:2*count]
+    z_send, y_send, x_send, d_send, plane_recv, x_recv, d_recv, own_sem = refs[2*count:]
+    me_d, me = lax.axis_index("dp"), lax.axis_index("tensor")
+    core, xpos = me_d % 2, (me_d // 2) % 2
+    line, side = me // 2, me % 2
+    depth = t_size // 2
+    y_mate = 2 * line + 1 - side
+    x_mate = me_d + 2 - 4 * xpos
+    sibling = me_d + 1 - 2 * core
+    barrier = pltpu.get_barrier_semaphore()
+    def z_mate(i):
+        return 2 * lax.rem(line + i, depth) + side
+    for p in [z_mate(i) for i in range(1, depth)] + [y_mate]:
+        pl.semaphore_signal(barrier, inc=1, device_id={"tensor": p}, device_id_type=MESH)
+    for p in (x_mate, sibling):
+        pl.semaphore_signal(barrier, inc=1, device_id={"dp": p}, device_id_type=MESH)
+    pl.semaphore_wait(barrier, depth + 2)
+
+    def rows_of(n, kind):
+        _, at, rows = pieces[n]
+        half = rows // 2
+        a = x_rows(half)
+        start = at + core * half
+        if kind == "plane":
+            return pl.ds(pl.multiple_of(start + xpos * a, 16), half - a)
+        if kind == "x_out":
+            return pl.ds(pl.multiple_of(start + xpos * (half - a), 16), a)
+        return pl.ds(pl.multiple_of(start + (1 - xpos) * (half - a), 16), a)
+    def has_x(n):
+        return x_rows(pieces[n][2] // 2) > 0
+    def remote(n, src, block, rows, ss, rs, device):
+        return pltpu.make_async_remote_copy(src, outs[pieces[n][0]].at[block, rows, :], ss, rs, device_id=device, device_id_type=MESH)
+    def z_copy(n, i):
+        rows = rows_of(n, "plane")
+        return remote(n, ins[pieces[n][0]].at[rows, :], me, rows, z_send.at[n, i], plane_recv.at[n, me], {"tensor": z_mate(i)})
+    def y_own(n):
+        rows = rows_of(n, "plane")
+        return remote(n, ins[pieces[n][0]].at[rows, :], me, rows, y_send.at[n, me // 2], plane_recv.at[n, me], {"tensor": y_mate})
+    def y_copy(n, block):
+        rows = rows_of(n, "plane")
+        return remote(n, outs[pieces[n][0]].at[block, rows, :], block, rows, y_send.at[n, block // 2], plane_recv.at[n, block], {"tensor": y_mate})
+    def x_copy(n, block):
+        rows = rows_of(n, "x_out")
+        return remote(n, outs[pieces[n][0]].at[block, rows, :], block, rows, x_send.at[n, block], x_recv.at[n, block], {"dp": x_mate})
+    def d_copy(n, block, k):
+        rows = rows_of(n, ("plane", "x_in")[k])
+        return remote(n, outs[pieces[n][0]].at[block, rows, :], block, rows, d_send.at[n, block, k], d_recv.at[n, block, k], {"dp": sibling})
+    def landed(n, block, kind, sem):
+        ref = outs[pieces[n][0]].at[block, rows_of(n, kind), :]
+        pltpu.make_async_copy(ref, ref, sem).wait()
+    def loop(lo, hi, body):
+        def step(i, _):
+            body(i)
+            return 0
+        lax.fori_loop(lo, hi, step, 0)
+    def own_copy(w):
+        return pltpu.make_async_copy(ins[w], outs[w].at[me], own_sem.at[w])
+
+    total = len(pieces)
+    def launch(n):
+        if n < total:
+            for i in range(1, depth):
+                z_copy(n, i).start()
+            y_own(n).start()
+    for n in range(gather_ahead):
+        launch(n)
+    for w in range(count):
+        own_copy(w).start()
+    for step in range(total + 2):
+        n = step
+        launch(n + gather_ahead)
+        if n < total:
+            def z_stage(i):
+                block = z_mate(depth - i)
+                landed(n, block, "plane", plane_recv.at[n, block])
+                y_copy(n, block).start()
+                if has_x(n):
+                    x_copy(n, block).start()
+                d_copy(n, block, 0).start()
+            loop(1, depth, z_stage)
+        n1 = step - 1
+        if 0 <= n1 < total:
+            def y_stage(i):
+                block = 2 * lax.rem(line + depth - i, depth) + 1 - side
+                landed(n1, block, "plane", plane_recv.at[n1, block])
+                if has_x(n1):
+                    x_copy(n1, block).start()
+                d_copy(n1, block, 0).start()
+            loop(0, depth, y_stage)
+        n2 = step - 2
+        if 0 <= n2 < total and has_x(n2):
+            def x_stage(i):
+                block = lax.rem(me + i, t_size)
+                landed(n2, block, "x_in", x_recv.at[n2, block])
+                d_copy(n2, block, 1).start()
+            loop(1, t_size, x_stage)
+    for w in range(count):
+        own_copy(w).wait()
+    for n in range(total):
+        loop(1, depth, lambda i: z_copy(n, i).wait_send())
+        y_own(n).wait_send()
+        loop(1, depth, lambda i: y_copy(n, z_mate(i)).wait_send())
+        def finish(i):
+            block = lax.rem(me + i, t_size)
+            for k in range(2 if has_x(n) else 1):
+                d_copy(n, block, k).wait_send()
+            if has_x(n):
+                x_copy(n, block).wait_send()
+        loop(1, t_size, finish)
+        def final(i):
+            block = lax.rem(me + i, t_size)
+            _, at, rows = pieces[n]
+            half = rows // 2
+            a = x_rows(half)
+            start = at + (1 - core) * half
+            got = pl.ds(pl.multiple_of(start + xpos * a, 16), half - a)
+            ref = outs[pieces[n][0]].at[block, got, :]
+            pltpu.make_async_copy(ref, ref, d_recv.at[n, block, 0]).wait()
+            if has_x(n):
+                got = pl.ds(pl.multiple_of(start + (1 - xpos) * (half - a), 16), a)
+                ref = outs[pieces[n][0]].at[block, got, :]
+                pltpu.make_async_copy(ref, ref, d_recv.at[n, block, 1]).wait()
+        loop(1, t_size, final)
+
+def gather_weights(weights, t, cid, size=1 << 17):
+    count = len(weights)
+    shapes = [w.shape for w in weights]
+    pieces = piece_list(shapes, size)
+    dma = pltpu.SemaphoreType.DMA
+    depth = t // 2
+    m = len(pieces)
+    return pl.pallas_call(
+        functools.partial(gather_kernel, t, pieces, count),
+        out_shape=[jax.ShapeDtypeStruct((t,) + w.shape, w.dtype) for w in weights],
+        in_specs=[pl.BlockSpec(memory_space=pl.ANY)] * count,
+        out_specs=[pl.BlockSpec(memory_space=pl.ANY)] * count,
+        scratch_shapes=[dma((m, depth)), dma((m, depth)), dma((m, t)), dma((m, t, 2)), dma((m, t)), dma((m, t)), dma((m, t, 2)), dma((count,))],
+        compiler_params=pltpu.CompilerParams(collective_id=cid, has_side_effects=True),
+    )(*weights)
+
+
+def reduce_kernel(depth, pieces, count, size, *refs):
+    ins, outs = refs[:count], refs[count:2*count]
+    own, r1, r2y, r2x, r3y, r3x, s3y, r4y, r4x, fin, send, recv, local, store = refs[2*count:]
+    H = size // 2
+    Hy = H // 2
+    Q = H // 4
+    me_d, me = lax.axis_index("dp"), lax.axis_index("tensor")
+    core, xpos = me_d % 2, (me_d // 2) % 2
+    line, side = me // 2, me % 2
+    y_mate = {"tensor": 2 * line + 1 - side}
+    x_mate = {"dp": me_d + 2 - 4 * xpos}
+    sibling = {"dp": me_d + 1 - 2 * core}
+    z_lines = [None] + [lax.rem(line + i, depth) for i in range(1, depth)]
+    barrier = pltpu.get_barrier_semaphore()
+    for p in [{"tensor": 2 * z + side} for z in z_lines[1:]] + [y_mate, x_mate, sibling]:
+        pl.semaphore_signal(barrier, inc=1, device_id=p, device_id_type=MESH)
+    pl.semaphore_wait(barrier, depth + 2)
+
+    def remote(src, dst, n, k, device):
+        return pltpu.make_async_remote_copy(src, dst, send.at[n, k], recv.at[n, k], device_id=device, device_id_type=MESH)
+    def at16(v):
+        return pl.multiple_of(v, 16)
+    def load(n):
+        w, at = pieces[n]
+        return pltpu.make_async_copy(ins[w].at[:, :, pl.ds(at16(at + core * H), H), :], own.at[n], local.at[n])
+    def copy_core(n):
+        w, at = pieces[n]
+        return remote(ins[w].at[:, :, pl.ds(at16(at + (1 - core) * H), H), :], r1.at[n], n, 0, sibling)
+    def copy_y(n):
+        return remote(r1.at[n, 1 - side, :, pl.ds(0, Hy), :], r2y.at[n], n, 1, y_mate)
+    def copy_x(n):
+        return remote(r1.at[n, :, :, pl.ds(at16(Hy + (1 - xpos) * Q), Q), :], r2x.at[n], n, 2, x_mate)
+    def copy_yz(n, i):
+        return remote(r2y.at[n, z_lines[i]], r3y.at[n, i - 1], n, 2 + i, {"tensor": 2 * z_lines[i] + side})
+    def copy_xy(n):
+        return remote(r2x.at[n, 1 - side], r3x.at[n], n, 2 + depth, y_mate)
+    def copy_yx(n):
+        return remote(s3y.at[n], r4y.at[n], n, 3 + depth, x_mate)
+    def copy_xz(n, i):
+        return remote(r3x.at[n, z_lines[i]], r4x.at[n, i - 1], n, 3 + depth + i, {"tensor": 2 * z_lines[i] + side})
+    def copy_xx(n):
+        ref = fin.at[n, pl.ds(at16(core * H + Hy + xpos * Q), Q), :]
+        return remote(ref, ref, n, 3 + 2 * depth, x_mate)
+    def copy_back(n):
+        ref = fin.at[n, pl.ds(at16(core * H), H), :]
+        return remote(ref, ref, n, 4 + 2 * depth, sibling)
+    def write(n):
+        w, at = pieces[n]
+        return pltpu.make_async_copy(fin.at[n], outs[w].at[pl.ds(at, size), :], store.at[n])
+    def loop(hi, body):
+        def step(i, _):
+            body(i)
+            return 0
+        lax.fori_loop(0, hi, step, 0)
+
+    total = len(pieces)
+    for n in range(total):
+        load(n).start()
+        copy_core(n).start()
+
+    def stage0(n):
+        load(n).wait()
+        copy_core(n).wait_recv()
+        def add(i):
+            a, b = i // depth, i % depth
+            r1[n, a, b] = r1[n, a, b] + own[n, a, b]
+        loop(2 * depth, add)
+        copy_y(n).start()
+        copy_x(n).start()
+    def stage1(n):
+        copy_y(n).wait_recv()
+        def add(i):
+            r2y[n, i] = r2y[n, i] + r1[n, side, i, 0:Hy, :]
+        loop(depth, add)
+        for i in range(1, depth):
+            copy_yz(n, i).start()
+        copy_x(n).wait_recv()
+        def addx(i):
+            a, b = i // depth, i % depth
+            r2x[n, a, b] = r2x[n, a, b] + r1[n, a, b, pl.ds(at16(Hy + xpos * Q), Q), :]
+        loop(2 * depth, addx)
+        copy_xy(n).start()
+    def stage2(n):
+        copy_xy(n).wait_recv()
+        def add(i):
+            r3x[n, i] = r3x[n, i] + r2x[n, side, i]
+        loop(depth, add)
+        for i in range(1, depth):
+            copy_xz(n, i).start()
+        for i in range(1, depth):
+            copy_yz(n, i).wait_recv()
+        part = r2y[n, line].astype(jnp.float32)
+        for i in range(1, depth):
+            part = part + r3y[n, i - 1].astype(jnp.float32)
+        s3y[n] = part.astype(jnp.bfloat16)
+        copy_yx(n).start()
+    def stage3(n):
+        for i in range(1, depth):
+            copy_xz(n, i).wait_recv()
+        part = r3x[n, line].astype(jnp.float32)
+        for i in range(1, depth):
+            part = part + r4x[n, i - 1].astype(jnp.float32)
+        fin[n, pl.ds(at16(core * H + Hy + xpos * Q), Q), :] = part.astype(jnp.bfloat16)
+        copy_xx(n).start()
+        copy_yx(n).wait_recv()
+        fin[n, pl.ds(at16(core * H), Hy), :] = s3y[n] + r4y[n]
+    def stage4(n):
+        copy_xx(n).wait_recv()
+        copy_back(n).start()
+    def stage5(n):
+        copy_back(n).wait_recv()
+        write(n).start()
+    stages = [stage0, stage1, stage2, stage3, stage4, stage5]
+    for step in range(total + len(stages) - 1):
+        for k in range(len(stages) - 1, -1, -1):
+            if 0 <= step - k < total:
+                stages[k](step - k)
+    for n in range(total):
+        copy_core(n).wait_send()
+        copy_y(n).wait_send()
+        copy_x(n).wait_send()
+        copy_xy(n).wait_send()
+        copy_yx(n).wait_send()
+        copy_xx(n).wait_send()
+        copy_back(n).wait_send()
+        for i in range(1, depth):
+            copy_yz(n, i).wait_send()
+            copy_xz(n, i).wait_send()
+        write(n).wait()
+
+def reduce_grads(grads, t, cid, size=1024):
+    count = len(grads)
+    depth = t // 2
+    pieces = [(w, at) for w, g in enumerate(grads) for at in range(0, g.shape[2], size)]
+    m = len(pieces)
+    H = size // 2
+    Hy, Q = H // 2, H // 4
+    dma = pltpu.SemaphoreType.DMA
+    def buf(*shape):
+        return pltpu.VMEM((m,) + shape + (LANES,), jnp.bfloat16)
+    return pl.pallas_call(
+        functools.partial(reduce_kernel, depth, pieces, count, size),
+        out_shape=[jax.ShapeDtypeStruct(g.shape[2:], jnp.bfloat16) for g in grads],
+        in_specs=[pl.BlockSpec(memory_space=pl.ANY)] * count,
+        out_specs=[pl.BlockSpec(memory_space=pl.ANY)] * count,
+        scratch_shapes=[buf(2, depth, H), buf(2, depth, H), buf(depth, Hy), buf(2, depth, Q), buf(depth - 1, Hy), buf(depth, Q), buf(Hy), buf(Hy), buf(depth - 1, Q), buf(size),
+            dma((m, 5 + 2 * depth)), dma((m, 5 + 2 * depth)), dma((m,)), dma((m,))],
+        compiler_params=pltpu.CompilerParams(collective_id=cid, has_side_effects=True, vmem_limit_bytes=56 << 20),
+    )(*grads)
 
 
 def normalize(rows_in, gain_row, shift_row):
@@ -414,11 +744,6 @@
 
 def product(values, weight):
     return jnp.dot(values, weight, preferred_element_type=jnp.float32)
-
-
-def rows_grad(left, right, t):
-    out = lax.dot_general(left, right, (((0,), (0,)), ((), ())), preferred_element_type=jnp.float32)
-    return out.astype(jnp.bfloat16).reshape(t, -1, right.shape[1])
 
 
 def per_device(
@@ -440,11 +765,11 @@
     low = jnp.bfloat16
     t = lax.axis_size("tensor")
     n, d = tokens.shape
-    w_qkv = widen(gather_weight(self_qkv.reshape(d, -1)), 3)
-    w_kv = widen(gather_weight(cross_kv.reshape(d, -1)), 2)
-    w_so = gather_weight(self_out).reshape(d, d)
-    w_cq = widen(gather_weight(cross_q), 1)
-    w_co = gather_weight(cross_out).reshape(d, d)
+    w_qkv, w_so, w_cq, w_kv, w_co = gather_weights(
+        [self_qkv.reshape(d, -1), self_out, cross_q, cross_kv.reshape(d, -1), cross_out], t, 8
+    )
+    w_qkv, w_cq, w_kv = widen(w_qkv, 3), widen(w_cq, 1), widen(w_kv, 2)
+    w_so, w_co = w_so.reshape(d, d), w_co.reshape(d, d)
     w_hid = gather_weight(hidden_weight)
     w_out = gather_weight(output_weight).reshape(-1, d)
     bias_all = lax.all_gather(hidden_bias, "tensor", axis=0, tiled=True)
@@ -479,31 +804,44 @@
     grad_three, gain_three, shift_three = pull_three(grad_output.astype(jnp.float32))
     bias_out_grad = jnp.sum(grad_three, axis=0)
     grad_three_low = grad_three.astype(low)
-    out_weight_grad = reduce_grad(rows_grad(activated_low, grad_three_low, t))
+    out_weight_part = rows_grad(activated_low, grad_three_low, t)
     grad_act = lax.dot_general(grad_three_low, w_out, NT, preferred_element_type=jnp.float32)
     grad_hidden = gelu_pull(grad_act)[0].astype(low)
     hidden_bias_grad = jnp.sum(grad_hidden, axis=0, dtype=jnp.float32)
-    hidden_weight_grad = reduce_grad(cols_grad(normed_two_low, [grad_hidden], t))
+    hidden_weight_part = cols_grad(normed_two_low, [grad_hidden], t)
+    size = LEN * 8 // t
+    out_weight_grad, hidden_weight_grad = reduce_grads([out_weight_part, hidden_weight_part], t, 9, size)
+    out_weight_grad = rows_result(settle(out_weight_grad), output_weight.shape[0], d)
+    hidden_weight_grad = cols_result(settle(hidden_weight_grad), 1, d, hidden_weight.shape[1])
     grad_two, gain_two, shift_two = pull_two(
         residual_alpha * grad_three + back_product([grad_hidden], w_hid)
     )
     grad_two_low = grad_two.astype(low)
-    cross_out_grad = reduce_grad(rows_grad(cross_heads, grad_two_low, t))
+    cross_out_part = rows_grad(cross_heads, grad_two_low, t)
     grad_co = lax.dot_general(grad_two_low, w_co, NT, preferred_element_type=jnp.float32).astype(low)
     (grad_co,) = to_heads([grad_co], t, 4)
     cross_grads = attend_bwd(cq, ck, cv, co, c_lse, grad_co, False, 256)
     g_cq, g_ck, g_cv = to_tokens(cross_grads, n, d, t, 5)
-    cross_q_grad = reduce_grad(cols_grad(normed_one_low, [g_cq], t))
-    cross_kv_grad = reduce_grad(cols_grad(memory, [g_ck, g_cv], t)).reshape(cross_kv.shape)
+    cross_q_part = cols_grad(normed_one_low, [g_cq], t)
+    cross_kv_part = cols_grad(memory, [g_ck, g_cv], t)
+    cross_out_grad, cross_q_grad, cross_kv_grad = reduce_grads(
+        [cross_out_part, cross_q_part, cross_kv_part], t, 10, size
+    )
+    cross_out_grad = rows_result(settle(cross_out_grad), cross_out.shape[0], d)
+    cross_q_grad = cols_result(settle(cross_q_grad), 1, d, cross_q.shape[1])
+    cross_kv_grad = cols_result(settle(cross_kv_grad), 2, d, cross_kv.shape[2]).reshape(cross_kv.shape)
     grad_memory = back_product([g_ck, g_cv], w_kv)
     grad_one, gain_one, shift_one = pull_one(residual_alpha * grad_two + back_product([g_cq], w_cq))
     grad_one_low = grad_one.astype(low)
-    self_out_grad = reduce_grad(rows_grad(self_heads, grad_one_low, t))
+    self_out_part = rows_grad(self_heads, grad_one_low, t)
     grad_so = lax.dot_general(grad_one_low, w_so, NT, preferred_element_type=jnp.float32).astype(low)
     (grad_so,) = to_heads([grad_so], t, 6)
     self_grads = attend_bwd(sq, sk, sv, so, s_lse, grad_so, True, 256)
     g_qkv = to_tokens(self_grads, n, d, t, 7)
-    self_qkv_grad = reduce_grad(cols_grad(tokens, g_qkv, t)).reshape(self_qkv.shape)
+    self_qkv_part = cols_grad(tokens, g_qkv, t)
+    self_out_grad, self_qkv_grad = reduce_grads([self_out_part, self_qkv_part], t, 11, size)
+    self_out_grad = rows_result(settle(self_out_grad), self_out.shape[0], d)
+    self_qkv_grad = cols_result(settle(self_qkv_grad), 3, d, self_qkv.shape[2]).reshape(self_qkv.shape)
     grad_tokens = residual_alpha * grad_one + back_product(g_qkv, w_qkv)
     gain_total, shift_total, bias_total, hidden_bias_total = lax.psum(
         (

time: 1250 us -> 871 us (0.70)
  waiting for transfers between devices: 447 us -> 0.08 us
  Pallas kernels: 334 us -> 674 us
  starting transfers between devices: 143 us -> 0.08 us
  local copies, waits for them, and re-layouts: 99.1 us -> 55.4 us
  other arithmetic: 63.6 us -> 22.2 us
  matrix products: 44.5 us -> 26.8 us
  blocking collectives: 83.3 us -> 67.7 us
    pallas_call x4 -> x11, Pallas kernels: 25.1 us -> 356 us  [the longest x3 204 us: reduce_grads(): pl.pallas_call(functools.partial(reduce_kernel, depth, pieces, count, siz...]
    all_gather x7 -> x2, waiting for transfers between devices: 283 us -> 0.04 us  [gather_weight(): whole = lax.all_gather(share, ('tensor', 'dp'), axis=0, tiled=True)]
    ppermute x70 -> x0, waiting for transfers between devices: 165 us -> none  [the longest x28 118 us: swap(): return lax.ppermute(value, axis, [(i, i ^ bit) for i in range(size)])]
    ppermute x70 -> x0, starting transfers between devices: 143 us -> none  [the longest x42 122 us: reduce_grad(): lax.ppermute(passed, 'tensor', [(2 * i + j, 2 * (i + sign) + j) for i in...]
    add x50 -> x0, other arithmetic: 40.4 us -> none  [the longest x7 15.9 us: reduce_grad(): total = pick(halves, core, 1) + swap(pick(halves, 1 - core, 1), 'dp', 1)]
    squeeze x20 -> x0, local copies, waits for them, and re-layouts: 19.1 us -> none  [pick(): return lax.dynamic_index_in_dim(value, index, axis, keepdims=False)]
    psum x1, blocking collectives: 55.4 us -> 39.8 us  [per_device(): lax.psum((jnp.stack([gain_one, gain_two, gain_three]), jnp.stack([shift_o...]
    dot_general x3 -> x0, matrix products: 15.1 us -> none  [rows_grad(): lax.dot_general(left, right, (((0,), (0,)), ((), ())), preferred_element_...]
  transfers between devices with their start and end apart: 77 -> 2, of which waited for: 30 -> 0; matrix products, arithmetic and copies ran while one was open for 9% -> 2% of each run, Pallas kernels for 13% -> 32%
where the time goes in v2:
time: 871 us; the launch traced here: 862 us
  Pallas kernels  674 us (77%)
  blocking collectives  67.7 us (8%)
  local copies, waits for them, and re-layouts  55.4 us (6%)
  matrix products  26.8 us (3%)
  other arithmetic  22.2 us (3%)
  between operations  15.4 us (2%)
    pallas_call x3, Pallas kernels, reduce_grads(): pl.pallas_call(functools.partial(reduce_kernel, depth, pieces, count, siz...  204 us
    pallas_call x4, Pallas kernels, to_heads(): pl.pallas_call(functools.partial(to_heads_kernel, count, tsize, pairs, bl...  118 us
    pallas_call x1, Pallas kernels, gather_weights(): pl.pallas_call(functools.partial(gather_kernel, t, pieces, count), out_sh...  113 us
    pallas_call x4, Pallas kernels, to_tokens(): pl.pallas_call(functools.partial(to_tokens_kernel, count, tsize, pairs, b...  95.9 us
    unnamed x165, local copies, waits for them, and re-layouts  48.6 us
    psum x1, blocking collectives, per_device(): lax.psum((jnp.stack([gain_one, gain_two, gain_three]), jnp.stack([shift_o...  39.8 us
    pallas_call x4, Pallas kernels, back_product(): pl.pallas_call(functools.partial(back_kernel, count), grid=(t,), out_shap...  29.2 us
    pallas_call x2, Pallas kernels, attend_bwd(): pl.pallas_call(functools.partial(bwd_kernel, causal, bq), grid=(pairs,),...  28.9 us
  transfers between devices with their start and end apart: 2, of which 0 were waited for; matrix products, arithmetic and copies ran while one was open for 2% of the time, Pallas kernels for 32%

profile of v2, /device:TPU:0, one launch (start us, length us, event | category | flops | bytes accessed | tf_op | source)
XLA Modules:
  0.0 862.1 jit_solution(7393455355679346686)
XLA Ops:
  9.2 1.7 constant_dynamic-slice_fusion
  10.9 27.9 %all-gather = bf16[8,1,512]{2,1,0:T(2,128)(2,1)S(1)} all-gather(bf16[1,1,512]{2,1,0:T(2,128)(2,1)S(1)} %reshape.242), channel_id=1, replica_groups=mesh['dp'=4,'tensor'=8] {'tensor'}, dimensions={0}, use_global_device_ids=true | all-gather | bytes 9216 | tf_op jit(solution)/shard_map/all_gather | solution.py:775
  41.2 112.6 %shard_map.245 = (bf16[8,1024,384]{2,1,0:T(8,128)(2,1)}, bf16[8,128,1024]{2,1,0:T(8,128)(2,1)}, bf16[8,1024,128]{2,1,0:T(8,128)(2,1)}, bf16[8,1024,256]{2,1,0:T(8,128)(2,1)}, bf16[8,128,1024]{2,1,0:T(8,128)(2,1)}) custom-call(bf16[1024,384]{1,0:T(8,128)(2,1)} %copy.42.refs_0_, bf16[128,1024]{1,0:T(8,128)(2,1)} %refs_1_.1, bf16[1024,128]{1,0:T(8,128)(2,1)} %refs_2_.1, ...), custom_call_target="tpu_custom_call" | custom-call | tf_op jit(solution)/shard_map/pallas_call | solution.py:573
  153.8 8.0 shard_map.246
  164.5 58.7 %shard_map.247 = (bf16[3,1024,128]{2,1,0:T(8,128)(2,1)}, bf16[3,1024,128]{2,1,0:T(8,128)(2,1)}, bf16[3,1024,128]{2,1,0:T(8,128)(2,1)}) custom-call(bf16[384,1024]{1,0:T(8,128)(2,1)} %copy-done.43, bf16[384,1024]{1,0:T(8,128)(2,1)} %copy-done.44, bf16[384,1024]{1,0:T(8,128)(2,1)} %copy-done.45), custom_call_target="tpu_custom_call" | custom-call | tf_op jit(solution)/shard_map/pallas_call | solution.py:77
  226.7 8.2 shard_map.248
  235.8 15.6 %shard_map.249.x_ref = bf16[384,1024]{1,0:T(8,128)(2,1)} custom-call(bf16[3,1024,128]{2,1,0:T(8,128)(2,1)} %copy-done.33), custom_call_target="tpu_custom_call" | custom-call | tf_op jit(solution)/shard_map/pallas_call | solution.py:134
  251.4 2.9 fusion.22
  256.7 3.1 shard_map.250.refs_0_
  259.8 6.7 shard_map.251
  268.3 31.2 %shard_map.252 = (bf16[3,1024,128]{2,1,0:T(8,128)(2,1)}, bf16[3,1024,128]{2,1,0:T(8,128)(2,1)}, bf16[3,1024,128]{2,1,0:T(8,128)(2,1)}) custom-call(bf16[384,1024]{1,0:T(8,128)(2,1)} %copy-done.26, bf16[384,1024]{1,0:T(8,128)(2,1)} %copy-done.46, bf16[384,1024]{1,0:T(8,128)(2,1)} %copy-done.47), custom_call_target="tpu_custom_call" | custom-call | tf_op jit(solution)/shard_map/pallas_call | solution.py:77
  302.9 10.6 %shard_map.253 = (bf16[3,1024,128]{2,1,0:T(8,128)(2,1)S(1)}, f32[3,8,1024]{2,1,0:T(8,128)S(1)}) custom-call(bf16[3,1024,128]{2,1,0:T(8,128)(2,1)S(1)} %copy-done.54, bf16[3,1024,128]{2,1,0:T(8,128)(2,1)S(1)} %copy-done.56, bf16[3,1024,128]{2,1,0:T(8,128)(2,1)S(1)} %copy-done.58), custom_call_target="tpu_custom_call" | custom-call | flops 1610612736 | bytes 3145728 | tf_op jit(solution)/shard_map/pallas_call | solution.py:183
  314.4 13.2 %shard_map.254.x_ref = bf16[384,1024]{1,0:T(8,128)(2,1)} custom-call(bf16[3,1024,128]{2,1,0:T(8,128)(2,1)} %copy-done.35), custom_call_target="tpu_custom_call" | custom-call | tf_op jit(solution)/shard_map/pallas_call | solution.py:134
  327.6 3.0 fusion.23
  332.1 10.1 %shard_map.255 = f32[384,4096]{1,0:T(8,128)} custom-call(bf16[384,1024]{1,0:T(8,128)(2,1)S(1)} %fusion.12.x_ref, bf16[8,1024,512]{2,1,0:T(8,128)(2,1)} %bitcast.74), custom_call_target="tpu_custom_call" | custom-call | flops 3221225472 | bytes 12320768 | tf_op jit(solution)/shard_map/pallas_call | solution.py:255
  342.2 4.1 multiply_convert_fusion.x_ref
  346.3 7.4 fusion.24
  358.6 9.7 %convert_reduce_fusion = (f32[4096]{0:T(1024)S(1)}, bf16[384,4096]{1,0:T(8,128)(2,1)S(1)}) fusion(f32[384,4096]{1,0:T(8,128)S(1)} %copy-done.60, f32[4096]{0:T(1024)S(1)} %bitcast.87, bf16[384,1024]{1,0:T(8,128)(2,1)S(1)} %add_convert_fusion.3.y_ref, bf16[4096,1024]{1,0:T(8,128)(2,1)} %all-gather.6.cloned.1.call-done), kind=kOutput, calls=%fused_computation.9 | convolution fusion | flops 3257397248 | bytes 18644992 | tf_op jit(solution)/shard_map/dot_general | solution.py:808
  368.4 10.0 %shard_map.256 = f32[384,1024]{1,0:T(8,128)S(1)} custom-call(bf16[384,4096]{1,0:T(8,128)(2,1)S(1)} %get-tuple-element.106.refs_0_, bf16[8,1024,512]{2,1,0:T(8,128)(2,1)} %bitcast.75), custom_call_target="tpu_custom_call" | custom-call | flops 3221225472 | bytes 13107200 | tf_op jit(solution)/shard_map/pallas_call | solution.py:290
  382.0 1.9 convolution_convert_fusion.1.refs_0_
  384.7 13.3 %shard_map.257.do_ref = bf16[3,1024,128]{2,1,0:T(8,128)(2,1)} custom-call(bf16[384,1024]{1,0:T(8,128)(2,1)} %convolution_convert_fusion.1.refs_0_), custom_call_target="tpu_custom_call" | custom-call | tf_op jit(solution)/shard_map/pallas_call | solution.py:77
  402.5 16.9 %shard_map.258 = (bf16[3,1024,128]{2,1,0:T(8,128)(2,1)S(1)}, bf16[3,1024,128]{2,1,0:T(8,128)(2,1)S(1)}, bf16[3,1024,128]{2,1,0:T(8,128)(2,1)S(1)}) custom-call(bf16[3,1024,128]{2,1,0:T(8,128)(2,1)S(1)} %copy-done.55, bf16[3,1024,128]{2,1,0:T(8,128)(2,1)S(1)} %copy-done.57, bf16[3,1024,128]{2,1,0:T(8,128)(2,1)S(1)} %copy-done.59, ...), custom_call_target="tpu_custom_call" | custom-call | flops 4026531840 | bytes 6291456 | tf_op jit(solution)/shard_map/pallas_call | solution.py:232
  422.1 32.7 %shard_map.259 = (bf16[384,1024]{1,0:T(8,128)(2,1)}, bf16[384,1024]{1,0:T(8,128)(2,1)}, bf16[384,1024]{1,0:T(8,128)(2,1)}) custom-call(bf16[3,1024,128]{2,1,0:T(8,128)(2,1)} %copy-done.37, bf16[3,1024,128]{2,1,0:T(8,128)(2,1)} %copy-done.38, bf16[3,1024,128]{2,1,0:T(8,128)(2,1)} %copy-done.39), custom_call_target="tpu_custom_call" | custom-call | tf_op jit(solution)/shard_map/pallas_call | solution.py:134
  454.8 1.6 copy-done.5
  457.5 4.3 shard_map.260
  461.9 3.6 shard_map.270.refs_1_
  466.9 2.9 shard_map.269.refs_0_
  472.0 2.0 copy-done.78
  474.0 1.9 convolution_convert_fusion.refs_0_
  475.8 3.0 shard_map.266.refs_0_
  480.1 14.6 %shard_map.261.do_ref = bf16[3,1024,128]{2,1,0:T(8,128)(2,1)} custom-call(bf16[384,1024]{1,0:T(8,128)(2,1)} %convolution_convert_fusion.refs_0_), custom_call_target="tpu_custom_call" | custom-call | tf_op jit(solution)/shard_map/pallas_call | solution.py:77
  499.3 11.9 %shard_map.262 = (bf16[3,1024,128]{2,1,0:T(8,128)(2,1)S(1)}, bf16[3,1024,128]{2,1,0:T(8,128)(2,1)S(1)}, bf16[3,1024,128]{2,1,0:T(8,128)(2,1)S(1)}) custom-call(bf16[3,1024,128]{2,1,0:T(8,128)(2,1)S(1)} %copy-done.49, bf16[3,1024,128]{2,1,0:T(8,128)(2,1)S(1)} %copy-done.51, bf16[3,1024,128]{2,1,0:T(8,128)(2,1)S(1)} %copy-done.53, ...), custom_call_target="tpu_custom_call" | custom-call | flops 4026531840 | bytes 6291456 | tf_op jit(solution)/shard_map/pallas_call | solution.py:232
  513.9 34.5 %shard_map.263 = (bf16[384,1024]{1,0:T(8,128)(2,1)}, bf16[384,1024]{1,0:T(8,128)(2,1)}, bf16[384,1024]{1,0:T(8,128)(2,1)}) custom-call(bf16[3,1024,128]{2,1,0:T(8,128)(2,1)} %copy-done.40, bf16[3,1024,128]{2,1,0:T(8,128)(2,1)} %copy-done.41, bf16[3,1024,128]{2,1,0:T(8,128)(2,1)} %copy-done.42), custom_call_target="tpu_custom_call" | custom-call | tf_op jit(solution)/shard_map/pallas_call | solution.py:134
  551.7 8.9 %shard_map.264 = f32[384,1024]{1,0:T(8,128)S(1)} custom-call(bf16[384,1024]{1,0:T(8,128)(2,1)S(1)} %copy-done.16, bf16[384,1024]{1,0:T(8,128)(2,1)S(1)} %copy-done.18, bf16[384,1024]{1,0:T(8,128)(2,1)S(1)} %copy-done.19, bf16[8,1024,384]{2,1,0:T(8,128)(2,1)} %get-tuple-element.53.w_ref.refs_3_), custom_call_target="tpu_custom_call" | custom-call | flops 2415919104 | bytes 10223616 | tf_op jit(solution)/shard_map/pallas_call | solution.py:290
  560.7 7.5 shard_map.267.refs_1_
  568.2 6.0 shard_map.265
  574.2 6.0 shard_map.271.refs_2_
  580.2 7.9 shard_map.273.refs_0_
  588.1 8.2 shard_map.274.refs_1_
  597.6 57.7 %shard_map.268 = (bf16[1024,128]{1,0:T(8,128)(2,1)}, bf16[3072,128]{1,0:T(8,128)(2,1)}) custom-call(bf16[2,4,1024,128]{3,2,1,0:T(8,128)(2,1)} %copy-done.8, bf16[2,4,3072,128]{3,2,1,0:T(8,128)(2,1)} %shard_map.267.refs_1_), custom_call_target="tpu_custom_call" | custom-call | tf_op jit(solution)/shard_map/pallas_call | solution.py:723
  655.4 2.4 convert_bitcast_fusion.2
  657.7 55.0 %shard_map.272 = (bf16[1024,128]{1,0:T(8,128)(2,1)}, bf16[1024,128]{1,0:T(8,128)(2,1)}, bf16[2048,128]{1,0:T(8,128)(2,1)}) custom-call(bf16[2,4,1024,128]{3,2,1,0:T(8,128)(2,1)} %copy-done.7, bf16[2,4,1024,128]{3,2,1,0:T(8,128)(2,1)} %copy-done.6, bf16[2,4,2048,128]{3,2,1,0:T(8,128)(2,1)} %shard_map.271.refs_2_), custom_call_target="tpu_custom_call" | custom-call | tf_op jit(solution)/shard_map/pallas_call | solution.py:723
  712.7 1.8 convert_element_type.64
  714.5 2.5 copy.59
  717.1 91.7 %shard_map.275 = (bf16[4096,128]{1,0:T(8,128)(2,1)}, bf16[4096,128]{1,0:T(8,128)(2,1)}) custom-call(bf16[2,4,4096,128]{3,2,1,0:T(8,128)(2,1)} %shard_map.273.refs_0_, bf16[2,4,4096,128]{3,2,1,0:T(8,128)(2,1)} %shard_map.274.refs_1_), custom_call_target="tpu_custom_call" | custom-call | tf_op jit(solution)/shard_map/pallas_call | solution.py:723
  808.7 2.9 copy_bitcast_fusion
  811.7 1.6 copy_bitcast_fusion.1
  813.3 39.8 %all-reduce = (f32[4096]{0:T(1024)S(1)}, f32[1024]{0:T(1024)}, f32[3,1024]{1,0:T(4,128)}, f32[3,1024]{1,0:T(4,128)}) all-reduce(f32[4096]{0:T(1024)S(1)} %get-tuple-element.105, f32[1024]{0:T(1024)S(1)} %get-tuple-element.116, f32[3,1024]{1,0:T(4,128)S(1)} %get-tuple-element.129, ...), channel_id=1, replica_groups=mesh['dp'=4,'tensor'=8] {'dp','tensor'}, use_global_device_ids=true, to_apply=%region_13.0 | all-reduce | flops 11264 | bytes 90112 | tf_op jit(solution)/shard_map/psum | solution.py:846
  (204 shorter events, 57.2 us)
Async XLA Ops:
  7.2 1.2 copy-start
  7.2 3.7 copy-start.77
  7.2 31.6 %copy-start.72 = (bf16[1024,2,128]{2,1,0:T(2,128)(2,1)S(1)}, bf16[1024,2,128]{2,1,0:T(2,128)(2,1)}, u32[]{:S(2)}) copy-start(bf16[1024,2,128]{2,1,0:T(2,128)(2,1)} %param.19) | copy-start | bytes 1572868
  7.2 32.5 %copy-start.71 = (bf16[1024,3,128]{2,0,1:T(8,128)(2,1)S(1)}, bf16[1024,3,128]{2,0,1:T(8,128)(2,1)}, u32[]{:S(2)}) copy-start(bf16[1024,3,128]{2,0,1:T(8,128)(2,1)} %param.16) | copy-start | bytes 2359300
  7.2 324.9 %all-gather.4.cloned.1.call-start = ((), (), s32[]{:S(2)}) async-start(), calls=%async_computation | async-start | bytes 8650752 | tf_op jit(solution)/shard_map/all_gather | solution.py:401
  9.2 337.2 %all-gather.6.cloned.1.call-start = ((), (), s32[]{:S(2)}) async-start(), calls=%async_computation.1 | async-start | bytes 8650752 | tf_op jit(solution)/shard_map/all_gather | solution.py:401
  40.0 113.8 %copy-start.29 = (bf16[384,1024]{1,0:T(8,128)(2,1)S(1)}, bf16[384,1024]{1,0:T(8,128)(2,1)}, u32[]{:S(2)}) copy-start(bf16[384,1024]{1,0:T(8,128)(2,1)} %x_ref.6) | copy-start | bytes 2359300
  223.2 1.2 copy-start.48
  254.3 73.3 %copy-start.61 = (f32[384,1024]{1,0:T(8,128)}, f32[384,1024]{1,0:T(8,128)S(1)}, u32[]{:S(2)}) copy-start(f32[384,1024]{1,0:T(8,128)S(1)} %get-tuple-element.124) | copy-start | bytes 4718596
  254.7 2.0 copy-start.4
  255.5 4.4 copy-start.9
  256.7 3.2 copy-start.31
  259.8 6.7 copy-start.26
  330.6 1.1 copy-start.63
  332.1 10.1 %copy-start.11 = (bf16[384,1024]{1,0:T(8,128)(2,1)}, bf16[384,1024]{1,0:T(8,128)(2,1)S(1)}, u32[]{:S(2)}) copy-start(bf16[384,1024]{1,0:T(8,128)(2,1)S(1)} %fusion.12.x_ref) | copy-start | bytes 2359300
  342.2 4.1 copy-start.80
  355.5 3.1 copy-start.60
  358.6 9.7 %copy-start.22 = (bf16[384,1024]{1,0:T(8,128)(2,1)}, bf16[384,1024]{1,0:T(8,128)(2,1)S(1)}, u32[]{:S(2)}) copy-start(bf16[384,1024]{1,0:T(8,128)(2,1)S(1)} %add_convert_fusion.3.y_ref) | copy-start | bytes 2359300
  368.3 10.0 %copy-start.2 = (bf16[384,4096]{1,0:T(8,128)(2,1)}, bf16[384,4096]{1,0:T(8,128)(2,1)S(1)}, u32[]{:S(2)}) copy-start(bf16[384,4096]{1,0:T(8,128)(2,1)S(1)} %get-tuple-element.106.refs_0_) | copy-start | bytes 9437188
  368.3 10.0 %copy-start.64 = (f32[384,1024]{1,0:T(8,128)S(1)}, f32[384,1024]{1,0:T(8,128)}, u32[]{:S(2)}) copy-start(f32[384,1024]{1,0:T(8,128)} %copy-done.63) | copy-start | bytes 4718596
  379.8 2.2 copy-start.79
  454.8 1.6 copy-start.5
  457.5 4.3 copy-start.10
  457.5 4.3 copy-start.28
  461.9 5.0 copy-start.21
  461.9 5.0 copy-start.25
  465.5 1.4 copy-start.6
  466.9 3.0 copy-start.62
  466.9 3.0 copy-start.68
  469.9 1.3 copy-start.7
  471.8 4.1 copy-start.65
  471.8 2.2 copy-start.78
  473.9 1.9 copy-start.20
  478.8 1.3 copy-start.8
  551.7 8.9 %copy-start.17 = (bf16[384,1024]{1,0:T(8,128)(2,1)S(1)}, bf16[384,1024]{1,0:T(8,128)(2,1)}, u32[]{:S(2)}) copy-start(bf16[384,1024]{1,0:T(8,128)(2,1)} %get-tuple-element.80.refs_0_) | copy-start | bytes 2359300
  551.7 8.9 %copy-start.30 = (bf16[384,1024]{1,0:T(8,128)(2,1)S(1)}, bf16[384,1024]{1,0:T(8,128)(2,1)}, u32[]{:S(2)}) copy-start(bf16[384,1024]{1,0:T(8,128)(2,1)} %x_ref.6) | copy-start | bytes 2359300
  560.7 7.5 copy-start.13
  560.7 7.5 copy-start.14
  560.7 7.5 copy-start.15
  568.2 6.0 copy-start.32
  574.2 6.0 copy-start.23
  580.2 7.9 copy-start.3
  580.2 7.9 copy-start.12
  588.1 8.2 copy-start.66
  808.7 2.9 copy-start.70
  811.7 42.1 %copy-start.73 = (bf16[1024,128]{1,0:T(8,128)(2,1)S(1)}, bf16[1024,128]{1,0:T(8,128)(2,1)}, u32[]{:S(2)}) copy-start(bf16[1024,128]{1,0:T(8,128)(2,1)} %get-tuple-element.86) | copy-start | bytes 786436
  811.7 42.1 %copy-start.74 = (bf16[1024,128]{1,0:T(8,128)(2,1)S(1)}, bf16[1024,128]{1,0:T(8,128)(2,1)}, u32[]{:S(2)}) copy-start(bf16[1024,128]{1,0:T(8,128)(2,1)} %get-tuple-element.89) | copy-start | bytes 786436
  811.7 43.2 %copy-start.1 = (bf16[1024,512]{1,0:T(8,128)(2,1)S(1)}, bf16[1024,512]{1,0:T(8,128)(2,1)}, u32[]{:S(2)}) copy-start(bf16[1024,512]{1,0:T(8,128)(2,1)} %param.21) | copy-start | bytes 3145732
  (35 other events, 35.4 us)
Sparse Core Ops, SparseCore 0:
  11.5 115.3 all-gather.3
  130.3 96.2 all-gather.5

commit v3 on v1

v3 whole, which is shorter than its diff:
```python
import functools
import math

import jax
import jax.numpy as jnp
from jax import lax
from jax.experimental import pallas as pl
from jax.experimental.pallas import tpu as pltpu
from jax.sharding import PartitionSpec as P

MESH = pl.DeviceIdType.MESH
DH = 64
LANES = 128
LEN = 1024

residual_alpha = 300.0**0.25
norm_eps = 1e-05


def loop(lo, hi, body):
    def step(i, _):
        body(i)
        return 0

    lax.fori_loop(lo, hi, step, 0)


def weave(main, back):
    for steps in main:
        while steps != 0 and next(back, None) is not None:
            steps -= 1
    for _ in back:
        pass


class Place:
    def __init__(self, t):
        self.t, self.depth = t, t // 2
        self.d, self.me = lax.axis_index("dp"), lax.axis_index("tensor")
        self.core, self.xpos = self.d % 2, (self.d // 2) % 2
        self.line, self.side = self.me // 2, self.me % 2
        self.y_mate = {"tensor": 2 * self.line + 1 - self.side}
        self.x_mate = {"dp": self.d + 2 - 4 * self.xpos}
        self.sibling = {"dp": self.d + 1 - 2 * self.core}

    def line_at(self, i):
        return lax.rem(self.line + i, self.depth)

    def z_mate(self, i):
        return {"tensor": 2 * self.line_at(i) + self.side}

    def greet(self):
        barrier = pltpu.get_barrier_semaphore()
        peers = [{"tensor": lax.rem(self.me + i, self.t)} for i in range(1, self.t)]
        for p in peers + [self.x_mate, self.sibling]:
            pl.semaphore_signal(barrier, inc=1, device_id=p, device_id_type=MESH)
        pl.semaphore_wait(barrier, self.t + 1)


def remote(src, dst, send, recv, device):
    return pltpu.make_async_remote_copy(src, dst, send, recv, device_id=device, device_id_type=MESH)


def landed(ref, sem):
    pltpu.make_async_copy(ref, ref, sem).wait()


def at16(v):
    return pl.multiple_of(v, 16)


def rows_at(start, count):
    return pl.ds(pl.multiple_of(start, count), count)


class Slots:
    def __init__(self, t, n, d):
        self.block = math.gcd(n, LEN)
        self.blocks = n // self.block
        self.per_seq = LEN // self.block
        self.wide = d // LANES
        self.total = n * t // LEN * self.wide
        self.pairs = -(-self.total // t)
        self.units = self.blocks * self.wide
        self.lands = self.pairs * self.per_seq


class ToHeads:
    def __init__(self, place, slots, ins, outs, send, recv):
        self.place, self.slots, self.ins, self.outs, self.send, self.recv = place, slots, ins, outs, send, recv

    def unit(self, a, u):
        s = self.slots
        j, p = u // s.wide, u % s.wide
        g = self.place.me * s.blocks + j
        q = (g // s.per_seq) * s.wide + p
        dst, slot, k = q // s.pairs, q % s.pairs, g % s.per_seq
        src = self.ins[a].at[rows_at(j * s.block, s.block), rows_at(p * LANES, LANES)]
        to = self.outs[a].at[slot, rows_at(k * s.block, s.block), :]
        return dst, src, to, self.send.at[a, u], self.recv.at[a, slot * s.per_seq + k]

    def start(self):
        for a in range(len(self.ins)):

            def one(u):
                dst, src, to, ss, rs = self.unit(a, u)

                @pl.when(dst == self.place.me)
                def _():
                    pltpu.make_async_copy(src, to, rs).start()

                @pl.when(dst != self.place.me)
                def _():
                    remote(src, to, ss, rs, {"tensor": dst}).start()

            loop(0, self.slots.units, one)

    def wait_slot(self, slot):
        s = self.slots

        @pl.when(self.place.me * s.pairs + slot < s.total)
        def _():
            for a in range(len(self.ins)):
                loop(
                    0,
                    s.per_seq,
                    lambda k: landed(
                        self.outs[a].at[slot, rows_at(k * s.block, s.block), :], self.recv.at[a, slot * s.per_seq + k]
                    ),
                )

    def finish(self):
        for a in range(len(self.ins)):

            def one(u):
                dst, src, to, ss, rs = self.unit(a, u)

                @pl.when(dst != self.place.me)
                def _():
                    remote(src, to, ss, rs, {"tensor": dst}).wait_send()

            loop(0, self.slots.units, one)


class ToTokens:
    def __init__(self, place, slots, ins, outs, send, recv):
        self.place, self.slots, self.ins, self.outs, self.send, self.recv = place, slots, ins, outs, send, recv

    def unit(self, a, slot, k):
        s = self.slots
        q = self.place.me * s.pairs + slot
        g = (q // s.wide) * s.per_seq + k
        dst, j, p = g // s.blocks, g % s.blocks, q % s.wide
        src = self.ins[a].at[slot, rows_at(k * s.block, s.block), :]
        to = self.outs[a].at[rows_at(j * s.block, s.block), rows_at(p * LANES, LANES)]
        return q < s.total, dst, src, to, self.send.at[a, slot * s.per_seq + k], self.recv.at[a, j * s.wide + p]

    def start_slot(self, slot):
        for a in range(len(self.ins)):

            def one(k):
                real, dst, src, to, ss, rs = self.unit(a, slot, k)

                @pl.when(real & (dst == self.place.me))
                def _():
                    pltpu.make_async_copy(src, to, rs).start()

                @pl.when(real & (dst != self.place.me))
                def _():
                    remote(src, to, ss, rs, {"tensor": dst}).start()

            loop(0, self.slots.per_seq, one)

    def finish(self):
        s = self.slots
        for a in range(len(self.ins)):

            def sent(u):
                real, dst, src, to, ss, rs = self.unit(a, u // s.per_seq, u % s.per_seq)

                @pl.when(real & (dst != self.place.me))
                def _():
                    remote(src, to, ss, rs, {"tensor": dst}).wait_send()

            loop(0, s.lands, sent)

            def got(r):
                j, p = r // s.wide, r % s.wide
                landed(
                    self.outs[a].at[rows_at(j * s.block, s.block), rows_at(p * LANES, LANES)], self.recv.at[a, r]
                )

            loop(0, s.units, got)


def reshard_sems(slots, heads, tokens):
    dma = pltpu.SemaphoreType.DMA
    return [dma((heads, slots.units)), dma((heads, slots.lands)), dma((tokens, slots.lands)), dma((tokens, slots.units))]


NT = (((1,), (1,)), ((), ()))
NN = (((1,), (0,)), ((), ()))
LOG2E = math.log2(math.e)


def dot(a, b, dims):
    return lax.dot_general(a, b, dims, preferred_element_type=jnp.float32)


def lane_half(shape, h):
    return (lax.broadcasted_iota(jnp.int32, shape, len(shape) - 1) // DH) == h


def attend_block(i, bq, causal, q_ref, k_ref, v_ref, o_ref, lse_ref):
    keys = bq * (i + 1) if causal else LEN
    rows = pl.ds(i * bq, bq)
    q = q_ref[rows, :] * jnp.bfloat16(0.125)
    k = k_ref[:keys, :]
    v = v_ref[:keys, :]
    total = None
    for h in (0, 1):
        qh = jnp.where(lane_half(q.shape, h), q, jnp.bfloat16(0))
        s = dot(qh, k, NT)
        if causal:
            tail = s[:, keys - bq :]
            r = lax.broadcasted_iota(jnp.int32, tail.shape, 0)
            c = lax.broadcasted_iota(jnp.int32, tail.shape, 1)
            tail = jnp.where(c <= r, tail, -1e30)
            s = tail if keys == bq else jnp.concatenate([s[:, : keys - bq], tail], 1)
        m = jnp.max(s, axis=-1, keepdims=True)
        e = jnp.exp2((s - m) * LOG2E)
        total_e = jnp.sum(e, axis=-1, keepdims=True)
        o = dot(e.astype(jnp.bfloat16), v, NN) / total_e
        total = o if h == 0 else jnp.where(lane_half(o.shape, 0), total, o)
        lse = m * LOG2E + jnp.log2(total_e)
        lse_ref[h : h + 1, rows] = jnp.transpose(jnp.broadcast_to(lse, (bq, LANES)))[0:1]
    o_ref[rows, :] = total.astype(jnp.bfloat16)


def attend_back_block(i, bq, causal, q_ref, k_ref, v_ref, o_ref, lse_ref, do_ref, dq_ref, kt_ref, dk_ref, dv_ref):
    keys = bq * (i + 1) if causal else LEN
    rows = pl.ds(i * bq, bq)
    q = q_ref[rows, :] * jnp.bfloat16(0.125)
    do = do_ref[rows, :]
    prod = jnp.transpose(do.astype(jnp.float32) * o_ref[rows, :].astype(jnp.float32))
    k = k_ref[:keys, :]
    v = v_ref[:keys, :]
    dqt = []
    for h in (0, 1):
        mask = lane_half(q.shape, h)
        qh = jnp.where(mask, q, jnp.bfloat16(0))
        doh = jnp.where(mask, do, jnp.bfloat16(0))
        delta = jnp.sum(prod[DH * h : DH * h + DH], axis=0, keepdims=True)
        p = jnp.exp2(dot(k, qh, NT) * LOG2E - lse_ref[h : h + 1, rows])
        if causal:
            tail = p[keys - bq :, :]
            r = lax.broadcasted_iota(jnp.int32, tail.shape, 1)
            c = lax.broadcasted_iota(jnp.int32, tail.shape, 0)
            tail = jnp.where(c <= r, tail, 0.0)
            p = tail if keys == bq else jnp.concatenate([p[: keys - bq], tail], 0)
        ds = (p * (dot(v, doh, NT) - delta)).astype(jnp.bfloat16)
        dv_ref[:keys, :] += dot(p.astype(jnp.bfloat16), doh, NN)
        dk_ref[:keys, :] += dot(ds, qh, NN)
        dqt.append(dot(kt_ref[DH * h : DH * h + DH, :keys], ds, NN))
    dq_ref[rows, :] = (jnp.transpose(jnp.concatenate(dqt, 0)) * 0.125).astype(jnp.bfloat16)


def x_rows(half):
    return min(int(half * 0.36 / 16 + 0.5) * 16, half // 32 * 16)


class Gather:
    def __init__(self, weights, t, size=1 << 17):
        self.t, self.depth = t, t // 2
        self.shapes = [w.shape for w in weights]
        self.pieces = []
        for w, (r, c) in enumerate(self.shapes):
            rows = r
            while rows % 64 == 0 and rows * c > size:
                rows //= 2
            self.pieces += [(w, at, rows) for at in range(0, r, rows)]
        m, dma = len(self.pieces), pltpu.SemaphoreType.DMA
        self.out_shape = [jax.ShapeDtypeStruct((t,) + w.shape, w.dtype) for w in weights]
        self.scratch = [
            dma((m, self.depth)),
            dma((m, self.depth)),
            dma((m, t)),
            dma((m, t, 2)),
            dma((m, t)),
            dma((m, t)),
            dma((m, t, 2)),
            dma((len(weights),)),
        ]

    def rows_of(self, n, kind, core):
        _, at, rows = self.pieces[n]
        half = rows // 2
        a = x_rows(half)
        start, xpos = at + core * half, self.place.xpos
        if kind == "plane":
            return pl.ds(at16(start + xpos * a), half - a)
        if kind == "x_out":
            return pl.ds(at16(start + xpos * (half - a)), a)
        return pl.ds(at16(start + (1 - xpos) * (half - a)), a)

    def steps(self, place, ins, outs, scratch):
        z_send, y_send, x_send, d_send, plane_recv, x_recv, d_recv, own_sem = scratch
        self.place = place
        me, depth, t, pieces = place.me, self.depth, self.t, self.pieces

        def has_x(n):
            return x_rows(pieces[n][2] // 2) > 0

        def rows_of(n, kind, core=place.core):
            return self.rows_of(n, kind, core)

        def part(n, block, kind, core=place.core):
            return outs[pieces[n][0]].at[block, rows_of(n, kind, core), :]

        def column(i, side):
            return 2 * place.line_at(depth - i) + side

        def own(n):
            return ins[pieces[n][0]].at[rows_of(n, "plane"), :]

        def z_copy(n, i):
            return remote(own(n), part(n, me, "plane"), z_send.at[n, i], plane_recv.at[n, me], place.z_mate(i))

        def y_own(n):
            return remote(own(n), part(n, me, "plane"), y_send.at[n, place.line], plane_recv.at[n, me], place.y_mate)

        def y_copy(n, block):
            ref = part(n, block, "plane")
            return remote(ref, ref, y_send.at[n, block // 2], plane_recv.at[n, block], place.y_mate)

        def x_copy(n, block):
            ref = part(n, block, "x_out")
            return remote(ref, ref, x_send.at[n, block], x_recv.at[n, block], place.x_mate)

        def d_copy(n, block, k):
            ref = part(n, block, ("plane", "x_in")[k])
            return remote(ref, ref, d_send.at[n, block, k], d_recv.at[n, block, k], place.sibling)

        def own_copy(w):
            return pltpu.make_async_copy(ins[w], outs[w].at[me], own_sem.at[w])

        total = len(pieces)

        def launch(n):
            if n < total:
                for i in range(1, depth):
                    z_copy(n, i).start()
                y_own(n).start()

        launch(0)
        for w in range(len(ins)):
            own_copy(w).start()
        yield True
        for step in range(total + 2):
            launch(step + 1)
            n = step
            if n < total:

                def z_stage(i):
                    block = column(i, place.side)
                    landed(part(n, block, "plane"), plane_recv.at[n, block])
                    y_copy(n, block).start()
                    if has_x(n):
                        x_copy(n, block).start()
                    d_copy(n, block, 0).start()

                loop(1, depth, z_stage)
            n1 = step - 1
            if 0 <= n1 < total:

                def y_stage(i):
                    block = column(i, 1 - place.side)
                    landed(part(n1, block, "plane"), plane_recv.at[n1, block])
                    if has_x(n1):
                        x_copy(n1, block).start()
                    d_copy(n1, block, 0).start()

                loop(0, depth, y_stage)
            n2 = step - 2
            if 0 <= n2 < total and has_x(n2):

                def x_stage(i):
                    block = lax.rem(me + i, t)
                    landed(part(n2, block, "x_in"), x_recv.at[n2, block])
                    d_copy(n2, block, 1).start()

                loop(1, t, x_stage)
            yield True
        for w in range(len(ins)):
            own_copy(w).wait()
        for n in range(total):
            loop(1, depth, lambda i: z_copy(n, i).wait_send())
            y_own(n).wait_send()
            loop(1, depth, lambda i: y_copy(n, column(i, place.side)).wait_send())

            def finish(i):
                block = lax.rem(me + i, t)
                for k in range(2 if has_x(n) else 1):
                    d_copy(n, block, k).wait_send()
                    landed(part(n, block, ("plane", "x_in")[k], 1 - place.core), d_recv.at[n, block, k])
                if has_x(n):
                    x_copy(n, block).wait_send()

            loop(1, t, finish)
        yield True


class Reduce:
    def __init__(self, grads, t, size):
        self.t, self.depth, self.size = t, t // 2, size
        self.pieces = [(w, at) for w, g in enumerate(grads) for at in range(0, g.shape[2], size)]
        m, depth, dma = len(self.pieces), self.depth, pltpu.SemaphoreType.DMA
        H, Hy, Q = size // 2, size // 4, size // 8

        def buf(*shape):
            return pltpu.VMEM((m,) + shape + (LANES,), jnp.bfloat16)

        self.out_shape = [jax.ShapeDtypeStruct(g.shape[2:], jnp.bfloat16) for g in grads]
        self.scratch = [
            buf(2, depth, H),
            buf(2, depth, H),
            buf(depth, Hy),
            buf(2, depth, Q),
            buf(depth - 1, Hy),
            buf(depth, Q),
            buf(Hy),
            buf(Hy),
            buf(depth - 1, Q),
            buf(size),
            dma((m, 5 + 2 * depth)),
            dma((m, 5 + 2 * depth)),
            dma((m,)),
            dma((m,)),
        ]

    def steps(self, place, ins, outs, scratch):
        own, r1, r2y, r2x, r3y, r3x, s3y, r4y, r4x, fin, send, recv, local, store = scratch
        size, depth, pieces = self.size, self.depth, self.pieces
        H, Hy, Q = size // 2, size // 4, size // 8
        core, xpos, line, side = place.core, place.xpos, place.line, place.side

        def move(src, dst, n, k, device):
            return remote(src, dst, send.at[n, k], recv.at[n, k], device)

        def load(n):
            w, at = pieces[n]
            return pltpu.make_async_copy(ins[w].at[:, :, pl.ds(at16(at + core * H), H), :], own.at[n], local.at[n])

        def copy_core(n):
            w, at = pieces[n]
            return move(ins[w].at[:, :, pl.ds(at16(at + (1 - core) * H), H), :], r1.at[n], n, 0, place.sibling)

        def copy_y(n):
            return move(r1.at[n, 1 - side, :, pl.ds(0, Hy), :], r2y.at[n], n, 1, place.y_mate)

        def copy_x(n):
            return move(r1.at[n, :, :, pl.ds(at16(Hy + (1 - xpos) * Q), Q), :], r2x.at[n], n, 2, place.x_mate)

        def copy_yz(n, i):
            return move(r2y.at[n, place.line_at(i)], r3y.at[n, i - 1], n, 2 + i, place.z_mate(i))

        def copy_xy(n):
            return move(r2x.at[n, 1 - side], r3x.at[n], n, 2 + depth, place.y_mate)

        def copy_yx(n):
            return move(s3y.at[n], r4y.at[n], n, 3 + depth, place.x_mate)

        def copy_xz(n, i):
            return move(r3x.at[n, place.line_at(i)], r4x.at[n, i - 1], n, 3 + depth + i, place.z_mate(i))

        def copy_xx(n):
            ref = fin.at[n, pl.ds(at16(core * H + Hy + xpos * Q), Q), :]
            return move(ref, ref, n, 3 + 2 * depth, place.x_mate)

        def copy_back(n):
            ref = fin.at[n, pl.ds(at16(core * H), H), :]
            return move(ref, ref, n, 4 + 2 * depth, place.sibling)

        def write(n):
            w, at = pieces[n]
            return pltpu.make_async_copy(fin.at[n], outs[w].at[pl.ds(at, size), :], store.at[n])

        total = len(pieces)
        for n in range(total):
            load(n).start()
            copy_core(n).start()
        yield True

        def stage0(n):
            load(n).wait()
            copy_core(n).wait_recv()

            def add(i):
                a, b = i // depth, i % depth
                r1[n, a, b] = r1[n, a, b] + own[n, a, b]

            loop(0, 2 * depth, add)
            copy_y(n).start()
            copy_x(n).start()

        def stage1(n):
            copy_y(n).wait_recv()

            def add(i):
                r2y[n, i] = r2y[n, i] + r1[n, side, i, 0:Hy, :]

            loop(0, depth, add)
            for i in range(1, depth):
                copy_yz(n, i).start()
            copy_x(n).wait_recv()

            def addx(i):
                a, b = i // depth, i % depth
                r2x[n, a, b] = r2x[n, a, b] + r1[n, a, b, pl.ds(at16(Hy + xpos * Q), Q), :]

            loop(0, 2 * depth, addx)
            copy_xy(n).start()

        def stage2(n):
            copy_xy(n).wait_recv()

            def add(i):
                r3x[n, i] = r3x[n, i] + r2x[n, side, i]

            loop(0, depth, add)
            for i in range(1, depth):
                copy_xz(n, i).start()
            for i in range(1, depth):
                copy_yz(n, i).wait_recv()
            part = r2y[n, line].astype(jnp.float32)
            for i in range(1, depth):
                part = part + r3y[n, i - 1].astype(jnp.float32)
            s3y[n] = part.astype(jnp.bfloat16)
            copy_yx(n).start()

        def stage3(n):
            for i in range(1, depth):
                copy_xz(n, i).wait_recv()
            part = r3x[n, line].astype(jnp.float32)
            for i in range(1, depth):
                part = part + r4x[n, i - 1].astype(jnp.float32)
            fin[n, pl.ds(at16(core * H + Hy + xpos * Q), Q), :] = part.astype(jnp.bfloat16)
            copy_xx(n).start()
            copy_yx(n).wait_recv()
            fin[n, pl.ds(at16(core * H), Hy), :] = s3y[n] + r4y[n]

        def stage4(n):
            copy_xx(n).wait_recv()
            copy_back(n).start()

        def stage5(n):
            copy_back(n).wait_recv()
            write(n).start()

        stages = [stage0, stage1, stage2, stage3, stage4, stage5]
        for step in range(total + len(stages) - 1):
            for k in range(len(stages) - 1, -1, -1):
                if 0 <= step - k < total:
                    stages[k](step - k)
            yield True
        for n in range(total):
            copy_core(n).wait_send()
            copy_y(n).wait_send()
            copy_x(n).wait_send()
            copy_xy(n).wait_send()
            copy_yx(n).wait_send()
            copy_xx(n).wait_send()
            copy_back(n).wait_send()
            for i in range(1, depth):
                copy_yz(n, i).wait_send()
                copy_xz(n, i).wait_send()
            write(n).wait()
        yield True


class Total:
    def __init__(self, value, t):
        self.depth = t // 2
        rows, dma = value.shape[0], pltpu.SemaphoreType.DMA
        self.out_shape = [jax.ShapeDtypeStruct(value.shape, jnp.float32)]
        self.scratch = [
            pltpu.VMEM((self.depth, rows, LANES), jnp.float32),
            pltpu.VMEM((3, 2, rows, LANES), jnp.float32),
            dma((self.depth + 3,)),
            dma((self.depth + 3,)),
            dma((2,)),
        ]

    def steps(self, place, ins, outs, scratch):
        along, pair, send, recv, local = scratch
        depth = self.depth

        def z_copy(i):
            return remote(ins[0], along.at[place.line], send.at[i], recv.at[i], place.z_mate(i))

        def swap_copy(k):
            device = (place.y_mate, place.x_mate, place.sibling)[k]
            return remote(pair.at[k, 0], pair.at[k, 1], send.at[depth + k], recv.at[depth + k], device)

        own = pltpu.make_async_copy(ins[0], along.at[place.line], local.at[0])
        own.start()
        for i in range(1, depth):
            z_copy(i).start()
        yield True
        own.wait()
        for i in range(1, depth):
            landed(along.at[place.line_at(depth - i)], recv.at[i])
        total = along[0]
        for i in range(1, depth):
            total = total + along[i]
        for k in range(3):
            pair[k, 0] = total
            swap_copy(k).start()
            yield True
            swap_copy(k).wait_recv()
            total = pair[k, 0] + pair[k, 1]
        for i in range(1, depth):
            z_copy(i).wait_send()
        for k in range(3):
            swap_copy(k).wait_send()
        pair[0, 0] = total
        out = pltpu.make_async_copy(pair.at[0, 0], outs[0], local.at[1])
        out.start()
        out.wait()
        yield True


class Nothing:
    out_shape, scratch = [], []

    def steps(self, place, ins, outs, scratch):
        yield from ()


ANY = pl.BlockSpec(memory_space=pl.ANY)
VMEM = pl.BlockSpec(memory_space=pltpu.VMEM)


def communicate(body, out_shape, ins, in_specs, out_specs, scratch, cid):
    return pl.pallas_call(
        body,
        out_shape=out_shape,
        in_specs=in_specs,
        out_specs=out_specs,
        scratch_shapes=scratch,
        compiler_params=pltpu.CompilerParams(collective_id=cid, has_side_effects=True, vmem_limit_bytes=58 << 20),
    )(*ins)


def jobs_kernel(jobs, groups, t, cid):
    counts = [len(g) for g in groups]
    sizes = [len(j.scratch) for j in jobs]

    def body(*refs):
        place = Place(t)
        place.greet()
        refs = list(refs)
        ins = [[refs.pop(0) for _ in range(c)] for c in counts]
        outs = [[refs.pop(0) for _ in range(c)] for c in counts]
        scratch = [[refs.pop(0) for _ in range(c)] for c in sizes]
        running = [j.steps(place, i, o, s) for j, i, o, s in zip(jobs, ins, outs, scratch)]
        while running:
            running = [g for g in running if next(g, None) is not None]

    total = sum(counts)
    return communicate(
        body,
        [s for j in jobs for s in j.out_shape],
        [a for g in groups for a in g],
        [ANY] * total,
        [ANY] * total,
        [s for j in jobs for s in j.scratch],
        cid,
    )


def attend(tokens_qkv, t, causal, bq, job, job_ins, lead, each, cid):
    n, d = tokens_qkv[0].shape
    slots = Slots(t, n, d)
    pairs = slots.pairs
    held = jax.ShapeDtypeStruct((pairs, LEN, LANES), jnp.bfloat16)
    extra = len(job_ins)

    def body(*refs):
        qkv, refs = refs[:3], refs[3:]
        job_refs, refs = refs[:extra], refs[extra:]
        out, saved, lse, refs = refs[0], refs[1:5], refs[5], refs[6:]
        job_outs, refs = refs[:extra], refs[extra:]
        here, (hs, hr, ts, tr, keep), refs = refs[:4], refs[4:9], refs[9:]
        place = Place(t)
        place.greet()

        def main():
            move = ToHeads(place, slots, qkv, here[:3], hs, hr)
            back = ToTokens(place, slots, here[3:], [out], ts, tr)
            move.start()
            yield lead
            for slot in range(pairs):
                move.wait_slot(slot)
                for i in range(LEN // bq):
                    attend_block(i, bq, causal, *(r.at[slot] for r in here), lse.at[slot])
                    yield each
                back.start_slot(slot)
            copies = [pltpu.make_async_copy(h, s, keep.at[i]) for i, (h, s) in enumerate(zip(here, saved))]
            for c in copies:
                c.start()
            move.finish()
            yield -1
            back.finish()
            for c in copies:
                c.wait()

        weave(main(), job.steps(place, job_refs, job_outs, refs))

    out = communicate(
        body,
        [jax.ShapeDtypeStruct((n, d), jnp.bfloat16)]
        + [held] * 4
        + [jax.ShapeDtypeStruct((pairs, 8, LEN), jnp.float32)]
        + job.out_shape,
        [*tokens_qkv, *job_ins],
        [ANY] * (3 + extra),
        [ANY] * 5 + [VMEM] + [ANY] * extra,
        [pltpu.VMEM(held.shape, held.dtype)] * 4
        + reshard_sems(slots, 3, 1)
        + [pltpu.SemaphoreType.DMA((4,))]
        + job.scratch,
        cid,
    )
    return out[0], out[1:6], out[6:]


def attend_back(grad, saved, t, causal, bq, job, job_ins, lead, every, cid):
    n, d = grad.shape
    slots = Slots(t, n, d)
    pairs = slots.pairs
    held = pltpu.VMEM((pairs, LEN, LANES), jnp.bfloat16)
    extra = len(job_ins)

    def body(grad_ref, q, k, v, o, lse, *refs):
        job_refs, refs = refs[:extra], refs[extra:]
        outs, refs = refs[:3], refs[3:]
        job_outs, refs = refs[:extra], refs[extra:]
        (do, *made, kt, dk, dv, hs, hr, ts, tr), refs = refs[:11], refs[11:]
        place = Place(t)
        place.greet()

        def main():
            move = ToHeads(place, slots, [grad_ref], [do], hs, hr)
            back = ToTokens(place, slots, made, outs, ts, tr)
            move.start()
            yield lead
            count = 0
            for slot in range(pairs):
                move.wait_slot(slot)
                dk[...] = jnp.zeros_like(dk)
                dv[...] = jnp.zeros_like(dv)
                kt[...] = jnp.transpose(k[slot])
                for i in range(LEN // bq):
                    attend_back_block(
                        i,
                        bq,
                        causal,
                        *(r.at[slot] for r in (q, k, v, o, lse, do, made[0])),
                        kt,
                        dk,
                        dv,
                    )
                    count += 1
                    yield 1 if count % every == 0 else 0
                made[1][slot] = dk[...].astype(jnp.bfloat16)
                made[2][slot] = dv[...].astype(jnp.bfloat16)
                back.start_slot(slot)
            move.finish()
            yield -1
            back.finish()

        weave(main(), job.steps(place, job_refs, job_outs, refs))

    out = communicate(
        body,
        [jax.ShapeDtypeStruct((n, d), jnp.bfloat16)] * 3 + job.out_shape,
        [grad, *saved, *job_ins],
        [ANY] + [VMEM] * 5 + [ANY] * extra,
        [ANY] * (3 + extra),
        [held] * 4
        + [pltpu.VMEM((LANES, LEN), jnp.bfloat16)]
        + [pltpu.VMEM((LEN, LANES), jnp.float32)] * 2
        + reshard_sems(slots, 1, 3)
        + job.scratch,
        cid,
    )
    return out[:3], out[3:]


def cols_kernel(count, x_ref, w_ref, *outs):
    out = dot(x_ref[...], w_ref[0], NN)
    width = out.shape[1] // count
    for i, o_ref in enumerate(outs):
        o_ref[...] = out[:, i * width : (i + 1) * width].astype(o_ref.dtype)


def cols_product(x, weight, count, dtype=jnp.bfloat16):
    n, d = x.shape
    t, _, c = weight.shape
    width = c // count
    return pl.pallas_call(
        functools.partial(cols_kernel, count),
        grid=(t,),
        out_shape=[jax.ShapeDtypeStruct((n, t * width), dtype)] * count,
        in_specs=[
            pl.BlockSpec((n, d), lambda i: (0, 0)),
            pl.BlockSpec((1, d, c), lambda i: (i, 0, 0)),
        ],
        out_specs=[pl.BlockSpec((n, width), lambda i: (0, i))] * count,
        compiler_params=pltpu.CompilerParams(vmem_limit_bytes=48 << 20),
        cost_estimate=pl.CostEstimate(
            flops=2 * n * d * t * c, bytes_accessed=2 * (t * d * c + n * d + n * t * c), transcendentals=0
        ),
    )(x, weight)


def back_kernel(count, *refs):
    ys, w_ref, o_ref = refs[:count], refs[count], refs[count + 1]
    y = jnp.concatenate([y_ref[...] for y_ref in ys], 1) if count > 1 else ys[0][...]
    term = dot(y, w_ref[0], NT)

    @pl.when(pl.program_id(0) == 0)
    def _():
        o_ref[...] = term

    @pl.when(pl.program_id(0) != 0)
    def _():
        o_ref[...] += term


def back_product(ys, weight):
    count = len(ys)
    n = ys[0].shape[0]
    t, d, c = weight.shape
    width = c // count
    return pl.pallas_call(
        functools.partial(back_kernel, count),
        grid=(t,),
        out_shape=jax.ShapeDtypeStruct((n, d), jnp.float32),
        in_specs=[pl.BlockSpec((n, width), lambda i: (0, i))] * count
        + [pl.BlockSpec((1, d, c), lambda i: (i, 0, 0))],
        out_specs=pl.BlockSpec((n, d), lambda i: (0, 0)),
        compiler_params=pltpu.CompilerParams(vmem_limit_bytes=48 << 20),
        cost_estimate=pl.CostEstimate(
            flops=2 * n * d * t * c, bytes_accessed=2 * (t * d * c + 2 * n * d + n * t * c), transcendentals=0
        ),
    )(*ys, weight)


def by_side(grad, t):
    return jnp.swapaxes(grad.reshape(t // 2, 2, *grad.shape[1:]), 0, 1)


def cols_grad_kernel(count, x_ref, *refs):
    ys, o_ref, xt_ref = refs[:count], refs[count], refs[count + 1]

    @pl.when(pl.program_id(0) == 0)
    def _():
        xt_ref[...] = jnp.transpose(x_ref[...])

    y = jnp.concatenate([y_ref[...] for y_ref in ys], 1) if count > 1 else ys[0][...]
    out = dot(xt_ref[...], y, NN).astype(o_ref.dtype)
    d = out.shape[0]
    for j in range(out.shape[1] // LANES):
        o_ref[0, 0, j * d : j * d + d, :] = out[:, j * LANES : j * LANES + LANES]


def cols_grad(x, ys, t):
    count = len(ys)
    n, d = x.shape
    blocks = min(t, ys[0].shape[1] // LANES)
    width = ys[0].shape[1] // blocks
    c = width * count
    whole = blocks == t
    out = pl.pallas_call(
        functools.partial(cols_grad_kernel, count),
        grid=(blocks,),
        out_shape=jax.ShapeDtypeStruct(
            (2, t // 2, c // LANES * d, LANES) if whole else (blocks, 1, c // LANES * d, LANES), jnp.bfloat16
        ),
        in_specs=[pl.BlockSpec((n, d), lambda i: (0, 0))]
        + [pl.BlockSpec((n, width), lambda i: (0, i))] * count,
        out_specs=pl.BlockSpec(
            (1, 1, c // LANES * d, LANES), (lambda i: (i % 2, i // 2, 0, 0)) if whole else (lambda i: (i, 0, 0, 0))
        ),
        scratch_shapes=[pltpu.VMEM((d, n), jnp.bfloat16)],
        compiler_params=pltpu.CompilerParams(vmem_limit_bytes=48 << 20),
        cost_estimate=pl.CostEstimate(
            flops=2 * n * d * blocks * c, bytes_accessed=2 * (blocks * d * c + n * d + n * blocks * c), transcendentals=0
        ),
    )(x, *ys)
    if whole:
        return out
    m = t // blocks
    parts = out.reshape(blocks, count, d, m, LANES // m).transpose(0, 3, 1, 2, 4)
    return by_side(parts.reshape(t, count * d // m, LANES), t)


def cols_result(total, count, d, width):
    total = total.astype(jnp.float32)
    if width < LANES:
        return total.reshape(count, d, width).transpose(1, 0, 2).reshape(d, count * width)
    return total.reshape(-1, d, LANES).transpose(1, 0, 2).reshape(d, count * width)


def rows_grad_kernel(x_ref, y_ref, o_ref):
    out = dot(jnp.transpose(x_ref[...]), y_ref[...], NN).astype(o_ref.dtype)
    r = out.shape[0]
    for j in range(out.shape[1] // LANES):
        o_ref[0, 0, j * r : j * r + r, :] = out[:, j * LANES : j * LANES + LANES]


def rows_grad(x, y, t):
    n, d = y.shape
    blocks = min(t, x.shape[1] // LANES)
    r = x.shape[1] // blocks
    whole = blocks == t
    size = d // LANES * r
    out = pl.pallas_call(
        rows_grad_kernel,
        grid=(blocks,),
        out_shape=jax.ShapeDtypeStruct((2, t // 2, size, LANES) if whole else (blocks, 1, size, LANES), jnp.bfloat16),
        in_specs=[pl.BlockSpec((n, r), lambda i: (0, i)), pl.BlockSpec((n, d), lambda i: (0, 0))],
        out_specs=pl.BlockSpec(
            (1, 1, size, LANES), (lambda i: (i % 2, i // 2, 0, 0)) if whole else (lambda i: (i, 0, 0, 0))
        ),
        compiler_params=pltpu.CompilerParams(vmem_limit_bytes=48 << 20),
        cost_estimate=pl.CostEstimate(
            flops=2 * n * d * blocks * r, bytes_accessed=2 * (blocks * d * r + n * d + n * blocks * r), transcendentals=0
        ),
    )(x, y)
    if whole:
        return out
    m = t // blocks
    parts = out.reshape(blocks, d // LANES, m, r // m, LANES).transpose(0, 2, 1, 3, 4)
    return by_side(parts.reshape(t, size // m, LANES), t)


def rows_result(total, r, d):
    return total.astype(jnp.float32).reshape(d // LANES, r, LANES).transpose(1, 0, 2).reshape(r, d)


def gather_weight(weight):
    dp, t = lax.axis_size("dp"), lax.axis_size("tensor")
    rows = weight.shape[0] // dp
    share = lax.dynamic_slice_in_dim(weight, lax.axis_index("dp") * rows, rows, 0)
    whole = lax.all_gather(share, ("tensor", "dp"), axis=0, tiled=True)
    return whole.reshape(t, weight.shape[0], weight.shape[1])


def widen(weight, count):
    t, r, c = weight.shape
    width = c // count
    if width % LANES == 0:
        return weight
    m = LANES // width
    parts = weight.reshape(t // m, m, r, count, width).transpose(0, 2, 3, 1, 4)
    return parts.reshape(t // m, r, count * LANES)


def swap(value, axis, bit):
    size = lax.axis_size(axis)
    return lax.ppermute(value, axis, [(i, i ^ bit) for i in range(size)])


def settle(total):
    bit = 4
    while bit < lax.axis_size("dp"):
        total = total + swap(total, "dp", bit)
        bit *= 2
    return total


def normalize(rows_in, gain_row, shift_row):
    row_mean = jnp.mean(rows_in, axis=-1, keepdims=True)
    centered = rows_in - row_mean
    variance = jnp.mean(centered * centered, axis=-1, keepdims=True)
    return centered * lax.rsqrt(variance + norm_eps) * gain_row + shift_row


def gelu_tanh(values):
    return jax.nn.gelu(values, approximate=True)


def product(values, weight):
    return jnp.dot(values, weight, preferred_element_type=jnp.float32)


def per_device(
    tokens,
    memory,
    self_qkv,
    self_out,
    cross_q,
    cross_kv,
    cross_out,
    hidden_weight,
    hidden_bias,
    output_weight,
    output_bias,
    norm_gain,
    norm_shift,
    grad_output,
):
    low = jnp.bfloat16
    t = lax.axis_size("tensor")
    n, d = tokens.shape
    size = LEN * 8 // t
    w_hid = gather_weight(hidden_weight)
    w_out = gather_weight(output_weight).reshape(-1, d)
    units = hidden_bias.shape[0]
    bias_block = jnp.pad(hidden_bias, (0, 64 * LANES - units)).reshape(64, LANES)
    first = [self_qkv.reshape(d, -1), bias_block]
    w_qkv, bias_all = jobs_kernel([Gather(first, t)], [first], t, 0)
    w_qkv = widen(w_qkv, 3)
    bias_all = bias_all.reshape(t, -1)[:, :units].reshape(-1)

    qkv = cols_product(tokens, w_qkv, 3)
    second = [self_out, cross_q, cross_kv.reshape(d, -1), cross_out]
    self_heads, self_saved, (w_so, w_cq, w_kv, w_co) = attend(
        qkv, t, True, 512, Gather(second, t), second, 4, 1, 1
    )
    w_cq, w_kv = widen(w_cq, 1), widen(w_kv, 2)
    w_so, w_co = w_so.reshape(d, d), w_co.reshape(d, d)
    branch_one = product(self_heads, w_so)
    normed_one, pull_one = jax.vjp(
        normalize, residual_alpha * tokens.astype(jnp.float32) + branch_one, norm_gain[0], norm_shift[0]
    )
    normed_one_low = normed_one.astype(low)
    kv = cols_product(memory, w_kv, 2)
    cq = cols_product(normed_one_low, w_cq, 1)
    cross_heads, cross_saved, _ = attend([*cq, *kv], t, False, 512, Nothing(), [], 0, 0, 2)
    branch_two = product(cross_heads, w_co)
    normed_two, pull_two = jax.vjp(
        normalize, residual_alpha * normed_one + branch_two, norm_gain[1], norm_shift[1]
    )
    normed_two_low = normed_two.astype(low)
    (hidden_low,) = cols_product(normed_two_low, w_hid, 1, jnp.float32)
    hidden_pre = hidden_low + bias_all
    activated, gelu_pull = jax.vjp(gelu_tanh, hidden_pre)
    activated_low = activated.astype(low)
    branch_three = product(activated_low, w_out)
    layer_out, pull_three = jax.vjp(
        normalize, residual_alpha * normed_two + branch_three + output_bias, norm_gain[2], norm_shift[2]
    )
    grad_three, gain_three, shift_three = pull_three(grad_output.astype(jnp.float32))
    bias_out_grad = jnp.sum(grad_three, axis=0)
    grad_three_low = grad_three.astype(low)
    out_weight_part = rows_grad(activated_low, grad_three_low, t)
    grad_act = lax.dot_general(grad_three_low, w_out, NT, preferred_element_type=jnp.float32)
    grad_hidden = gelu_pull(grad_act)[0].astype(low)
    hidden_bias_grad = jnp.sum(grad_hidden, axis=0, dtype=jnp.float32)
    hidden_weight_part = cols_grad(normed_two_low, [grad_hidden], t)
    grad_two, gain_two, shift_two = pull_two(
        residual_alpha * grad_three + back_product([grad_hidden], w_hid)
    )
    grad_two_low = grad_two.astype(low)
    cross_out_part = rows_grad(cross_heads, grad_two_low, t)
    grad_co = lax.dot_general(grad_two_low, w_co, NT, preferred_element_type=jnp.float32).astype(low)
    ff_parts = [out_weight_part, hidden_weight_part]
    (g_cq, g_ck, g_cv), (out_weight_grad, hidden_weight_grad) = attend_back(
        grad_co, cross_saved, t, False, 256, Reduce(ff_parts, t, size), ff_parts, 2, 2, 3
    )
    cross_q_part = cols_grad(normed_one_low, [g_cq], t)
    cross_kv_part = cols_grad(memory, [g_ck, g_cv], t)
    grad_one, gain_one, shift_one = pull_one(residual_alpha * grad_two + back_product([g_cq], w_cq))
    grad_one_low = grad_one.astype(low)
    self_out_part = rows_grad(self_heads, grad_one_low, t)
    grad_so = lax.dot_general(grad_one_low, w_so, NT, preferred_element_type=jnp.float32).astype(low)
    parts = [cross_out_part, cross_q_part, cross_kv_part, self_out_part]
    g_qkv, (cross_out_grad, cross_q_grad, cross_kv_grad, self_out_grad) = attend_back(
        grad_so, self_saved, t, True, 256, Reduce(parts, t, size), parts, 2, 2, 4
    )
    self_qkv_part = cols_grad(tokens, g_qkv, t)
    small = jnp.concatenate(
        [gain_one, gain_two, gain_three, shift_one, shift_two, shift_three, bias_out_grad, hidden_bias_grad]
    ).reshape(-1, LANES)
    self_qkv_grad, small = jobs_kernel(
        [Reduce([self_qkv_part], t, size), Total(small, t)], [[self_qkv_part], [small]], t, 5
    )
    small = settle(small).reshape(-1)
    gain_total, shift_total = small[: 3 * d].reshape(3, d), small[3 * d : 6 * d].reshape(3, d)
    bias_total = small[6 * d : 7 * d]
    hidden_bias_total = lax.dynamic_slice_in_dim(small, 7 * d + lax.axis_index("tensor") * units, units, 0)
    out_weight_grad = rows_result(settle(out_weight_grad), output_weight.shape[0], d)
    hidden_weight_grad = cols_result(settle(hidden_weight_grad), 1, d, hidden_weight.shape[1])
    cross_out_grad = rows_result(settle(cross_out_grad), cross_out.shape[0], d)
    cross_q_grad = cols_result(settle(cross_q_grad), 1, d, cross_q.shape[1])
    cross_kv_grad = cols_result(settle(cross_kv_grad), 2, d, cross_kv.shape[2]).reshape(cross_kv.shape)
    self_out_grad = rows_result(settle(self_out_grad), self_out.shape[0], d)
    self_qkv_grad = cols_result(settle(self_qkv_grad), 3, d, self_qkv.shape[2]).reshape(self_qkv.shape)
    grad_memory = back_product([g_ck, g_cv], w_kv)
    grad_tokens = residual_alpha * grad_one + back_product(g_qkv, w_qkv)
    return (
        layer_out.astype(low),
        grad_tokens,
        grad_memory,
        self_qkv_grad,
        self_out_grad,
        cross_q_grad,
        cross_kv_grad,
        cross_out_grad,
        hidden_weight_grad,
        hidden_bias_total,
        out_weight_grad,
        bias_total,
        gain_total,
        shift_total,
    )


def solution(mesh):
    return jax.shard_map(
        per_device,
        mesh=mesh,
        in_specs=(
            P(("dp", "tensor"), None),
            P(("dp", "tensor"), None),
            P(None, None, "tensor"),
            P("tensor", None),
            P(None, "tensor"),
            P(None, None, "tensor"),
            P("tensor", None),
            P(None, "tensor"),
            P("tensor"),
            P("tensor", None),
            P(),
            P(),
            P(),
            P(("dp", "tensor"), None),
        ),
        out_specs=(
            P(("dp", "tensor"), None),
            P(("dp", "tensor"), None),
            P(("dp", "tensor"), None),
            P(None, None, "tensor"),
            P("tensor", None),
            P(None, "tensor"),
            P(None, None, "tensor"),
            P("tensor", None),
            P(None, "tensor"),
            P("tensor"),
            P("tensor", None),
            P(),
            P(),
            P(),
        ),
        check_vma=False,
    )
```

time: 1250 us -> 735 us (0.59)
  waiting for transfers between devices: 447 us -> 0.08 us
  Pallas kernels: 334 us -> 628 us
  starting transfers between devices: 143 us -> 0.08 us
  blocking collectives: 83.3 us -> 0 us
  local copies, waits for them, and re-layouts: 99.1 us -> 35.4 us
  other arithmetic: 63.6 us -> 18.8 us
  matrix products: 44.5 us -> 26.1 us
    pallas_call x16 -> x13, Pallas kernels: 278 us -> 572 us  [the longest x6 533 us: communicate(): pl.pallas_call(body, out_shape=out_shape, in_specs=in_specs, out_specs=ou...]
    all_gather x7 -> x2, waiting for transfers between devices: 283 us -> 0.04 us  [gather_weight(): whole = lax.all_gather(share, ('tensor', 'dp'), axis=0, tiled=True)]
    ppermute x70 -> x0, waiting for transfers between devices: 165 us -> none  [the longest x28 118 us: swap(): return lax.ppermute(value, axis, [(i, i ^ bit) for i in range(size)])]
    ppermute x70 -> x0, starting transfers between devices: 143 us -> none  [the longest x42 122 us: reduce_grad(): lax.ppermute(passed, 'tensor', [(2 * i + j, 2 * (i + sign) + j) for i in...]
    psum x1 -> x0, blocking collectives: 55.4 us -> none  [per_device(): lax.psum((jnp.stack([gain_one, gain_two, gain_three]), jnp.stack([shift_o...]
    add x50 -> x0, other arithmetic: 40.4 us -> none  [the longest x7 15.9 us: reduce_grad(): total = pick(halves, core, 1) + swap(pick(halves, 1 - core, 1), 'dp', 1)]
    all_gather x1 -> x0, blocking collectives: 27.9 us -> none  [per_device(): bias_all = lax.all_gather(hidden_bias, 'tensor', axis=0, tiled=True)]
    unnamed x220 -> x125, local copies, waits for them, and re-layouts: 47.6 us -> 25.2 us
  transfers between devices with their start and end apart: 77 -> 2, of which waited for: 30 -> 0; matrix products, arithmetic and copies ran while one was open for 9% -> 2% of each run, Pallas kernels for 13% -> 39%
where the time goes in v3:
time: 735 us; the launch traced here: 724 us
  Pallas kernels  628 us (85%)
  local copies, waits for them, and re-layouts  35.4 us (5%)
  matrix products  26.1 us (4%)
  other arithmetic  18.8 us (3%)
  between operations  15.2 us (2%)
    pallas_call x6, Pallas kernels, communicate(): pl.pallas_call(body, out_shape=out_shape, in_specs=in_specs, out_specs=ou...  533 us
    pallas_call x4, Pallas kernels, back_product(): pl.pallas_call(functools.partial(back_kernel, count), grid=(t,), out_shap...  28.3 us
    pallas_call x4, Pallas kernels, cols_product(): pl.pallas_call(functools.partial(cols_kernel, count), grid=(t,), out_shap...  28.2 us
    pallas_call x4, Pallas kernels, cols_grad(): pl.pallas_call(functools.partial(cols_grad_kernel, count), grid=(blocks,)...  25.3 us
    unnamed x125, local copies, waits for them, and re-layouts  25.2 us
  transfers between devices with their start and end apart: 2, of which 0 were waited for; matrix products, arithmetic and copies ran while one was open for 2% of the time, Pallas kernels for 39%

profile of v3, /device:TPU:0, one launch (start us, length us, event | category | flops | bytes accessed | tf_op | source)
XLA Modules:
  0.0 723.9 jit_solution(14627159257846446773)
XLA Ops:
  7.3 1.1 copy-done
  9.2 1.7 constant_dynamic-slice_fusion
  12.1 1.2 copy.35.refs_0_
  13.9 57.2 %shard_map.245 = (bf16[8,1024,384]{2,1,0:T(8,128)(2,1)}, bf16[8,64,128]{2,1,0:T(8,128)(2,1)}) custom-call(bf16[1024,384]{1,0:T(8,128)(2,1)} %copy.35.refs_0_, bf16[64,128]{1,0:T(8,128)(2,1)} %pad_bitcast_fusion.refs_1_), custom_call_target="tpu_custom_call" | custom-call | tf_op jit(solution)/shard_map/pallas_call | solution.py:645
  72.1 8.1 %shard_map.246 = (bf16[384,1024]{1,0:T(8,128)(2,1)S(1)}, bf16[384,1024]{1,0:T(8,128)(2,1)S(1)}, bf16[384,1024]{1,0:T(8,128)(2,1)S(1)}) custom-call(bf16[384,1024]{1,0:T(8,128)(2,1)S(1)} %copy-done.23, bf16[8,1024,384]{2,1,0:T(8,128)(2,1)} %get-tuple-element.51.w_ref.refs_3_), custom_call_target="tpu_custom_call" | custom-call | flops 2415919104 | bytes 9437184 | tf_op jit(solution)/shard_map/pallas_call | solution.py:812
  82.8 121.6 %shard_map.247 = (bf16[384,1024]{1,0:T(8,128)(2,1)}, bf16[3,1024,128]{2,1,0:T(8,128)(2,1)}, bf16[3,1024,128]{2,1,0:T(8,128)(2,1)}, bf16[3,1024,128]{2,1,0:T(8,12...) custom-call(bf16[384,1024]{1,0:T(8,128)(2,1)} %copy-done.27, ...), custom_call_target="tpu_custom_call" | custom-call | tf_op jit(solution)/shard_map/pallas_call | solution.py:645
  204.4 3.0 fusion.23
  208.6 1.4 copy-done.5
  209.9 3.1 shard_map.248.refs_0_
  213.1 6.8 shard_map.249
  221.7 73.2 %shard_map.250 = (bf16[384,1024]{1,0:T(8,128)(2,1)}, bf16[3,1024,128]{2,1,0:T(8,128)(2,1)}, bf16[3,1024,128]{2,1,0:T(8,128)(2,1)}, bf16[3,1024,128]{2,1,0:T(8,12...) custom-call(bf16[384,1024]{1,0:T(8,128)(2,1)} %copy-done.18, bf16[384,1024]{1,0:T(8,128)(2,1)} %copy-done.30, ...), custom_call_target="tpu_custom_call" | custom-call | tf_op jit(solution)/shard_map/pallas_call | solution.py:645
  294.9 2.3 fusion.24
  298.7 10.1 %shard_map.251 = f32[384,4096]{1,0:T(8,128)} custom-call(bf16[384,1024]{1,0:T(8,128)(2,1)S(1)} %fusion.12.x_ref, bf16[8,1024,512]{2,1,0:T(8,128)(2,1)} %bitcast.80), custom_call_target="tpu_custom_call" | custom-call | flops 3221225472 | bytes 12320768 | tf_op jit(solution)/shard_map/pallas_call | solution.py:812
  308.8 4.1 multiply_convert_fusion.x_ref
  312.9 7.4 %fusion.25 = (f32[384]{0:T(512)S(1)}, f32[384,1024]{1,0:T(8,128)S(1)}) fusion(f32[1024]{0:T(1024)S(1)} %copy-done.56, bf16[384,4096]{1,0:T(8,128)(2,1)S(1)} %multiply_convert_fusion.x_ref, bf16[4096,1024]{1,0:T(8,128)(2,1)} %all-gather.5.cloned.1.call-done, f32[1024]{0:T(1024)S(1)} %bitcast.110, f32[1024]{0:T(1024)S(1)} %bitcast.97, f32[384]{0:T(512)S(1)} %fusion.14, ...), kind=kOutput, calls=%fused_computation.93 | convolution fusion | flops 3224370688 | bytes 14696960 | tf_op jit(solution)/shard_map/dot_general | solution.py:997
  322.1 1.6 fusion.19
  323.8 1.3 copy-done.32
  325.2 9.6 %convert_reduce_fusion = (f32[4096]{0:T(1024)S(1)}, bf16[384,4096]{1,0:T(8,128)(2,1)S(1)}) fusion(f32[384,4096]{1,0:T(8,128)S(1)} %copy-done.32, f32[4096]{0:T(1024)S(1)} %bitcast.95, bf16[384,1024]{1,0:T(8,128)(2,1)S(1)} %add_convert_fusion.3.y_ref, bf16[4096,1024]{1,0:T(8,128)(2,1)} %all-gather.5.cloned.1.call-done), kind=kOutput, calls=%fused_computation.9 | convolution fusion | flops 3257397248 | bytes 18644992 | tf_op jit(solution)/shard_map/dot_general | solution.py:1061
  334.8 9.1 %shard_map.252 = f32[384,1024]{1,0:T(8,128)S(1)} custom-call(bf16[384,4096]{1,0:T(8,128)(2,1)S(1)} %get-tuple-element.98.refs_0_, bf16[8,1024,512]{2,1,0:T(8,128)(2,1)} %bitcast.81), custom_call_target="tpu_custom_call" | custom-call | flops 3221225472 | bytes 13107200 | tf_op jit(solution)/shard_map/pallas_call | solution.py:847
  345.6 2.0 copy-done.55
  347.5 1.9 convolution_convert_fusion.1.grad_ref
  349.4 3.0 shard_map.257.refs_0_
  352.4 1.3 copy-done.2
  353.7 7.9 %shard_map.253.refs_0_ = bf16[2,4,4096,128]{3,2,1,0:T(8,128)(2,1)} custom-call(bf16[384,4096]{1,0:T(8,128)(2,1)S(1)} %multiply_convert_fusion.x_ref, bf16[384,1024]{1,0:T(8,128)(2,1)S(1)} %add_convert_fusion.3.y_ref), custom_call_target="tpu_custom_call" | custom-call | flops 3221225472 | bytes 12320768 | tf_op jit(solution)/shard_map/pallas_call | solution.py:930
  361.6 8.0 %shard_map.254.refs_1_ = bf16[2,4,4096,128]{3,2,1,0:T(8,128)(2,1)} custom-call(bf16[384,1024]{1,0:T(8,128)(2,1)S(1)} %copy-done.10, bf16[384,4096]{1,0:T(8,128)(2,1)S(1)} %get-tuple-element.98.refs_0_), custom_call_target="tpu_custom_call" | custom-call | flops 3221225472 | bytes 12320768 | tf_op jit(solution)/shard_map/pallas_call | solution.py:886
  369.7 128.3 %shard_map.255 = (bf16[384,1024]{1,0:T(8,128)(2,1)}, bf16[384,1024]{1,0:T(8,128)(2,1)}, bf16[384,1024]{1,0:T(8,128)(2,1)}, bf16[4096,128]{1,0:T(8,128)(2,1)}, bf16[4096,128]{1,0:T(8,128)(2,1)}) custom-call(bf16[384,1024]{1,0:T(8,128)(2,1)} %convolution_convert_fusion.1.grad_ref, bf16[3,1024,128]{2,1,0:T(8,128)(2,1)} %get-tuple-element.64.q, ...), custom_call_target="tpu_custom_call" | custom-call | tf_op jit(solution)/shard_map/pallas_call | solution.py:645
  499.2 4.3 shard_map.256
  505.1 1.4 copy-done.53
  506.5 1.9 convolution_convert_fusion.grad_ref
  508.4 3.0 shard_map.260.refs_3_
  511.3 1.4 copy-done.3
  512.7 3.6 shard_map.258.refs_1_
  516.3 1.3 copy-done.4
  517.7 6.0 shard_map.263
  523.7 5.9 shard_map.259.refs_2_
  529.6 102.6 %shard_map.261 = (bf16[384,1024]{1,0:T(8,128)(2,1)}, bf16[384,1024]{1,0:T(8,128)(2,1)}, bf16[384,1024]{1,0:T(8,128)(2,1)}, bf16[1024,128]{1,0:T(8,128)(2,1)}, bf...) custom-call(bf16[384,1024]{1,0:T(8,128)(2,1)} %convolution_convert_fusion.grad_ref, ...), custom_call_target="tpu_custom_call" | custom-call | tf_op jit(solution)/shard_map/pallas_call | solution.py:645
  633.3 1.1 copy-done.16
  634.4 1.1 copy-done.17
  635.6 8.9 %shard_map.262 = f32[384,1024]{1,0:T(8,128)S(1)} custom-call(bf16[384,1024]{1,0:T(8,128)(2,1)S(1)} %copy-done.14, bf16[384,1024]{1,0:T(8,128)(2,1)S(1)} %copy-done.16, bf16[384,1024]{1,0:T(8,128)(2,1)S(1)} %copy-done.17, bf16[8,1024,384]{2,1,0:T(8,128)(2,1)} %get-tuple-element.51.w_ref.refs_3_), custom_call_target="tpu_custom_call" | custom-call | flops 2415919104 | bytes 10223616 | tf_op jit(solution)/shard_map/pallas_call | solution.py:847
  644.5 7.7 %shard_map.264.refs_0_ = bf16[2,4,3072,128]{3,2,1,0:T(8,128)(2,1)} custom-call(bf16[384,1024]{1,0:T(8,128)(2,1)S(1)} %copy-done.24, bf16[384,1024]{1,0:T(8,128)(2,1)S(1)} %copy-done.15, bf16[384,1024]{1,0:T(8,128)(2,1)S(1)} %copy-done.16, bf16[384,1024]{1,0:T(8,128)(2,1)S(1)} %copy-done.17), custom_call_target="tpu_custom_call" | custom-call | flops 2415919104 | bytes 9437184 | tf_op jit(solution)/shard_map/pallas_call | solution.py:886
  652.9 49.9 %shard_map.265 = (bf16[3072,128]{1,0:T(8,128)(2,1)}, f32[88,128]{1,0:T(8,128)}) custom-call(bf16[2,4,3072,128]{3,2,1,0:T(8,128)(2,1)} %shard_map.264.refs_0_, f32[88,128]{1,0:T(8,128)} %bitcast.104), custom_call_target="tpu_custom_call" | custom-call | tf_op jit(solution)/shard_map/pallas_call | solution.py:645
  702.8 1.3 slice_bitcast_fusion
  704.8 1.6 copy_bitcast_fusion
  706.4 1.6 copy_bitcast_fusion.1
  708.0 1.4 multiply_add_fusion
  710.2 1.5 copy.55
  713.0 1.2 convert_bitcast_fusion.2
  715.3 1.3 dynamic_slice.11
  (157 shorter events, 22.5 us)
Async XLA Ops:
  7.2 1.2 copy-start
  7.2 3.7 copy-start.45
  7.2 4.6 copy-start.42
  7.2 291.5 %all-gather.3.cloned.1.call-start = ((), (), s32[]{:S(2)}) async-start(), calls=%async_computation | async-start | bytes 8650752 | tf_op jit(solution)/shard_map/all_gather | solution.py:958
  9.2 303.8 %all-gather.5.cloned.1.call-start = ((), (), s32[]{:S(2)}) async-start(), calls=%async_computation.1 | async-start | bytes 8650752 | tf_op jit(solution)/shard_map/all_gather | solution.py:958
  11.8 1.5 copy-start.52
  12.1 60.0 %copy-start.23 = (bf16[384,1024]{1,0:T(8,128)(2,1)S(1)}, bf16[384,1024]{1,0:T(8,128)(2,1)}, u32[]{:S(2)}) copy-start(bf16[384,1024]{1,0:T(8,128)(2,1)} %x_ref.7) | copy-start | bytes 2359300
  207.4 87.5 %copy-start.33 = (f32[384,1024]{1,0:T(8,128)}, f32[384,1024]{1,0:T(8,128)S(1)}, u32[]{:S(2)}) copy-start(f32[384,1024]{1,0:T(8,128)S(1)} %get-tuple-element.118) | copy-start | bytes 4718596
  207.8 2.2 copy-start.5
  208.5 4.5 copy-start.7
  209.9 3.2 copy-start.21
  213.1 6.8 copy-start.18
  221.7 73.2 %copy-start.54 = (bf16[8,128,1024]{2,1,0:T(8,128)(2,1)S(1)}, bf16[8,128,1024]{2,1,0:T(8,128)(2,1)}, u32[]{:S(2)}) copy-start(bf16[8,128,1024]{2,1,0:T(8,128)(2,1)} %get-tuple-element.62) | copy-start | bytes 6291460
  297.2 1.1 copy-start.35
  298.6 10.2 %copy-start.9 = (bf16[384,1024]{1,0:T(8,128)(2,1)}, bf16[384,1024]{1,0:T(8,128)(2,1)S(1)}, u32[]{:S(2)}) copy-start(bf16[384,1024]{1,0:T(8,128)(2,1)S(1)} %fusion.12.x_ref) | copy-start | bytes 2359300
  308.8 4.1 copy-start.56
  320.3 1.1 copy-start.39
  322.1 3.1 copy-start.32
  334.8 9.1 %copy-start.36 = (f32[384,1024]{1,0:T(8,128)S(1)}, f32[384,1024]{1,0:T(8,128)}, u32[]{:S(2)}) copy-start(f32[384,1024]{1,0:T(8,128)} %copy-done.35) | copy-start | bytes 4718596
  345.4 4.1 copy-start.37
  345.4 2.2 copy-start.55
  347.5 1.9 copy-start.26
  352.4 1.3 copy-start.2
  353.7 7.9 %copy-start.10 = (bf16[384,1024]{1,0:T(8,128)(2,1)S(1)}, bf16[384,1024]{1,0:T(8,128)(2,1)}, u32[]{:S(2)}) copy-start(bf16[384,1024]{1,0:T(8,128)(2,1)} %copy-done.9) | copy-start | bytes 2359300
  369.7 128.4 %copy-start.6 = (bf16[8,1024,128]{2,1,0:T(8,128)(2,1)S(1)}, bf16[8,1024,128]{2,1,0:T(8,128)(2,1)}, u32[]{:S(2)}) copy-start(bf16[8,1024,128]{2,1,0:T(8,128)(2,1)} %get-tuple-element.57.w_ref.refs_1_) | copy-start | bytes 6291460
  499.2 4.3 copy-start.34
  499.2 4.3 copy-start.38
  504.9 1.6 copy-start.53
  506.5 1.9 copy-start.25
  506.5 6.2 copy-start.20
  508.4 4.4 copy-start.8
  508.4 9.3 %copy-start.11 = (bf16[8,1024,256]{2,1,0:T(8,128)(2,1)S(1)}, bf16[8,1024,256]{2,1,0:T(8,128)(2,1)}, u32[]{:S(2)}) copy-start(bf16[8,1024,256]{2,1,0:T(8,128)(2,1)} %get-tuple-element.58.w_ref.refs_2_) | copy-start | bytes 12582916
  511.3 1.4 copy-start.3
  512.7 4.9 copy-start.12
  512.7 4.9 copy-start.13
  516.3 1.3 copy-start.4
  517.7 6.0 copy-start.22
  632.2 1.1 copy-start.14
  635.6 8.9 %copy-start.15 = (bf16[384,1024]{1,0:T(8,128)(2,1)S(1)}, bf16[384,1024]{1,0:T(8,128)(2,1)}, u32[]{:S(2)}) copy-start(bf16[384,1024]{1,0:T(8,128)(2,1)} %get-tuple-element.77.refs_0_) | copy-start | bytes 2359300
  635.6 8.9 %copy-start.24 = (bf16[384,1024]{1,0:T(8,128)(2,1)S(1)}, bf16[384,1024]{1,0:T(8,128)(2,1)}, u32[]{:S(2)}) copy-start(bf16[384,1024]{1,0:T(8,128)(2,1)} %x_ref.7) | copy-start | bytes 2359300
  652.9 51.9 %copy-start.41 = (bf16[4096,128]{1,0:T(8,128)(2,1)S(1)}, bf16[4096,128]{1,0:T(8,128)(2,1)}, u32[]{:S(2)}) copy-start(bf16[4096,128]{1,0:T(8,128)(2,1)} %get-tuple-element.87) | copy-start | bytes 3145732
  704.8 1.6 copy-start.40
  708.0 1.4 copy-start.46
  708.0 2.2 copy-start.44
  709.4 3.6 copy-start.43
  711.7 2.5 copy-start.47
  711.7 2.5 copy-start.48
  713.0 3.7 copy-start.1
  (11 other events, 9.9 us)
Sparse Core Ops, SparseCore 0:
  11.5 109.4 all-gather.2
  124.4 97.1 all-gather.4

commit v4 on v3

--- a/solution.py
+++ b/solution.py
@@ -265,13 +265,10 @@
     dq_ref[rows, :] = (jnp.transpose(jnp.concatenate(dqt, 0)) * 0.125).astype(jnp.bfloat16)
 
 
-def x_rows(half):
-    return min(int(half * 0.36 / 16 + 0.5) * 16, half // 32 * 16)
-
-
 class Gather:
-    def __init__(self, weights, t, size=1 << 17):
-        self.t, self.depth = t, t // 2
+    def __init__(self, weights, t, share, size=1 << 17):
+        self.t, self.depth, self.share = t, t // 2, share
+        self.ins, self.specs = list(weights), [ANY] * len(weights)
         self.shapes = [w.shape for w in weights]
         self.pieces = []
         for w, (r, c) in enumerate(self.shapes):
@@ -292,10 +289,14 @@
             dma((len(weights),)),
         ]
 
+    def x_rows(self, n):
+        half = self.pieces[n][2] // 2
+        return min(int(half * self.share / 16 + 0.5) * 16, half // 32 * 16)
+
     def rows_of(self, n, kind, core):
         _, at, rows = self.pieces[n]
         half = rows // 2
-        a = x_rows(half)
+        a = self.x_rows(n)
         start, xpos = at + core * half, self.place.xpos
         if kind == "plane":
             return pl.ds(at16(start + xpos * a), half - a)
@@ -309,7 +310,7 @@
         me, depth, t, pieces = place.me, self.depth, self.t, self.pieces
 
         def has_x(n):
-            return x_rows(pieces[n][2] // 2) > 0
+            return self.x_rows(n) > 0
 
         def rows_of(n, kind, core=place.core):
             return self.rows_of(n, kind, core)
@@ -410,50 +411,84 @@
         yield True
 
 
+class Weight:
+    def __init__(self, x, ys, by_cols, t):
+        self.arrays, self.by_cols = [x, *ys], by_cols
+        n, m = x.shape
+        wide = ys[0].shape[1]
+        if by_cols:
+            self.height, self.width = m, wide // t
+            self.rows = len(ys) * m * self.width // LANES
+        else:
+            self.height, self.width = m // t, wide
+            self.rows = m // t * wide // LANES
+
+    def term(self, xt, ys, at, half, t, which):
+        high = self.height
+        if self.by_cols and self.width < LANES:
+            panel, row = at // (high // 2), at % (high // 2) + which * half
+            y = ys[panel][:, rows_at(t // 2 * LANES, LANES)]
+            first, second = (dot(xt[rows_at(r, half), :], y, NN) for r in (row, row + high // 2))
+            odd = t % 2 == 1
+            first = jnp.where(odd, pltpu.roll(first, DH, 1), first)
+            second = jnp.where(odd, second, pltpu.roll(second, DH, 1))
+            return [jnp.where(lane_half(first.shape, 0), first, second)]
+        if self.by_cols:
+            panel, row = at // high, at % high
+            per = self.width // LANES
+            y, col = ys[panel // per], t * self.width + panel % per * LANES
+            return [dot(xt[rows_at(row + which * half, half), :], y[:, rows_at(col, LANES)], NN)]
+        panels = half // high
+        cols = rows_at((at // high + which * panels) * LANES, panels * LANES)
+        out = dot(xt[rows_at(t * high, high), :], ys[0][:, cols], NN)
+        return [out[:, i * LANES : i * LANES + LANES] for i in range(panels)]
+
+
 class Reduce:
-    def __init__(self, grads, t, size):
-        self.t, self.depth, self.size = t, t // 2, size
-        self.pieces = [(w, at) for w, g in enumerate(grads) for at in range(0, g.shape[2], size)]
+    def __init__(self, weights, t, size, y_first):
+        self.t, self.depth, self.size, self.weights = t, t // 2, size, weights
+        self.y_rows = int(size // 2 * y_first) // 32 * 32
+        self.ins = [a for w in weights for a in w.arrays]
+        self.specs = [VMEM] * len(self.ins)
+        self.pieces = [(w, at) for w, g in enumerate(weights) for at in range(0, g.rows, size)]
         m, depth, dma = len(self.pieces), self.depth, pltpu.SemaphoreType.DMA
-        H, Hy, Q = size // 2, size // 4, size // 8
+        H, Hy, Q = size // 2, self.y_rows, (size // 2 - self.y_rows) // 2
 
         def buf(*shape):
-            return pltpu.VMEM((m,) + shape + (LANES,), jnp.bfloat16)
-
-        self.out_shape = [jax.ShapeDtypeStruct(g.shape[2:], jnp.bfloat16) for g in grads]
+            return pltpu.VMEM(shape + (LANES,), jnp.bfloat16)
+
+        self.out_shape = [jax.ShapeDtypeStruct((g.rows, LANES), jnp.bfloat16) for g in weights]
         self.scratch = [
-            buf(2, depth, H),
-            buf(2, depth, H),
-            buf(depth, Hy),
-            buf(2, depth, Q),
-            buf(depth - 1, Hy),
-            buf(depth, Q),
-            buf(Hy),
-            buf(Hy),
-            buf(depth - 1, Q),
-            buf(size),
+            buf(2, 2, depth, H),
+            buf(2, 2, depth, H),
+            buf(m, 2, depth, H),
+            buf(m, depth, Hy),
+            buf(m, 2, depth, Q),
+            buf(m, depth - 1, Hy),
+            buf(m, depth, Q),
+            buf(m, Hy),
+            buf(m, Hy),
+            buf(m, depth - 1, Q),
+            buf(m, size),
             dma((m, 5 + 2 * depth)),
             dma((m, 5 + 2 * depth)),
             dma((m,)),
-            dma((m,)),
-        ]
+        ] + [pltpu.VMEM(w.arrays[0].shape[::-1], jnp.bfloat16) for w in weights]
 
     def steps(self, place, ins, outs, scratch):
-        own, r1, r2y, r2x, r3y, r3x, s3y, r4y, r4x, fin, send, recv, local, store = scratch
-        size, depth, pieces = self.size, self.depth, self.pieces
-        H, Hy, Q = size // 2, size // 4, size // 8
+        away, own, r1, r2y, r2x, r3y, r3x, s3y, r4y, r4x, fin, send, recv, store = scratch[:14]
+        size, depth, pieces, t = self.size, self.depth, self.pieces, self.t
+        H, Hy, Q = size // 2, self.y_rows, (size // 2 - self.y_rows) // 2
         core, xpos, line, side = place.core, place.xpos, place.line, place.side
+        turned, ins, arrays = scratch[14:], list(ins), []
+        for w in self.weights:
+            arrays.append([ins.pop(0) for _ in w.arrays])
 
         def move(src, dst, n, k, device):
             return remote(src, dst, send.at[n, k], recv.at[n, k], device)
 
-        def load(n):
-            w, at = pieces[n]
-            return pltpu.make_async_copy(ins[w].at[:, :, pl.ds(at16(at + core * H), H), :], own.at[n], local.at[n])
-
         def copy_core(n):
-            w, at = pieces[n]
-            return move(ins[w].at[:, :, pl.ds(at16(at + (1 - core) * H), H), :], r1.at[n], n, 0, place.sibling)
+            return move(away.at[n % 2], r1.at[n], n, 0, place.sibling)
 
         def copy_y(n):
             return move(r1.at[n, 1 - side, :, pl.ds(0, Hy), :], r2y.at[n], n, 1, place.y_mate)
@@ -485,33 +520,47 @@
             w, at = pieces[n]
             return pltpu.make_async_copy(fin.at[n], outs[w].at[pl.ds(at, size), :], store.at[n])
 
-        total = len(pieces)
-        for n in range(total):
-            load(n).start()
-            copy_core(n).start()
-        yield True
+        def make(n):
+            w, at = pieces[n]
+            weight, (x, *ys) = self.weights[w], arrays[w]
+            if n == 0 or pieces[n - 1][0] != w:
+                turned[w][...] = jnp.transpose(x[...])
+            if n >= 2:
+                copy_core(n - 2).wait_send()
+            for which, into in ((1 - core, away), (core, own)):
+
+                def block(i):
+                    parts = weight.term(turned[w], ys, at, H, i, which)
+                    high = parts[0].shape[0]
+                    for j, part in enumerate(parts):
+                        into[n % 2, i % 2, i // 2, j * high : j * high + high, :] = part.astype(jnp.bfloat16)
+
+                loop(0, t, block)
+                if into is away:
+                    copy_core(n).start()
 
         def stage0(n):
-            load(n).wait()
             copy_core(n).wait_recv()
 
             def add(i):
                 a, b = i // depth, i % depth
-                r1[n, a, b] = r1[n, a, b] + own[n, a, b]
+                r1[n, a, b] = r1[n, a, b] + own[n % 2, a, b]
 
             loop(0, 2 * depth, add)
-            copy_y(n).start()
+            if Hy:
+                copy_y(n).start()
             copy_x(n).start()
 
         def stage1(n):
-            copy_y(n).wait_recv()
-
-            def add(i):
-                r2y[n, i] = r2y[n, i] + r1[n, side, i, 0:Hy, :]
-
-            loop(0, depth, add)
-            for i in range(1, depth):
-                copy_yz(n, i).start()
+            if Hy:
+                copy_y(n).wait_recv()
+
+                def add(i):
+                    r2y[n, i] = r2y[n, i] + r1[n, side, i, 0:Hy, :]
+
+                loop(0, depth, add)
+                for i in range(1, depth):
+                    copy_yz(n, i).start()
             copy_x(n).wait_recv()
 
             def addx(i):
@@ -530,13 +579,14 @@
             loop(0, depth, add)
             for i in range(1, depth):
                 copy_xz(n, i).start()
-            for i in range(1, depth):
-                copy_yz(n, i).wait_recv()
-            part = r2y[n, line].astype(jnp.float32)
-            for i in range(1, depth):
-                part = part + r3y[n, i - 1].astype(jnp.float32)
-            s3y[n] = part.astype(jnp.bfloat16)
-            copy_yx(n).start()
+            if Hy:
+                for i in range(1, depth):
+                    copy_yz(n, i).wait_recv()
+                part = r2y[n, line].astype(jnp.float32)
+                for i in range(1, depth):
+                    part = part + r3y[n, i - 1].astype(jnp.float32)
+                s3y[n] = part.astype(jnp.bfloat16)
+                copy_yx(n).start()
 
         def stage3(n):
             for i in range(1, depth):
@@ -546,8 +596,9 @@
                 part = part + r4x[n, i - 1].astype(jnp.float32)
             fin[n, pl.ds(at16(core * H + Hy + xpos * Q), Q), :] = part.astype(jnp.bfloat16)
             copy_xx(n).start()
-            copy_yx(n).wait_recv()
-            fin[n, pl.ds(at16(core * H), Hy), :] = s3y[n] + r4y[n]
+            if Hy:
+                copy_yx(n).wait_recv()
+                fin[n, pl.ds(at16(core * H), Hy), :] = s3y[n] + r4y[n]
 
         def stage4(n):
             copy_xx(n).wait_recv()
@@ -557,24 +608,72 @@
             copy_back(n).wait_recv()
             write(n).start()
 
+        total = len(pieces)
+        make(0)
+        yield True
         stages = [stage0, stage1, stage2, stage3, stage4, stage5]
         for step in range(total + len(stages) - 1):
             for k in range(len(stages) - 1, -1, -1):
                 if 0 <= step - k < total:
                     stages[k](step - k)
+            if step + 1 < total:
+                make(step + 1)
             yield True
         for n in range(total):
-            copy_core(n).wait_send()
-            copy_y(n).wait_send()
+            if n >= total - 2:
+                copy_core(n).wait_send()
             copy_x(n).wait_send()
             copy_xy(n).wait_send()
-            copy_yx(n).wait_send()
             copy_xx(n).wait_send()
             copy_back(n).wait_send()
             for i in range(1, depth):
-                copy_yz(n, i).wait_send()
                 copy_xz(n, i).wait_send()
+            if Hy:
+                copy_y(n).wait_send()
+                copy_yx(n).wait_send()
+                for i in range(1, depth):
+                    copy_yz(n, i).wait_send()
             write(n).wait()
+        yield True
+
+
+class Back:
+    def __init__(self, ys, weight, rest=None, factor=1.0):
+        self.count, self.has_rest, self.factor = len(ys), rest is not None, factor
+        self.ins = [*ys, weight] + ([rest] if self.has_rest else [])
+        self.specs = [VMEM] * self.count + [ANY] + [VMEM] * self.has_rest
+        n, (t, d, c) = ys[0].shape[0], weight.shape
+        self.blocks = t
+        self.out_shape = [jax.ShapeDtypeStruct((n, d), jnp.float32)]
+        self.scratch = [
+            pltpu.VMEM((2, d, c), jnp.bfloat16),
+            pltpu.VMEM((n, d), jnp.float32),
+            pltpu.SemaphoreType.DMA((3,)),
+        ]
+
+    def steps(self, place, ins, outs, scratch):
+        held, total, sem = scratch
+        ys, weight = ins[: self.count], ins[self.count]
+        width = held.shape[2] // self.count
+
+        def load(i):
+            return pltpu.make_async_copy(weight.at[i], held.at[i % 2], sem.at[i % 2])
+
+        load(0).start()
+        for i in range(self.blocks):
+            load(i).wait()
+            if i + 1 < self.blocks:
+                load(i + 1).start()
+            y = [y_ref[:, i * width : i * width + width] for y_ref in ys]
+            term = dot(jnp.concatenate(y, 1) if len(y) > 1 else y[0], held[i % 2], NT)
+            if i:
+                total[...] += term
+            else:
+                total[...] = term + self.factor * ins[-1][...] if self.has_rest else term
+            yield True
+        out = pltpu.make_async_copy(total, outs[0], sem.at[2])
+        out.start()
+        out.wait()
         yield True
 
 
@@ -582,6 +681,7 @@
     def __init__(self, value, t):
         self.depth = t // 2
         rows, dma = value.shape[0], pltpu.SemaphoreType.DMA
+        self.ins, self.specs = [value], [ANY]
         self.out_shape = [jax.ShapeDtypeStruct(value.shape, jnp.float32)]
         self.scratch = [
             pltpu.VMEM((self.depth, rows, LANES), jnp.float32),
@@ -631,7 +731,7 @@
 
 
 class Nothing:
-    out_shape, scratch = [], []
+    ins, specs, out_shape, scratch = [], [], [], []
 
     def steps(self, place, ins, outs, scratch):
         yield from ()
@@ -652,8 +752,9 @@
     )(*ins)
 
 
-def jobs_kernel(jobs, groups, t, cid):
-    counts = [len(g) for g in groups]
+def jobs_kernel(jobs, t, cid):
+    counts = [len(j.ins) for j in jobs]
+    gives = [len(j.out_shape) for j in jobs]
     sizes = [len(j.scratch) for j in jobs]
 
     def body(*refs):
@@ -661,36 +762,35 @@
         place.greet()
         refs = list(refs)
         ins = [[refs.pop(0) for _ in range(c)] for c in counts]
-        outs = [[refs.pop(0) for _ in range(c)] for c in counts]
+        outs = [[refs.pop(0) for _ in range(c)] for c in gives]
         scratch = [[refs.pop(0) for _ in range(c)] for c in sizes]
         running = [j.steps(place, i, o, s) for j, i, o, s in zip(jobs, ins, outs, scratch)]
         while running:
             running = [g for g in running if next(g, None) is not None]
 
-    total = sum(counts)
     return communicate(
         body,
         [s for j in jobs for s in j.out_shape],
-        [a for g in groups for a in g],
-        [ANY] * total,
-        [ANY] * total,
+        [a for j in jobs for a in j.ins],
+        [a for j in jobs for a in j.specs],
+        [ANY] * sum(gives),
         [s for j in jobs for s in j.scratch],
         cid,
     )
 
 
-def attend(tokens_qkv, t, causal, bq, job, job_ins, lead, each, cid):
+def attend(tokens_qkv, t, causal, bq, job, lead, each, cid):
     n, d = tokens_qkv[0].shape
     slots = Slots(t, n, d)
     pairs = slots.pairs
     held = jax.ShapeDtypeStruct((pairs, LEN, LANES), jnp.bfloat16)
-    extra = len(job_ins)
+    extra, gives = len(job.ins), len(job.out_shape)
 
     def body(*refs):
         qkv, refs = refs[:3], refs[3:]
         job_refs, refs = refs[:extra], refs[extra:]
         out, saved, lse, refs = refs[0], refs[1:5], refs[5], refs[6:]
-        job_outs, refs = refs[:extra], refs[extra:]
+        job_outs, refs = refs[:gives], refs[gives:]
         here, (hs, hr, ts, tr, keep), refs = refs[:4], refs[4:9], refs[9:]
         place = Place(t)
         place.greet()
@@ -723,9 +823,9 @@
         + [held] * 4
         + [jax.ShapeDtypeStruct((pairs, 8, LEN), jnp.float32)]
         + job.out_shape,
-        [*tokens_qkv, *job_ins],
-        [ANY] * (3 + extra),
-        [ANY] * 5 + [VMEM] + [ANY] * extra,
+        [*tokens_qkv, *job.ins],
+        [ANY] * 3 + job.specs,
+        [ANY] * 5 + [VMEM] + [ANY] * gives,
         [pltpu.VMEM(held.shape, held.dtype)] * 4
         + reshard_sems(slots, 3, 1)
         + [pltpu.SemaphoreType.DMA((4,))]
@@ -735,17 +835,17 @@
     return out[0], out[1:6], out[6:]
 
 
-def attend_back(grad, saved, t, causal, bq, job, job_ins, lead, every, cid):
+def attend_back(grad, saved, t, causal, bq, job, lead, every, cid):
     n, d = grad.shape
     slots = Slots(t, n, d)
     pairs = slots.pairs
     held = pltpu.VMEM((pairs, LEN, LANES), jnp.bfloat16)
-    extra = len(job_ins)
+    extra, gives = len(job.ins), len(job.out_shape)
 
     def body(grad_ref, q, k, v, o, lse, *refs):
         job_refs, refs = refs[:extra], refs[extra:]
         outs, refs = refs[:3], refs[3:]
-        job_outs, refs = refs[:extra], refs[extra:]
+        job_outs, refs = refs[:gives], refs[gives:]
         (do, *made, kt, dk, dv, hs, hr, ts, tr), refs = refs[:11], refs[11:]
         place = Place(t)
         place.greet()
@@ -785,9 +885,9 @@
     out = communicate(
         body,
         [jax.ShapeDtypeStruct((n, d), jnp.bfloat16)] * 3 + job.out_shape,
-        [grad, *saved, *job_ins],
-        [ANY] + [VMEM] * 5 + [ANY] * extra,
-        [ANY] * (3 + extra),
+        [grad, *saved, *job.ins],
+        [ANY] + [VMEM] * 5 + job.specs,
+        [ANY] * (3 + gives),
         [held] * 4
         + [pltpu.VMEM((LANES, LEN), jnp.bfloat16)]
         + [pltpu.VMEM((LEN, LANES), jnp.float32)] * 2
@@ -858,59 +958,106 @@
     )(*ys, weight)
 
 
-def by_side(grad, t):
-    return jnp.swapaxes(grad.reshape(t // 2, 2, *grad.shape[1:]), 0, 1)
-
-
-def cols_grad_kernel(count, x_ref, *refs):
-    ys, o_ref, xt_ref = refs[:count], refs[count], refs[count + 1]
+def forward_kernel(x_ref, w_ref, b_ref, v_ref, act_ref, slope_ref, o_ref):
+    v = dot(x_ref[...], w_ref[0], NN) + b_ref[...].astype(jnp.float32)
+    square = v * v
+    th = jnp.tanh(math.sqrt(2 / math.pi) * v * (1 + 0.044715 * square))
+    half = 0.5 * (1 + th)
+    act = (v * half).astype(jnp.bfloat16)
+    act_ref[...] = act
+    inner = math.sqrt(2 / math.pi) * (1 + 3 * 0.044715 * square)
+    slope_ref[...] = (half + 0.5 * v * (1 - th * th) * inner).astype(jnp.bfloat16)
+    term = dot(act, v_ref[0], NN)
 
     @pl.when(pl.program_id(0) == 0)
     def _():
-        xt_ref[...] = jnp.transpose(x_ref[...])
-
-    y = jnp.concatenate([y_ref[...] for y_ref in ys], 1) if count > 1 else ys[0][...]
-    out = dot(xt_ref[...], y, NN).astype(o_ref.dtype)
-    d = out.shape[0]
-    for j in range(out.shape[1] // LANES):
-        o_ref[0, 0, j * d : j * d + d, :] = out[:, j * LANES : j * LANES + LANES]
-
-
-def cols_grad(x, ys, t):
-    count = len(ys)
+        o_ref[...] = term
+
+    @pl.when(pl.program_id(0) != 0)
+    def _():
+        o_ref[...] += term
+
+
+def forward_hidden(x, w_hid, bias, w_out):
     n, d = x.shape
-    blocks = min(t, ys[0].shape[1] // LANES)
-    width = ys[0].shape[1] // blocks
-    c = width * count
-    whole = blocks == t
-    out = pl.pallas_call(
-        functools.partial(cols_grad_kernel, count),
-        grid=(blocks,),
-        out_shape=jax.ShapeDtypeStruct(
-            (2, t // 2, c // LANES * d, LANES) if whole else (blocks, 1, c // LANES * d, LANES), jnp.bfloat16
-        ),
-        in_specs=[pl.BlockSpec((n, d), lambda i: (0, 0))]
-        + [pl.BlockSpec((n, width), lambda i: (0, i))] * count,
-        out_specs=pl.BlockSpec(
-            (1, 1, c // LANES * d, LANES), (lambda i: (i % 2, i // 2, 0, 0)) if whole else (lambda i: (i, 0, 0, 0))
-        ),
-        scratch_shapes=[pltpu.VMEM((d, n), jnp.bfloat16)],
+    t, _, c = w_hid.shape
+    low = jax.ShapeDtypeStruct((n, t * c), jnp.bfloat16)
+    part = pl.BlockSpec((n, c), lambda i: (0, i))
+    whole = pl.BlockSpec((n, d), lambda i: (0, 0))
+    return pl.pallas_call(
+        forward_kernel,
+        grid=(t,),
+        out_shape=[low, low, jax.ShapeDtypeStruct((n, d), jnp.float32)],
+        in_specs=[
+            whole,
+            pl.BlockSpec((1, d, c), lambda i: (i, 0, 0)),
+            pl.BlockSpec((1, c), lambda i: (0, i)),
+            pl.BlockSpec((1, c, d), lambda i: (i, 0, 0)),
+        ],
+        out_specs=[part, part, whole],
         compiler_params=pltpu.CompilerParams(vmem_limit_bytes=48 << 20),
         cost_estimate=pl.CostEstimate(
-            flops=2 * n * d * blocks * c, bytes_accessed=2 * (blocks * d * c + n * d + n * blocks * c), transcendentals=0
+            flops=4 * n * d * t * c, bytes_accessed=4 * t * d * c + 4 * n * t * c, transcendentals=n * t * c
         ),
-    )(x, *ys)
-    if whole:
-        return out
-    m = t // blocks
-    parts = out.reshape(blocks, count, d, m, LANES // m).transpose(0, 3, 1, 2, 4)
-    return by_side(parts.reshape(t, count * d // m, LANES), t)
+    )(x, w_hid, bias, w_out)
+
+
+def backward_kernel(g_ref, v_ref, slope_ref, w_ref, gh_ref, sum_ref, o_ref):
+    grad = dot(g_ref[...], v_ref[0], NT) * slope_ref[...].astype(jnp.float32)
+    grad = grad.astype(jnp.bfloat16)
+    gh_ref[...] = grad
+    sum_ref[...] = jnp.sum(grad.astype(jnp.float32), axis=0, keepdims=True)
+    term = dot(grad, w_ref[0], NT)
+
+    @pl.when(pl.program_id(0) == 0)
+    def _():
+        o_ref[...] = term
+
+    @pl.when(pl.program_id(0) != 0)
+    def _():
+        o_ref[...] += term
+
+
+def backward_hidden(grad, w_out, slopes, w_hid):
+    n, d = grad.shape
+    t, _, c = w_hid.shape
+    part = pl.BlockSpec((n, c), lambda i: (0, i))
+    whole = pl.BlockSpec((n, d), lambda i: (0, 0))
+    return pl.pallas_call(
+        backward_kernel,
+        grid=(t,),
+        out_shape=[
+            jax.ShapeDtypeStruct((n, t * c), jnp.bfloat16),
+            jax.ShapeDtypeStruct((1, t * c), jnp.float32),
+            jax.ShapeDtypeStruct((n, d), jnp.float32),
+        ],
+        in_specs=[
+            whole,
+            pl.BlockSpec((1, c, d), lambda i: (i, 0, 0)),
+            part,
+            pl.BlockSpec((1, d, c), lambda i: (i, 0, 0)),
+        ],
+        out_specs=[part, pl.BlockSpec((1, c), lambda i: (0, i)), whole],
+        compiler_params=pltpu.CompilerParams(vmem_limit_bytes=48 << 20),
+        cost_estimate=pl.CostEstimate(
+            flops=4 * n * d * t * c, bytes_accessed=4 * t * d * c + 4 * n * t * c, transcendentals=0
+        ),
+    )(grad, w_out, slopes, w_hid)
+
+
+def cols_weight(x, ys, t):
+    return Weight(x, ys, True, t)
+
+
+def rows_weight(x, y, t):
+    return Weight(x, [y], False, t)
 
 
 def cols_result(total, count, d, width):
     total = total.astype(jnp.float32)
     if width < LANES:
-        return total.reshape(count, d, width).transpose(1, 0, 2).reshape(d, count * width)
+        parts = total.reshape(count, d // 2, 2, width).transpose(2, 1, 0, 3)
+        return parts.reshape(d, count * width)
     return total.reshape(-1, d, LANES).transpose(1, 0, 2).reshape(d, count * width)
 
 
@@ -1017,19 +1164,17 @@
     t = lax.axis_size("tensor")
     n, d = tokens.shape
     size = LEN * 8 // t
-    w_hid = gather_weight(hidden_weight)
-    w_out = gather_weight(output_weight).reshape(-1, d)
     units = hidden_bias.shape[0]
     bias_block = jnp.pad(hidden_bias, (0, 64 * LANES - units)).reshape(64, LANES)
     first = [self_qkv.reshape(d, -1), bias_block]
-    w_qkv, bias_all = jobs_kernel([Gather(first, t)], [first], t, 0)
+    w_qkv, bias_all = jobs_kernel([Gather(first, t, 0.36)], t, 0)
     w_qkv = widen(w_qkv, 3)
-    bias_all = bias_all.reshape(t, -1)[:, :units].reshape(-1)
+    bias_all = bias_all.reshape(t, -1)[:, :units].reshape(1, -1)
 
     qkv = cols_product(tokens, w_qkv, 3)
     second = [self_out, cross_q, cross_kv.reshape(d, -1), cross_out]
     self_heads, self_saved, (w_so, w_cq, w_kv, w_co) = attend(
-        qkv, t, True, 512, Gather(second, t), second, 4, 1, 1
+        qkv, t, True, 512, Gather(second, t, 0.36), 4, 1, 1
     )
     w_cq, w_kv = widen(w_cq, 1), widen(w_kv, 2)
     w_so, w_co = w_so.reshape(d, d), w_co.reshape(d, d)
@@ -1040,54 +1185,61 @@
     normed_one_low = normed_one.astype(low)
     kv = cols_product(memory, w_kv, 2)
     cq = cols_product(normed_one_low, w_cq, 1)
-    cross_heads, cross_saved, _ = attend([*cq, *kv], t, False, 512, Nothing(), [], 0, 0, 2)
+    third = [hidden_weight, output_weight]
+    cross_heads, cross_saved, (w_hid, w_out) = attend([*cq, *kv], t, False, 512, Gather(third, t, 0.36), 4, 1, 2)
     branch_two = product(cross_heads, w_co)
     normed_two, pull_two = jax.vjp(
         normalize, residual_alpha * normed_one + branch_two, norm_gain[1], norm_shift[1]
     )
     normed_two_low = normed_two.astype(low)
-    (hidden_low,) = cols_product(normed_two_low, w_hid, 1, jnp.float32)
-    hidden_pre = hidden_low + bias_all
-    activated, gelu_pull = jax.vjp(gelu_tanh, hidden_pre)
-    activated_low = activated.astype(low)
-    branch_three = product(activated_low, w_out)
+    activated, slopes, branch_three = forward_hidden(normed_two_low, w_hid, bias_all, w_out)
     layer_out, pull_three = jax.vjp(
         normalize, residual_alpha * normed_two + branch_three + output_bias, norm_gain[2], norm_shift[2]
     )
     grad_three, gain_three, shift_three = pull_three(grad_output.astype(jnp.float32))
     bias_out_grad = jnp.sum(grad_three, axis=0)
     grad_three_low = grad_three.astype(low)
-    out_weight_part = rows_grad(activated_low, grad_three_low, t)
-    grad_act = lax.dot_general(grad_three_low, w_out, NT, preferred_element_type=jnp.float32)
-    grad_hidden = gelu_pull(grad_act)[0].astype(low)
-    hidden_bias_grad = jnp.sum(grad_hidden, axis=0, dtype=jnp.float32)
-    hidden_weight_part = cols_grad(normed_two_low, [grad_hidden], t)
+    grad_hidden, hidden_bias_grad, grad_normed = backward_hidden(grad_three_low, w_out, slopes, w_hid)
     grad_two, gain_two, shift_two = pull_two(
-        residual_alpha * grad_three + back_product([grad_hidden], w_hid)
+        residual_alpha * grad_three + grad_normed
     )
     grad_two_low = grad_two.astype(low)
-    cross_out_part = rows_grad(cross_heads, grad_two_low, t)
     grad_co = lax.dot_general(grad_two_low, w_co, NT, preferred_element_type=jnp.float32).astype(low)
-    ff_parts = [out_weight_part, hidden_weight_part]
+    reduce_ff = Reduce(
+        [rows_weight(activated, grad_three_low, t), cols_weight(normed_two_low, [grad_hidden], t)], t, size, 0.25
+    )
     (g_cq, g_ck, g_cv), (out_weight_grad, hidden_weight_grad) = attend_back(
-        grad_co, cross_saved, t, False, 256, Reduce(ff_parts, t, size), ff_parts, 2, 2, 3
-    )
-    cross_q_part = cols_grad(normed_one_low, [g_cq], t)
-    cross_kv_part = cols_grad(memory, [g_ck, g_cv], t)
+        grad_co, cross_saved, t, False, 256, reduce_ff, 2, 2, 3
+    )
     grad_one, gain_one, shift_one = pull_one(residual_alpha * grad_two + back_product([g_cq], w_cq))
     grad_one_low = grad_one.astype(low)
-    self_out_part = rows_grad(self_heads, grad_one_low, t)
     grad_so = lax.dot_general(grad_one_low, w_so, NT, preferred_element_type=jnp.float32).astype(low)
-    parts = [cross_out_part, cross_q_part, cross_kv_part, self_out_part]
+    reduce_cross = Reduce(
+        [
+            rows_weight(cross_heads, grad_two_low, t),
+            cols_weight(normed_one_low, [g_cq], t),
+            cols_weight(memory, [g_ck, g_cv], t),
+            rows_weight(self_heads, grad_one_low, t),
+        ],
+        t,
+        size,
+        0.25,
+    )
     g_qkv, (cross_out_grad, cross_q_grad, cross_kv_grad, self_out_grad) = attend_back(
-        grad_so, self_saved, t, True, 256, Reduce(parts, t, size), parts, 2, 2, 4
-    )
-    self_qkv_part = cols_grad(tokens, g_qkv, t)
+        grad_so, self_saved, t, True, 256, reduce_cross, 2, 2, 4
+    )
     small = jnp.concatenate(
-        [gain_one, gain_two, gain_three, shift_one, shift_two, shift_three, bias_out_grad, hidden_bias_grad]
+        [gain_one, gain_two, gain_three, shift_one, shift_two, shift_three, bias_out_grad, hidden_bias_grad[0]]
     ).reshape(-1, LANES)
-    self_qkv_grad, small = jobs_kernel(
-        [Reduce([self_qkv_part], t, size), Total(small, t)], [[self_qkv_part], [small]], t, 5
+    self_qkv_grad, small, grad_tokens, grad_memory = jobs_kernel(
+        [
+            Reduce([cols_weight(tokens, g_qkv, t)], t, size, 0.5),
+            Total(small, t),
+            Back(g_qkv, w_qkv, grad_one, residual_alpha),
+            Back([g_ck, g_cv], w_kv),
+        ],
+        t,
+        5,
     )
     small = settle(small).reshape(-1)
     gain_total, shift_total = small[: 3 * d].reshape(3, d), small[3 * d : 6 * d].reshape(3, d)
@@ -1100,8 +1252,6 @@
     cross_kv_grad = cols_result(settle(cross_kv_grad), 2, d, cross_kv.shape[2]).reshape(cross_kv.shape)
     self_out_grad = rows_result(settle(self_out_grad), self_out.shape[0], d)
     self_qkv_grad = cols_result(settle(self_qkv_grad), 3, d, self_qkv.shape[2]).reshape(self_qkv.shape)
-    grad_memory = back_product([g_ck, g_cv], w_kv)
-    grad_tokens = residual_alpha * grad_one + back_product(g_qkv, w_qkv)
     return (
         layer_out.astype(low),
         grad_tokens,

time: 735 us -> 671 us (0.913)
  Pallas kernels: 628 us -> 610 us
  matrix products: 26.1 us -> 9.01 us
  between operations: 15.2 us -> 1.61 us
  local copies, waits for them, and re-layouts: 35.4 us -> 23.9 us
    pallas_call x6, Pallas kernels: 533 us -> 559 us  [communicate(): pl.pallas_call(body, out_shape=out_shape, in_specs=in_specs, out_specs=ou...]
    pallas_call x4 -> x1, Pallas kernels: 28.3 us -> 4.32 us  [back_product(): pl.pallas_call(functools.partial(back_kernel, count), grid=(t,), out_shap...]
    pallas_call x4 -> x3, Pallas kernels: 28.2 us -> 17.5 us  [cols_product(): pl.pallas_call(functools.partial(cols_kernel, count), grid=(t,), out_shap...]
    pallas_call x7 -> x2, Pallas kernels: 39.1 us -> 29.2 us  [the longest x1 15.8 us: forward_hidden(): pl.pallas_call(forward_kernel, grid=(t,), out_shape=[low, low, jax.ShapeD...]
    dot_general x1 -> x0, matrix products: 9.64 us -> none  [per_device(): lax.dot_general(grad_three_low, w_out, NT, preferred_element_type=jnp.flo...]
    dot_general x3 -> x2, matrix products: 12.7 us -> 5.22 us  [product(): return jnp.dot(values, weight, preferred_element_type=jnp.float32)]
    unnamed x125 -> x90, local copies, waits for them, and re-layouts: 25.2 us -> 18.2 us
  transfers between devices with their start and end apart: 2 -> 0, of which waited for: 0 -> 0; matrix products, arithmetic and copies ran while one was open for 2% -> 0% of each run, Pallas kernels for 39% -> 0%
where the time goes in v4:
time: 671 us; the launch traced here: 661 us
  Pallas kernels  610 us (91%)
  local copies, waits for them, and re-layouts  23.9 us (4%)
  other arithmetic  16.5 us (2%)
  matrix products  9.01 us (1%)
    pallas_call x6, Pallas kernels, communicate(): pl.pallas_call(body, out_shape=out_shape, in_specs=in_specs, out_specs=ou...  559 us
    unnamed x90, local copies, waits for them, and re-layouts  18.2 us
    pallas_call x3, Pallas kernels, cols_product(): pl.pallas_call(functools.partial(cols_kernel, count), grid=(t,), out_shap...  17.5 us
    pallas_call x1, Pallas kernels, forward_hidden(): pl.pallas_call(forward_kernel, grid=(t,), out_shape=[low, low, jax.ShapeD...  15.8 us
    pallas_call x1, Pallas kernels, backward_hidden(): pl.pallas_call(backward_kernel, grid=(t,), out_shape=[jax.ShapeDtypeStruc...  13.5 us

profile of v4, /device:TPU:0, one launch (start us, length us, event | category | flops | bytes accessed | tf_op | source)
XLA Modules:
  0.0 661.5 jit_solution(14035209117166738230)
XLA Ops:
  0.7 1.4 copy.34
  2.1 1.2 copy.35.refs_0_
  3.8 44.4 %shard_map.245 = (bf16[8,1024,384]{2,1,0:T(8,128)(2,1)}, bf16[8,64,128]{2,1,0:T(8,128)(2,1)}) custom-call(bf16[1024,384]{1,0:T(8,128)(2,1)} %copy.35.refs_0_, bf16[64,128]{1,0:T(8,128)(2,1)} %pad_bitcast_fusion.refs_1_), custom_call_target="tpu_custom_call" | custom-call | tf_op jit(solution)/shard_map/pallas_call | solution.py:745
  48.2 8.0 %shard_map.246 = (bf16[384,1024]{1,0:T(8,128)(2,1)S(1)}, bf16[384,1024]{1,0:T(8,128)(2,1)S(1)}, bf16[384,1024]{1,0:T(8,128)(2,1)S(1)}) custom-call(bf16[384,1024]{1,0:T(8,128)(2,1)S(1)} %copy-done.8, bf16[8,1024,384]{2,1,0:T(8,128)(2,1)} %get-tuple-element.61.w_ref.refs_8_), custom_call_target="tpu_custom_call" | custom-call | flops 2415919104 | bytes 9437184 | tf_op jit(solution)/shard_map/pallas_call | solution.py:912
  56.3 0.9 copy-done.9
  57.1 0.9 copy-done.10
  58.0 0.9 copy-done.11
  58.9 0.9 copy.56
  59.8 102.5 %shard_map.247 = (bf16[384,1024]{1,0:T(8,128)(2,1)}, bf16[3,1024,128]{2,1,0:T(8,128)(2,1)}, bf16[3,1024,128]{2,1,0:T(8,128)(2,1)}, bf16[3,1024,128]{2,1,0:T(8,12...) custom-call(bf16[384,1024]{1,0:T(8,128)(2,1)} %copy-done.9, ...), custom_call_target="tpu_custom_call" | custom-call | tf_op jit(solution)/shard_map/pallas_call | solution.py:745
  162.3 2.9 fusion.17
  166.0 1.5 copy-done
  167.5 3.1 shard_map.248.refs_0_
  170.7 0.9 copy-done.6
  171.5 6.4 shard_map.249
  177.9 0.9 copy-done.12
  178.8 0.9 copy-done.13
  179.7 117.4 %shard_map.250 = (bf16[384,1024]{1,0:T(8,128)(2,1)}, bf16[3,1024,128]{2,1,0:T(8,128)(2,1)}, bf16[3,1024,128]{2,1,0:T(8,128)(2,1)}, bf16[3,1024,128]{2,1,0:T(8,12...) custom-call(bf16[384,1024]{1,0:T(8,128)(2,1)} %copy-done.6, ...), custom_call_target="tpu_custom_call" | custom-call | tf_op jit(solution)/shard_map/pallas_call | solution.py:745
  297.1 2.3 fusion.18
  300.8 15.8 %shard_map.251 = (bf16[384,4096]{1,0:T(8,128)(2,1)S(1)}, bf16[384,4096]{1,0:T(8,128)(2,1)}, f32[384,1024]{1,0:T(8,128)S(1)}) custom-call(bf16[384,1024]{1,0:T(8,128)(2,1)S(1)} %fusion.5.x_ref.refs_2_, bf16[8,1024,512]{2,1,0:T(8,128)(2,1)} %get-tuple-element.73.w_ref, bf16[1,4096]{1,0:T(2,128)(2,1)S(1)} %bitcast.77, bf16[8,512,1024]{2,1,0:T(8,128)(2,1)} %get-tuple-element.75.v_ref), custom_call_target="tpu_custom_call" | custom-call | flops 6442450944 | bytes 23068672 | tf_op jit(solution)/shard_map/pallas_call | solution.py:987
  316.5 0.7 fusion.13
  317.2 1.1 copy-done.4
  318.6 0.8 copy-done.17
  319.4 0.6 fusion.3
  320.1 1.6 fusion.12
  321.8 13.5 %shard_map.252 = (bf16[384,4096]{1,0:T(8,128)(2,1)S(1)}, f32[1,4096]{1,0:T(1,128)S(1)}, f32[384,1024]{1,0:T(8,128)S(1)}) custom-call(bf16[384,1024]{1,0:T(8,128)(2,1)S(1)} %add_convert_fusion.2.g_ref.refs_1_, bf16[8,512,1024]{2,1,0:T(8,128)(2,1)} %get-tuple-element.75.v_ref, bf16[384,4096]{1,0:T(8,128)(2,1)} %get-tuple-element.77.slope_ref, ...), custom_call_target="tpu_custom_call" | custom-call | flops 6442450944 | bytes 23068672 | tf_op jit(solution)/shard_map/pallas_call | solution.py:1026
  335.3 0.9 multiply_reduce_fusion
  336.2 0.8 copy-done.5
  337.7 1.9 convolution_convert_fusion.1.grad_ref
  339.6 136.5 %shard_map.253 = (bf16[384,1024]{1,0:T(8,128)(2,1)}, bf16[384,1024]{1,0:T(8,128)(2,1)}, bf16[384,1024]{1,0:T(8,128)(2,1)}, bf16[4096,128]{1,0:T(8,128)(2,1)}, bf16[4096,128]{1,0:T(8,128)(2,1)}) custom-call(bf16[384,1024]{1,0:T(8,128)(2,1)} %convolution_convert_fusion.1.grad_ref, bf16[3,1024,128]{2,1,0:T(8,128)(2,1)} %get-tuple-element.79.q, ...), custom_call_target="tpu_custom_call" | custom-call | tf_op jit(solution)/shard_map/pallas_call | solution.py:745
  476.1 1.1 copy-done.7
  477.2 4.3 shard_map.254
  481.6 0.8 multiply_reduce_fusion.1
  483.0 1.4 fusion.9
  484.3 0.8 copy-done.36
  485.1 1.9 convolution_convert_fusion.grad_ref
  487.0 98.5 %shard_map.255 = (bf16[384,1024]{1,0:T(8,128)(2,1)}, bf16[384,1024]{1,0:T(8,128)(2,1)}, bf16[384,1024]{1,0:T(8,128)(2,1)}, bf16[1024,128]{1,0:T(8,128)(2,1)}, bf...) custom-call(bf16[384,1024]{1,0:T(8,128)(2,1)} %convolution_convert_fusion.grad_ref, ...), custom_call_target="tpu_custom_call" | custom-call | tf_op jit(solution)/shard_map/pallas_call | solution.py:745
  586.2 60.1 %shard_map.256 = (bf16[3072,128]{1,0:T(8,128)(2,1)}, f32[88,128]{1,0:T(8,128)}, f32[384,1024]{1,0:T(8,128)}, f32[384,1024]{1,0:T(8,128)}) custom-call(bf16[384,1024]{1,0:T(8,128)(2,1)} %refs_0_.1, bf16[384,1024]{1,0:T(8,128)(2,1)} %get-tuple-element.94.refs_1_.refs_5_, bf16[384,1024]{1,0:T(8,128)(2,1)} %get-tuple-element.95.refs_2_.refs_6_, ...), custom_call_target="tpu_custom_call" | custom-call | tf_op jit(solution)/shard_map/pallas_call | solution.py:745
  646.3 2.4 convert_bitcast_fusion.2
  648.8 1.1 copy_bitcast_fusion.4
  649.9 0.8 convert_element_type.51
  650.7 1.5 copy.55
  652.2 1.6 copy_bitcast_fusion.1
  653.8 0.7 dynamic_slice.3
  654.5 1.6 copy_bitcast_fusion
  656.7 0.6 reshape.228
  657.9 1.1 copy.67
  659.0 0.8 copy-done.20
  659.9 1.1 copy.68
  (101 shorter events, 6.3 us)
Async XLA Ops:
  0.6 2.6 copy-start.35
  2.1 46.2 %copy-start.8 = (bf16[384,1024]{1,0:T(8,128)(2,1)S(1)}, bf16[384,1024]{1,0:T(8,128)(2,1)}, u32[]{:S(2)}) copy-start(bf16[384,1024]{1,0:T(8,128)(2,1)} %refs_0_.1) | copy-start | bytes 2359300
  48.2 10.7 %copy-start.25 = (bf16[1024,2,128]{2,1,0:T(2,128)(2,1)S(1)}, bf16[1024,2,128]{2,1,0:T(2,128)(2,1)}, u32[]{:S(2)}) copy-start(bf16[1024,2,128]{2,1,0:T(2,128)(2,1)} %param.19) | copy-start | bytes 1572868
  56.3 0.9 copy-start.9
  57.1 0.9 copy-start.10
  58.0 0.9 copy-start.11
  162.3 2.9 copy-start.32
  162.3 3.0 copy-start.33
  165.6 1.9 copy-start
  166.0 4.7 copy-start.1
  167.5 4.0 copy-start.14
  170.6 0.9 copy-start.6
  177.9 0.9 copy-start.12
  178.8 0.9 copy-start.13
  179.7 117.4 %copy-start.37 = (bf16[8,128,1024]{2,1,0:T(8,128)(2,1)S(1)}, bf16[8,128,1024]{2,1,0:T(8,128)(2,1)}, u32[]{:S(2)}) copy-start(bf16[8,128,1024]{2,1,0:T(8,128)(2,1)} %get-tuple-element.72) | copy-start | bytes 6291460
  299.7 0.9 copy-start.29
  300.1 16.5 %copy-start.2 = (bf16[384,1024]{1,0:T(8,128)(2,1)}, bf16[384,1024]{1,0:T(8,128)(2,1)S(1)}, u32[]{:S(2)}) copy-start(bf16[384,1024]{1,0:T(8,128)(2,1)S(1)} %fusion.5.x_ref.refs_2_) | copy-start | bytes 2359300
  300.8 15.8 %copy-start.34 = (f32[1024]{0:T(1024)S(1)}, f32[1024]{0:T(1024)}, u32[]{:S(2)}) copy-start(f32[1024]{0:T(1024)} %param.24) | copy-start | bytes 12292
  316.5 1.7 copy-start.4
  318.3 1.1 copy-start.17
  321.8 13.5 %copy-start.3 = (bf16[384,1024]{1,0:T(8,128)(2,1)}, bf16[384,1024]{1,0:T(8,128)(2,1)S(1)}, u32[]{:S(2)}) copy-start(bf16[384,1024]{1,0:T(8,128)(2,1)S(1)} %add_convert_fusion.2.g_ref.refs_1_) | copy-start | bytes 2359300
  335.3 1.7 copy-start.5
  337.5 2.1 copy-start.15
  337.7 1.9 copy-start.19
  476.1 1.1 copy-start.7
  477.2 4.3 copy-start.16
  483.0 2.2 copy-start.36
  484.3 2.7 copy-start.18
  585.6 0.6 copy-start.30
  646.3 2.5 copy-start.27
  646.3 2.5 copy-start.28
  646.3 3.6 copy-start.26
  648.8 1.9 copy-start.24
  649.9 2.3 copy-start.23
  652.2 1.6 copy-start.31
  652.2 2.3 copy-start.22
  654.5 3.4 copy-start.21
  657.9 2.0 copy-start.20

commit v5 on v4

--- a/solution.py
+++ b/solution.py
@@ -280,6 +280,7 @@
         self.out_shape = [jax.ShapeDtypeStruct((t,) + w.shape, w.dtype) for w in weights]
         self.scratch = [
             dma((m, self.depth)),
+            dma((m, 2)),
             dma((m, self.depth)),
             dma((m, t)),
             dma((m, t, 2)),
@@ -305,7 +306,7 @@
         return pl.ds(at16(start + (1 - xpos) * (half - a)), a)
 
     def steps(self, place, ins, outs, scratch):
-        z_send, y_send, x_send, d_send, plane_recv, x_recv, d_recv, own_sem = scratch
+        z_send, own_send, y_send, x_send, d_send, plane_recv, x_recv, d_recv, own_sem = scratch
         self.place = place
         me, depth, t, pieces = place.me, self.depth, self.t, self.pieces
 
@@ -318,17 +319,22 @@
         def part(n, block, kind, core=place.core):
             return outs[pieces[n][0]].at[block, rows_of(n, kind, core), :]
 
-        def column(i, side):
-            return 2 * place.line_at(depth - i) + side
-
         def own(n):
             return ins[pieces[n][0]].at[rows_of(n, "plane"), :]
 
-        def z_copy(n, i):
-            return remote(own(n), part(n, me, "plane"), z_send.at[n, i], plane_recv.at[n, me], place.z_mate(i))
+        line, side = place.line, place.side
+
+        def along(n, block, sign):
+            src = part(n, block, "plane")
+            device = {"tensor": 2 * (line + sign) + side}
+            return remote(src, src, z_send.at[n, block // 2], plane_recv.at[n, block], device)
+
+        def z_own(n, sign):
+            device = {"tensor": 2 * (line + sign) + side}
+            return remote(own(n), part(n, me, "plane"), own_send.at[n, (1 - sign) // 2], plane_recv.at[n, me], device)
 
         def y_own(n):
-            return remote(own(n), part(n, me, "plane"), y_send.at[n, place.line], plane_recv.at[n, me], place.y_mate)
+            return remote(own(n), part(n, me, "plane"), y_send.at[n, line], plane_recv.at[n, me], place.y_mate)
 
         def y_copy(n, block):
             ref = part(n, block, "plane")
@@ -345,59 +351,104 @@
         def own_copy(w):
             return pltpu.make_async_copy(ins[w], outs[w].at[me], own_sem.at[w])
 
+        def ends(distance):
+            yield line >= distance, line - distance, line < depth - 1, 1
+            yield line < depth - distance, line + distance, line > 0, -1
+
         total = len(pieces)
 
         def launch(n):
             if n < total:
-                for i in range(1, depth):
-                    z_copy(n, i).start()
+                for sign, there in ((1, line < depth - 1), (-1, line > 0)):
+
+                    @pl.when(there)
+                    def _():
+                        z_own(n, sign).start()
+
                 y_own(n).start()
+
+        def z_stage(n, distance):
+            for there, at, more, sign in ends(distance):
+
+                @pl.when(there)
+                def _():
+                    block = 2 * at + side
+                    landed(part(n, block, "plane"), plane_recv.at[n, block])
+
+                    @pl.when(more)
+                    def _():
+                        along(n, block, sign).start()
+
+                    y_copy(n, block).start()
+                    if has_x(n):
+                        x_copy(n, block).start()
+                    d_copy(n, block, 0).start()
+
+        def y_stage(n, distance):
+            for there, at, _, sign in ends(distance):
+                if distance == 0 and sign < 0:
+                    continue
+
+                @pl.when(there)
+                def _():
+                    block = 2 * at + 1 - side
+                    landed(part(n, block, "plane"), plane_recv.at[n, block])
+                    if has_x(n):
+                        x_copy(n, block).start()
+                    d_copy(n, block, 0).start()
+
+        def x_stage(n, distance, same):
+            if not has_x(n):
+                return
+            for there, at, _, sign in ends(distance):
+                if distance == 0 and sign < 0:
+                    continue
+
+                @pl.when(there)
+                def _():
+                    block = 2 * at + (side if same else 1 - side)
+                    landed(part(n, block, "x_in"), x_recv.at[n, block])
+                    d_copy(n, block, 1).start()
 
         launch(0)
         for w in range(len(ins)):
             own_copy(w).start()
         yield True
-        for step in range(total + 2):
+        for step in range(total + depth):
             launch(step + 1)
-            n = step
-            if n < total:
-
-                def z_stage(i):
-                    block = column(i, place.side)
-                    landed(part(n, block, "plane"), plane_recv.at[n, block])
-                    y_copy(n, block).start()
-                    if has_x(n):
-                        x_copy(n, block).start()
-                    d_copy(n, block, 0).start()
-
-                loop(1, depth, z_stage)
-            n1 = step - 1
-            if 0 <= n1 < total:
-
-                def y_stage(i):
-                    block = column(i, 1 - place.side)
-                    landed(part(n1, block, "plane"), plane_recv.at[n1, block])
-                    if has_x(n1):
-                        x_copy(n1, block).start()
-                    d_copy(n1, block, 0).start()
-
-                loop(0, depth, y_stage)
-            n2 = step - 2
-            if 0 <= n2 < total and has_x(n2):
-
-                def x_stage(i):
-                    block = lax.rem(me + i, t)
-                    landed(part(n2, block, "x_in"), x_recv.at[n2, block])
-                    d_copy(n2, block, 1).start()
-
-                loop(1, t, x_stage)
+            for late in range(depth, -1, -1):
+                n = step - late
+                if not 0 <= n < total:
+                    continue
+                if late < depth - 1:
+                    z_stage(n, late + 1)
+                if late < depth:
+                    y_stage(n, late)
+                if 0 < late < depth:
+                    x_stage(n, late, True)
+                if late > 0:
+                    x_stage(n, late - 1, False)
             yield True
         for w in range(len(ins)):
             own_copy(w).wait()
         for n in range(total):
-            loop(1, depth, lambda i: z_copy(n, i).wait_send())
             y_own(n).wait_send()
-            loop(1, depth, lambda i: y_copy(n, column(i, place.side)).wait_send())
+            for sign, there in ((1, line < depth - 1), (-1, line > 0)):
+
+                @pl.when(there)
+                def _():
+                    z_own(n, sign).wait_send()
+
+            for distance in range(1, depth):
+                for there, at, more, sign in ends(distance):
+
+                    @pl.when(there)
+                    def _():
+                        y_copy(n, 2 * at + side).wait_send()
+
+                    @pl.when(there & more)
+                    def _():
+                        along(n, 2 * at + side, sign).wait_send()
 
             def finish(i):
                 block = lax.rem(me + i, t)

time: 671 us -> 660 us (0.984)
  Pallas kernels: 610 us -> 600 us
    pallas_call x6, Pallas kernels: 559 us -> 549 us  [communicate(): pl.pallas_call(body, out_shape=out_shape, in_specs=in_specs, out_specs=ou...]
where the time goes in v5:
time: 660 us; the launch traced here: 651 us
  Pallas kernels  600 us (91%)
  local copies, waits for them, and re-layouts  23.9 us (4%)
  other arithmetic  16.5 us (2%)
  matrix products  9.02 us (1%)
    pallas_call x6, Pallas kernels, communicate(): pl.pallas_call(body, out_shape=out_shape, in_specs=in_specs, out_specs=ou...  549 us
    unnamed x90, local copies, waits for them, and re-layouts  18.2 us
    pallas_call x3, Pallas kernels, cols_product(): pl.pallas_call(functools.partial(cols_kernel, count), grid=(t,), out_shap...  17.5 us
    pallas_call x1, Pallas kernels, forward_hidden(): pl.pallas_call(forward_kernel, grid=(t,), out_shape=[low, low, jax.ShapeD...  15.8 us
    pallas_call x1, Pallas kernels, backward_hidden(): pl.pallas_call(backward_kernel, grid=(t,), out_shape=[jax.ShapeDtypeStruc...  13.5 us

profile of v5, /device:TPU:0, one launch (start us, length us, event | category | flops | bytes accessed | tf_op | source)
XLA Modules:
  0.0 651.0 jit_solution(2668938986887670489)
XLA Ops:
  0.7 1.4 copy.34
  2.1 1.2 copy.35.refs_0_
  3.8 47.5 %shard_map.245 = (bf16[8,1024,384]{2,1,0:T(8,128)(2,1)}, bf16[8,64,128]{2,1,0:T(8,128)(2,1)}) custom-call(bf16[1024,384]{1,0:T(8,128)(2,1)} %copy.35.refs_0_, bf16[64,128]{1,0:T(8,128)(2,1)} %pad_bitcast_fusion.refs_1_), custom_call_target="tpu_custom_call" | custom-call | tf_op jit(solution)/shard_map/pallas_call | solution.py:796
  51.3 8.0 %shard_map.246 = (bf16[384,1024]{1,0:T(8,128)(2,1)S(1)}, bf16[384,1024]{1,0:T(8,128)(2,1)S(1)}, bf16[384,1024]{1,0:T(8,128)(2,1)S(1)}) custom-call(bf16[384,1024]{1,0:T(8,128)(2,1)S(1)} %copy-done.8, bf16[8,1024,384]{2,1,0:T(8,128)(2,1)} %get-tuple-element.61.w_ref.refs_8_), custom_call_target="tpu_custom_call" | custom-call | flops 2415919104 | bytes 9437184 | tf_op jit(solution)/shard_map/pallas_call | solution.py:963
  59.4 0.9 copy-done.9
  60.2 0.9 copy-done.10
  61.1 0.9 copy-done.11
  62.0 0.9 copy.56
  62.9 94.2 %shard_map.247 = (bf16[384,1024]{1,0:T(8,128)(2,1)}, bf16[3,1024,128]{2,1,0:T(8,128)(2,1)}, bf16[3,1024,128]{2,1,0:T(8,128)(2,1)}, bf16[3,1024,128]{2,1,0:T(8,12...) custom-call(bf16[384,1024]{1,0:T(8,128)(2,1)} %copy-done.9, ...), custom_call_target="tpu_custom_call" | custom-call | tf_op jit(solution)/shard_map/pallas_call | solution.py:796
  157.1 2.9 fusion.17
  160.7 1.5 copy-done
  162.2 3.1 shard_map.248.refs_0_
  165.4 0.9 copy-done.6
  166.3 6.4 shard_map.249
  172.7 0.9 copy-done.12
  173.5 0.9 copy-done.13
  174.4 117.7 %shard_map.250 = (bf16[384,1024]{1,0:T(8,128)(2,1)}, bf16[3,1024,128]{2,1,0:T(8,128)(2,1)}, bf16[3,1024,128]{2,1,0:T(8,128)(2,1)}, bf16[3,1024,128]{2,1,0:T(8,12...) custom-call(bf16[384,1024]{1,0:T(8,128)(2,1)} %copy-done.6, ...), custom_call_target="tpu_custom_call" | custom-call | tf_op jit(solution)/shard_map/pallas_call | solution.py:796
  292.1 2.3 fusion.18
  295.8 15.8 %shard_map.251 = (bf16[384,4096]{1,0:T(8,128)(2,1)S(1)}, bf16[384,4096]{1,0:T(8,128)(2,1)}, f32[384,1024]{1,0:T(8,128)S(1)}) custom-call(bf16[384,1024]{1,0:T(8,128)(2,1)S(1)} %fusion.5.x_ref.refs_2_, bf16[8,1024,512]{2,1,0:T(8,128)(2,1)} %get-tuple-element.73.w_ref, bf16[1,4096]{1,0:T(2,128)(2,1)S(1)} %bitcast.77, bf16[8,512,1024]{2,1,0:T(8,128)(2,1)} %get-tuple-element.75.v_ref), custom_call_target="tpu_custom_call" | custom-call | flops 6442450944 | bytes 23068672 | tf_op jit(solution)/shard_map/pallas_call | solution.py:1038
  311.6 0.7 fusion.13
  312.2 1.1 copy-done.4
  313.6 0.8 copy-done.17
  314.4 0.6 fusion.3
  315.1 1.6 fusion.12
  316.8 13.5 %shard_map.252 = (bf16[384,4096]{1,0:T(8,128)(2,1)S(1)}, f32[1,4096]{1,0:T(1,128)S(1)}, f32[384,1024]{1,0:T(8,128)S(1)}) custom-call(bf16[384,1024]{1,0:T(8,128)(2,1)S(1)} %add_convert_fusion.2.g_ref.refs_1_, bf16[8,512,1024]{2,1,0:T(8,128)(2,1)} %get-tuple-element.75.v_ref, bf16[384,4096]{1,0:T(8,128)(2,1)} %get-tuple-element.77.slope_ref, ...), custom_call_target="tpu_custom_call" | custom-call | flops 6442450944 | bytes 23068672 | tf_op jit(solution)/shard_map/pallas_call | solution.py:1077
  330.3 0.9 multiply_reduce_fusion
  331.2 0.8 copy-done.5
  332.7 1.9 convolution_convert_fusion.1.grad_ref
  334.6 131.1 %shard_map.253 = (bf16[384,1024]{1,0:T(8,128)(2,1)}, bf16[384,1024]{1,0:T(8,128)(2,1)}, bf16[384,1024]{1,0:T(8,128)(2,1)}, bf16[4096,128]{1,0:T(8,128)(2,1)}, bf16[4096,128]{1,0:T(8,128)(2,1)}) custom-call(bf16[384,1024]{1,0:T(8,128)(2,1)} %convolution_convert_fusion.1.grad_ref, bf16[3,1024,128]{2,1,0:T(8,128)(2,1)} %get-tuple-element.79.q, ...), custom_call_target="tpu_custom_call" | custom-call | tf_op jit(solution)/shard_map/pallas_call | solution.py:796
  465.8 1.1 copy-done.7
  466.9 4.5 shard_map.254
  471.4 0.8 multiply_reduce_fusion.1
  472.8 1.4 fusion.9
  474.2 0.8 copy-done.36
  475.0 1.9 convolution_convert_fusion.grad_ref
  476.9 99.8 %shard_map.255 = (bf16[384,1024]{1,0:T(8,128)(2,1)}, bf16[384,1024]{1,0:T(8,128)(2,1)}, bf16[384,1024]{1,0:T(8,128)(2,1)}, bf16[1024,128]{1,0:T(8,128)(2,1)}, bf...) custom-call(bf16[384,1024]{1,0:T(8,128)(2,1)} %convolution_convert_fusion.grad_ref, ...), custom_call_target="tpu_custom_call" | custom-call | tf_op jit(solution)/shard_map/pallas_call | solution.py:796
  577.4 58.5 %shard_map.256 = (bf16[3072,128]{1,0:T(8,128)(2,1)}, f32[88,128]{1,0:T(8,128)}, f32[384,1024]{1,0:T(8,128)}, f32[384,1024]{1,0:T(8,128)}) custom-call(bf16[384,1024]{1,0:T(8,128)(2,1)} %refs_0_.1, bf16[384,1024]{1,0:T(8,128)(2,1)} %get-tuple-element.94.refs_1_.refs_5_, bf16[384,1024]{1,0:T(8,128)(2,1)} %get-tuple-element.95.refs_2_.refs_6_, ...), custom_call_target="tpu_custom_call" | custom-call | tf_op jit(solution)/shard_map/pallas_call | solution.py:796
  635.9 2.4 convert_bitcast_fusion.2
  638.3 1.1 copy_bitcast_fusion.4
  639.4 0.8 convert_element_type.51
  640.3 1.5 copy.55
  641.8 1.6 copy_bitcast_fusion.1
  643.4 0.7 dynamic_slice.3
  644.0 1.6 copy_bitcast_fusion
  646.2 0.6 reshape.228
  647.4 1.1 copy.67
  648.6 0.8 copy-done.20
  649.4 1.1 copy.68
  (101 shorter events, 6.3 us)
Async XLA Ops:
  0.6 2.6 copy-start.35
  2.1 49.3 %copy-start.8 = (bf16[384,1024]{1,0:T(8,128)(2,1)S(1)}, bf16[384,1024]{1,0:T(8,128)(2,1)}, u32[]{:S(2)}) copy-start(bf16[384,1024]{1,0:T(8,128)(2,1)} %refs_0_.1) | copy-start | bytes 2359300
  51.3 10.7 %copy-start.25 = (bf16[1024,2,128]{2,1,0:T(2,128)(2,1)S(1)}, bf16[1024,2,128]{2,1,0:T(2,128)(2,1)}, u32[]{:S(2)}) copy-start(bf16[1024,2,128]{2,1,0:T(2,128)(2,1)} %param.19) | copy-start | bytes 1572868
  59.4 0.9 copy-start.9
  60.2 0.9 copy-start.10
  61.1 0.9 copy-start.11
  157.1 2.9 copy-start.32
  157.1 3.0 copy-start.33
  160.4 1.9 copy-start
  160.7 4.7 copy-start.1
  162.2 4.0 copy-start.14
  165.4 0.9 copy-start.6
  172.7 0.9 copy-start.12
  173.5 0.9 copy-start.13
  174.4 117.7 %copy-start.37 = (bf16[8,128,1024]{2,1,0:T(8,128)(2,1)S(1)}, bf16[8,128,1024]{2,1,0:T(8,128)(2,1)}, u32[]{:S(2)}) copy-start(bf16[8,128,1024]{2,1,0:T(8,128)(2,1)} %get-tuple-element.72) | copy-start | bytes 6291460
  294.7 0.9 copy-start.29
  295.1 16.5 %copy-start.2 = (bf16[384,1024]{1,0:T(8,128)(2,1)}, bf16[384,1024]{1,0:T(8,128)(2,1)S(1)}, u32[]{:S(2)}) copy-start(bf16[384,1024]{1,0:T(8,128)(2,1)S(1)} %fusion.5.x_ref.refs_2_) | copy-start | bytes 2359300
  295.8 15.8 %copy-start.34 = (f32[1024]{0:T(1024)S(1)}, f32[1024]{0:T(1024)}, u32[]{:S(2)}) copy-start(f32[1024]{0:T(1024)} %param.24) | copy-start | bytes 12292
  311.5 1.7 copy-start.4
  313.3 1.1 copy-start.17
  316.8 13.5 %copy-start.3 = (bf16[384,1024]{1,0:T(8,128)(2,1)}, bf16[384,1024]{1,0:T(8,128)(2,1)S(1)}, u32[]{:S(2)}) copy-start(bf16[384,1024]{1,0:T(8,128)(2,1)S(1)} %add_convert_fusion.2.g_ref.refs_1_) | copy-start | bytes 2359300
  330.3 1.7 copy-start.5
  332.5 2.1 copy-start.15
  332.7 1.9 copy-start.19
  465.8 1.1 copy-start.7
  466.9 4.5 copy-start.16
  472.8 2.2 copy-start.36
  474.2 2.7 copy-start.18
  576.7 0.6 copy-start.30
  635.8 2.5 copy-start.27
  635.9 2.5 copy-start.28
  635.9 3.6 copy-start.26
  638.3 1.9 copy-start.24
  639.4 2.3 copy-start.23
  641.8 1.6 copy-start.31
  641.8 2.3 copy-start.22
  644.0 3.4 copy-start.21
  647.4 2.0 copy-start.20

commit v6 on v5

--- a/solution.py
+++ b/solution.py
@@ -779,6 +779,25 @@
         out.start()
         out.wait()
         yield True
+
+
+class Together:
+    def __init__(self, *jobs):
+        self.jobs = jobs
+        self.ins = [a for j in jobs for a in j.ins]
+        self.specs = [a for j in jobs for a in j.specs]
+        self.out_shape = [a for j in jobs for a in j.out_shape]
+        self.scratch = [a for j in jobs for a in j.scratch]
+
+    def steps(self, place, ins, outs, scratch):
+        ins, outs, scratch, running = list(ins), list(outs), list(scratch), []
+        for j in self.jobs:
+            a, b, c = len(j.ins), len(j.out_shape), len(j.scratch)
+            running.append(j.steps(place, ins[:a], outs[:b], scratch[:c]))
+            ins, outs, scratch = ins[a:], outs[b:], scratch[c:]
+        while running:
+            running = [g for g in running if next(g, None) is not None]
+            yield True
 
 
 class Nothing:
@@ -1218,7 +1237,7 @@
     units = hidden_bias.shape[0]
     bias_block = jnp.pad(hidden_bias, (0, 64 * LANES - units)).reshape(64, LANES)
     first = [self_qkv.reshape(d, -1), bias_block]
-    w_qkv, bias_all = jobs_kernel([Gather(first, t, 0.36)], t, 0)
+    w_qkv, bias_all = jobs_kernel([Gather(first, t, 0.36, 1 << 18)], t, 0)
     w_qkv = widen(w_qkv, 3)
     bias_all = bias_all.reshape(t, -1)[:, :units].reshape(1, -1)
 
@@ -1276,18 +1295,18 @@
         size,
         0.25,
     )
-    g_qkv, (cross_out_grad, cross_q_grad, cross_kv_grad, self_out_grad) = attend_back(
-        grad_so, self_saved, t, True, 256, reduce_cross, 2, 2, 4
+    beside = Together(reduce_cross, Back([g_ck, g_cv], w_kv))
+    g_qkv, (cross_out_grad, cross_q_grad, cross_kv_grad, self_out_grad, grad_memory) = attend_back(
+        grad_so, self_saved, t, True, 256, beside, 2, 2, 4
     )
     small = jnp.concatenate(
         [gain_one, gain_two, gain_three, shift_one, shift_two, shift_three, bias_out_grad, hidden_bias_grad[0]]
     ).reshape(-1, LANES)
-    self_qkv_grad, small, grad_tokens, grad_memory = jobs_kernel(
+    self_qkv_grad, small, grad_tokens = jobs_kernel(
         [
             Reduce([cols_weight(tokens, g_qkv, t)], t, size, 0.5),
             Total(small, t),
             Back(g_qkv, w_qkv, grad_one, residual_alpha),
-            Back([g_ck, g_cv], w_kv),
         ],
         t,
         5,

time: 660 us -> 656 us (level)
  no operation moved by 1% of the time
where the time goes in v6:
time: 656 us; the launch traced here: 648 us
  Pallas kernels  597 us (91%)
  local copies, waits for them, and re-layouts  23.9 us (4%)
  other arithmetic  16.5 us (3%)
  matrix products  9.02 us (1%)
    pallas_call x6, Pallas kernels, communicate(): pl.pallas_call(body, out_shape=out_shape, in_specs=in_specs, out_specs=ou...  545 us
    unnamed x90, local copies, waits for them, and re-layouts  18.2 us
    pallas_call x3, Pallas kernels, cols_product(): pl.pallas_call(functools.partial(cols_kernel, count), grid=(t,), out_shap...  17.5 us
    pallas_call x1, Pallas kernels, forward_hidden(): pl.pallas_call(forward_kernel, grid=(t,), out_shape=[low, low, jax.ShapeD...  15.8 us
    pallas_call x1, Pallas kernels, backward_hidden(): pl.pallas_call(backward_kernel, grid=(t,), out_shape=[jax.ShapeDtypeStruc...  13.5 us

profile of v6, /device:TPU:0, one launch (start us, length us, event | category | flops | bytes accessed | tf_op | source)
XLA Modules:
  0.0 647.7 jit_solution(6880524203695092295)
XLA Ops:
  0.7 1.4 copy.34
  2.1 1.2 copy.35.refs_0_
  3.8 44.9 %shard_map.245 = (bf16[8,1024,384]{2,1,0:T(8,128)(2,1)}, bf16[8,64,128]{2,1,0:T(8,128)(2,1)}) custom-call(bf16[1024,384]{1,0:T(8,128)(2,1)} %copy.35.refs_0_, bf16[64,128]{1,0:T(8,128)(2,1)} %pad_bitcast_fusion.refs_1_), custom_call_target="tpu_custom_call" | custom-call | tf_op jit(solution)/shard_map/pallas_call | solution.py:815
  48.8 8.0 %shard_map.246 = (bf16[384,1024]{1,0:T(8,128)(2,1)S(1)}, bf16[384,1024]{1,0:T(8,128)(2,1)S(1)}, bf16[384,1024]{1,0:T(8,128)(2,1)S(1)}) custom-call(bf16[384,1024]{1,0:T(8,128)(2,1)S(1)} %copy-done.14, bf16[8,1024,384]{2,1,0:T(8,128)(2,1)} %get-tuple-element.61.w_ref.refs_8_), custom_call_target="tpu_custom_call" | custom-call | flops 2415919104 | bytes 9437184 | tf_op jit(solution)/shard_map/pallas_call | solution.py:982
  56.8 0.9 copy-done.9
  57.7 0.9 copy-done.10
  58.6 0.9 copy-done.11
  59.5 0.9 copy.56
  60.3 94.5 %shard_map.247 = (bf16[384,1024]{1,0:T(8,128)(2,1)}, bf16[3,1024,128]{2,1,0:T(8,128)(2,1)}, bf16[3,1024,128]{2,1,0:T(8,128)(2,1)}, bf16[3,1024,128]{2,1,0:T(8,12...) custom-call(bf16[384,1024]{1,0:T(8,128)(2,1)} %copy-done.9, ...), custom_call_target="tpu_custom_call" | custom-call | tf_op jit(solution)/shard_map/pallas_call | solution.py:815
  154.9 2.9 fusion.17
  158.5 1.5 copy-done
  160.0 3.1 shard_map.248.refs_0_
  163.2 0.9 copy-done.7
  164.1 6.4 shard_map.249
  170.4 0.9 copy-done.12
  171.3 0.9 copy-done.13
  172.2 117.6 %shard_map.250 = (bf16[384,1024]{1,0:T(8,128)(2,1)}, bf16[3,1024,128]{2,1,0:T(8,128)(2,1)}, bf16[3,1024,128]{2,1,0:T(8,128)(2,1)}, bf16[3,1024,128]{2,1,0:T(8,12...) custom-call(bf16[384,1024]{1,0:T(8,128)(2,1)} %copy-done.7, ...), custom_call_target="tpu_custom_call" | custom-call | tf_op jit(solution)/shard_map/pallas_call | solution.py:815
  289.8 2.3 fusion.18
  293.5 15.8 %shard_map.251 = (bf16[384,4096]{1,0:T(8,128)(2,1)S(1)}, bf16[384,4096]{1,0:T(8,128)(2,1)}, f32[384,1024]{1,0:T(8,128)S(1)}) custom-call(bf16[384,1024]{1,0:T(8,128)(2,1)S(1)} %fusion.5.x_ref.refs_2_, bf16[8,1024,512]{2,1,0:T(8,128)(2,1)} %get-tuple-element.73.w_ref, bf16[1,4096]{1,0:T(2,128)(2,1)S(1)} %bitcast.77, bf16[8,512,1024]{2,1,0:T(8,128)(2,1)} %get-tuple-element.75.v_ref), custom_call_target="tpu_custom_call" | custom-call | flops 6442450944 | bytes 23068672 | tf_op jit(solution)/shard_map/pallas_call | solution.py:1057
  309.3 0.7 fusion.13
  309.9 1.1 copy-done.5
  311.3 0.8 copy-done.19
  312.1 0.6 fusion.3
  312.8 1.6 fusion.12
  314.5 13.5 %shard_map.252 = (bf16[384,4096]{1,0:T(8,128)(2,1)S(1)}, f32[1,4096]{1,0:T(1,128)S(1)}, f32[384,1024]{1,0:T(8,128)S(1)}) custom-call(bf16[384,1024]{1,0:T(8,128)(2,1)S(1)} %add_convert_fusion.2.g_ref.refs_1_, bf16[8,512,1024]{2,1,0:T(8,128)(2,1)} %get-tuple-element.75.v_ref, bf16[384,4096]{1,0:T(8,128)(2,1)} %get-tuple-element.77.slope_ref, ...), custom_call_target="tpu_custom_call" | custom-call | flops 6442450944 | bytes 23068672 | tf_op jit(solution)/shard_map/pallas_call | solution.py:1096
  328.1 0.9 multiply_reduce_fusion
  328.9 0.8 copy-done.6
  330.4 1.9 convolution_convert_fusion.1.grad_ref
  332.3 131.2 %shard_map.253 = (bf16[384,1024]{1,0:T(8,128)(2,1)}, bf16[384,1024]{1,0:T(8,128)(2,1)}, bf16[384,1024]{1,0:T(8,128)(2,1)}, bf16[4096,128]{1,0:T(8,128)(2,1)}, bf16[4096,128]{1,0:T(8,128)(2,1)}) custom-call(bf16[384,1024]{1,0:T(8,128)(2,1)} %convolution_convert_fusion.1.grad_ref, bf16[3,1024,128]{2,1,0:T(8,128)(2,1)} %get-tuple-element.79.q, ...), custom_call_target="tpu_custom_call" | custom-call | tf_op jit(solution)/shard_map/pallas_call | solution.py:815
  463.5 1.1 copy-done.2
  464.7 4.5 shard_map.254
  469.2 0.8 multiply_reduce_fusion.1
  470.6 1.4 fusion.9
  472.0 0.8 copy-done.36
  472.8 1.9 convolution_convert_fusion.grad_ref
  474.7 99.4 %shard_map.255 = (bf16[384,1024]{1,0:T(8,128)(2,1)}, bf16[384,1024]{1,0:T(8,128)(2,1)}, bf16[384,1024]{1,0:T(8,128)(2,1)}, bf16[1024,128]{1,0:T(8,128)(2,1)}, bf...) custom-call(bf16[384,1024]{1,0:T(8,128)(2,1)} %convolution_convert_fusion., ...), custom_call_target="tpu_custom_call" | custom-call | tf_op jit(solution)/shard_map/pallas_call | solution.py:815
  574.8 57.8 %shard_map.256 = (bf16[3072,128]{1,0:T(8,128)(2,1)}, f32[88,128]{1,0:T(8,128)}, f32[384,1024]{1,0:T(8,128)}) custom-call(bf16[384,1024]{1,0:T(8,128)(2,1)} %refs_0_.1, bf16[384,1024]{1,0:T(8,128)(2,1)} %get-tuple-element.94.refs_1_.refs_5_, bf16[384,1024]{1,0:T(8,128)(2,1)} %get-tuple-element.95.refs_2_.refs_6_, ...), custom_call_target="tpu_custom_call" | custom-call | tf_op jit(solution)/shard_map/pallas_call | solution.py:815
  632.6 2.4 convert_bitcast_fusion.2
  635.0 1.1 copy_bitcast_fusion.4
  636.1 0.8 convert_element_type.51
  637.0 1.5 copy.55
  638.5 1.6 copy_bitcast_fusion.1
  640.1 0.7 dynamic_slice.3
  640.7 1.6 copy_bitcast_fusion
  642.9 0.6 reshape.228
  644.2 1.1 copy.67
  645.3 0.8 copy-done.20
  646.1 1.1 copy.68
  (101 shorter events, 6.3 us)
Async XLA Ops:
  0.6 2.6 copy-start.35
  2.1 46.7 %copy-start.14 = (bf16[384,1024]{1,0:T(8,128)(2,1)S(1)}, bf16[384,1024]{1,0:T(8,128)(2,1)}, u32[]{:S(2)}) copy-start(bf16[384,1024]{1,0:T(8,128)(2,1)} %refs_0_.1) | copy-start | bytes 2359300
  48.8 10.7 %copy-start.25 = (bf16[1024,2,128]{2,1,0:T(2,128)(2,1)S(1)}, bf16[1024,2,128]{2,1,0:T(2,128)(2,1)}, u32[]{:S(2)}) copy-start(bf16[1024,2,128]{2,1,0:T(2,128)(2,1)} %param.19) | copy-start | bytes 1572868
  56.8 0.9 copy-start.9
  57.7 0.9 copy-start.10
  58.6 0.9 copy-start.11
  154.8 2.9 copy-start.32
  154.8 3.0 copy-start.33
  158.1 1.9 copy-start
  158.5 4.7 copy-start.1
  160.0 4.0 copy-start.8
  163.2 0.9 copy-start.7
  170.4 0.9 copy-start.12
  171.3 0.9 copy-start.13
  172.2 117.6 %copy-start.37 = (bf16[8,128,1024]{2,1,0:T(8,128)(2,1)S(1)}, bf16[8,128,1024]{2,1,0:T(8,128)(2,1)}, u32[]{:S(2)}) copy-start(bf16[8,128,1024]{2,1,0:T(8,128)(2,1)} %get-tuple-element.72) | copy-start | bytes 6291460
  292.5 0.9 copy-start.29
  292.8 16.5 %copy-start.3 = (bf16[384,1024]{1,0:T(8,128)(2,1)}, bf16[384,1024]{1,0:T(8,128)(2,1)S(1)}, u32[]{:S(2)}) copy-start(bf16[384,1024]{1,0:T(8,128)(2,1)S(1)} %fusion.5.x_ref.refs_2_) | copy-start | bytes 2359300
  293.5 15.8 %copy-start.34 = (f32[1024]{0:T(1024)S(1)}, f32[1024]{0:T(1024)}, u32[]{:S(2)}) copy-start(f32[1024]{0:T(1024)} %param.24) | copy-start | bytes 12292
  309.3 1.7 copy-start.5
  311.0 1.1 copy-start.19
  314.5 13.5 %copy-start.4 = (bf16[384,1024]{1,0:T(8,128)(2,1)}, bf16[384,1024]{1,0:T(8,128)(2,1)S(1)}, u32[]{:S(2)}) copy-start(bf16[384,1024]{1,0:T(8,128)(2,1)S(1)} %add_convert_fusion.2.g_ref.refs_1_) | copy-start | bytes 2359300
  328.0 1.7 copy-start.6
  330.3 2.1 copy-start.15
  330.4 1.9 copy-start.18
  463.5 1.1 copy-start.2
  464.7 4.5 copy-start.16
  470.6 2.2 copy-start.36
  472.0 2.7 copy-start.17
  574.1 0.6 copy-start.30
  632.6 2.5 copy-start.27
  632.6 2.5 copy-start.28
  632.6 3.6 copy-start.26
  635.0 1.9 copy-start.24
  636.1 2.3 copy-start.23
  638.5 1.6 copy-start.31
  638.5 2.3 copy-start.22
  640.7 3.4 copy-start.21
  644.2 2.0 copy-start.20
